TPU v7x, 32 devices: a whole 2x2x4 slice. The times are simulated.
32 devices in a mesh: groups: 2 (over x), fsdp: 16 (over z, y, core).
Axes of the slice: x: 2, y: 2, z: 4, core: 2. Of those that a mesh axis runs over, the one named last changes fastest.
Arguments:
- tokens: bfloat16 [4096, 8192], P(('groups', 'fsdp')), parts along dimension 0
- upstream: bfloat16 [4096, 1024], P(('groups', 'fsdp')), parts along dimension 0, may hold values from -3 to 3
- norm_gain: float32 [8192], replicated, may hold values from 0.25 to 1.75
- value_weight: bfloat16 [8192, 1024], P('fsdp'), may hold values from -0.0625 to 0.0625
- down_factor: bfloat16 [8192, 2048], P('fsdp'), may hold values from -0.0625 to 0.0625
- up_factor: bfloat16 [1024, 2048], P('fsdp'), may hold values from -0.75 to 0.75
- tenant: int32 [64], P('groups'), parts along dimension 0, may hold values from 0 to 31
Outputs:
- adapted_values: bfloat16 [4096, 1024], P(('groups', 'fsdp')), parts along dimension 0
- grad_tokens: bfloat16 [4096, 8192], P(('groups', 'fsdp')), parts along dimension 0
- grad_down: float32 [16384, 2048], P(('groups', 'fsdp')), parts along dimension 0
- grad_up: float32 [2048, 2048], P(('groups', 'fsdp')), parts along dimension 0
There are 2 independent parts, one for each index of `groups`. A program takes and returns all parts, laid end to end along the dimension named above; an argument that names none is the same for every part. Nothing has to cross between parts.
Inputs may be any that keep to these rules, and one draw needn't show every extreme that they name: `tenant`: adapter ids, one for each block of 64 tokens.
All inputs are finite; a program needn't handle non-finite values.
Results may differ from a plain program's by a relative error of at most 0.0051.
Values may be sent and summed in bfloat16 or wider, within the bound.
No kernel may reach another device: no remote copies, remote signals or barrier semaphores. Data moves between devices by JAX's collectives and lax.ppermute only.
A program may use at most 128 MiB of HBM per device.

v0:
```python
import jax
import jax.numpy as jnp
from jax import lax
from jax.sharding import PartitionSpec as P

RANK = 64
BLK = 64


adapter_scale = 0.5
norm_eps = 1e-05


def block_split(matrix, blocks):
    return matrix.reshape(blocks, matrix.shape[0] // blocks, matrix.shape[1])


def low_part(columns, factor_rows, blocks):
    return jnp.einsum(
        "yci,iya->yca",
        block_split(columns, blocks),
        factor_rows.reshape(factor_rows.shape[0], blocks, RANK),
        preferred_element_type=jnp.float32,
    )


def back_part(scaled_update, factor_rows, blocks):
    product = jnp.einsum(
        "pvq,opq->pvo",
        scaled_update,
        factor_rows.reshape(factor_rows.shape[0], blocks, RANK),
        preferred_element_type=jnp.float32,
    )
    return product.reshape(-1, factor_rows.shape[0])


def on_device(tokens, upstream, norm_gain, value_weight, down_factor, up_factor, tenant):
    token_rows = tokens.shape[0]
    blocks = token_rows // BLK
    features = tokens.shape[1]
    value_width = upstream.shape[1]
    adapters = down_factor.shape[1] // RANK
    wide_tokens = tokens.astype(jnp.float32)
    inverse = lax.rsqrt(jnp.mean(wide_tokens * wide_tokens, axis=1, keepdims=True) + norm_eps)
    normed = (wide_tokens * inverse * norm_gain).astype(jnp.bfloat16)
    normalized_blocks = block_split(normed, blocks)
    upstream_blocks = block_split(upstream, blocks)
    down_table = jnp.take(
        down_factor.reshape(down_factor.shape[0], adapters, RANK), tenant, axis=1
    ).reshape(down_factor.shape[0], -1)
    up_table = jnp.take(
        up_factor.reshape(up_factor.shape[0], adapters, RANK), tenant, axis=1
    ).reshape(up_factor.shape[0], -1)
    down_mine, up_mine = (
        lax.all_to_all(down_table, "fsdp", split_axis=1, concat_axis=0, tiled=True),
        lax.all_to_all(up_table, "fsdp", split_axis=1, concat_axis=0, tiled=True),
    )
    up_blocks = up_mine.reshape(value_width, blocks, RANK)
    mixed_output = jnp.einsum(
        "bkv,vbr->bkr", upstream_blocks, up_blocks, preferred_element_type=jnp.float32
    )
    scaled_update = (adapter_scale * mixed_output).astype(jnp.bfloat16)
    piece = lax.all_gather(value_weight, "fsdp", axis=0, tiled=True)
    value_total = jnp.dot(normed, piece, preferred_element_type=jnp.float32)
    result = lax.dot_general(
        upstream, piece, (((1,), (1,)), ((), ())), preferred_element_type=jnp.float32
    )
    back = result
    low_sum = low_part(normed, down_mine, blocks)
    back = back + back_part(scaled_update, down_mine, blocks)
    low_rank_rows = low_sum.astype(jnp.bfloat16)
    adapter_branch = jnp.einsum(
        "bkr,vbr->bkv", low_rank_rows, up_blocks, preferred_element_type=jnp.float32
    ).reshape(token_rows, value_width)
    adapted_values = (value_total + adapter_scale * adapter_branch).astype(jnp.bfloat16)
    gained = norm_gain * back
    inner = jnp.sum(gained * wide_tokens, axis=1, keepdims=True)
    grad_tokens = (
        inverse * gained - wide_tokens * (inverse * inverse * inverse) * inner / features
    ).astype(jnp.bfloat16)
    term_down = jnp.einsum(
        "mao,mah->omh", normalized_blocks, scaled_update, preferred_element_type=jnp.float32
    ).reshape(features, blocks * RANK)
    up_contribution = adapter_scale * jnp.einsum(
        "bkv,bkr->vbr", upstream_blocks, low_rank_rows, preferred_element_type=jnp.float32
    ).reshape(value_width, blocks * RANK)
    down_received, up_received = (
        lax.all_to_all(term_down, "fsdp", split_axis=0, concat_axis=1, tiled=True),
        lax.all_to_all(up_contribution, "fsdp", split_axis=0, concat_axis=1, tiled=True),
    )
    owner_table = (tenant[:, None] == jnp.arange(adapters, dtype=jnp.int32)[None, :]).astype(
        jnp.float32
    )
    grad_down = jnp.einsum(
        "kqr,qa->kar",
        down_received.reshape(down_received.shape[0], -1, RANK),
        owner_table,
        precision=lax.Precision.HIGHEST,
    ).reshape(down_received.shape[0], adapters * RANK)
    grad_up = jnp.einsum(
        "kqr,qa->kar",
        up_received.reshape(up_received.shape[0], -1, RANK),
        owner_table,
        precision=lax.Precision.HIGHEST,
    ).reshape(up_received.shape[0], adapters * RANK)
    return (adapted_values, grad_tokens, grad_down, grad_up)


def solution(mesh):
    in_specs = (
        P(("groups", "fsdp"), None),
        P(("groups", "fsdp"), None),
        P(),
        P("fsdp", None),
        P("fsdp", None),
        P("fsdp", None),
        P("groups"),
    )
    out_specs = (
        P(("groups", "fsdp"), None),
        P(("groups", "fsdp"), None),
        P(("groups", "fsdp"), None),
        P(("groups", "fsdp"), None),
    )
    return jax.shard_map(
        on_device, mesh=mesh, in_specs=in_specs, out_specs=out_specs, check_vma=False
    )
```

profile of v0, /device:TPU:15, one launch (start us, length us, event | category | flops | bytes accessed | tf_op | source)
XLA Modules:
  0.0 344.0 jit_solution(13918858231570661229)
XLA Ops:
  8.9 1.5 reshape.113
  13.3 6.6 %all-to-all-start.1 = ((bf16[64,16,128]{2,0,1:T(8,128)(2,1)}), bf16[64,16,128]{2,0,1:T(8,128)(2,1)S(1)}, u32[]{:S(2)}, u32[]{:S(2)}) async-start(bf16[64,16,128]{2,0,1:T(8,128)(2,1)} %copy.42), calls=%async_computation.1 | async-start | bytes 524288 | tf_op jit(solution)/shard_map/all_to_all | solution.py:56
  19.8 3.1 copy.38
  22.9 2.0 gather_fusion
  24.9 2.7 broadcast_select_fusion
  27.7 5.6 %all-to-all-done.1 = bf16[64,16,128]{2,0,1:T(8,128)(2,1)S(1)} async-done(((bf16[64,16,128]{2,0,1:T(8,128)(2,1)}), bf16[64,16,128]{2,0,1:T(8,128)(2,1)S(1)}, u32[]{:S(2)}, u32[]{:S(2)}) %all-to-all-start.1) | async-done | bytes 262176 | tf_op jit(solution)/shard_map/all_to_all | solution.py:56
  33.3 6.2 %all-to-all-start = ((bf16[512,16,128]{0,2,1:T(8,128)(2,1)}), bf16[512,16,128]{0,2,1:T(8,128)(2,1)S(1)}, u32[]{:S(2)}, u32[]{:S(2)}) async-start(bf16[512,16,128]{0,2,1:T(8,128)(2,1)} %broadcast_select_fusion), calls=%async_computation | async-start | bytes 4194304 | tf_op jit(solution)/shard_map/all_to_all | solution.py:55
  40.4 78.6 %all-to-all-done = bf16[512,16,128]{0,2,1:T(8,128)(2,1)S(1)} async-done(((bf16[512,16,128]{0,2,1:T(8,128)(2,1)}), bf16[512,16,128]{0,2,1:T(8,128)(2,1)S(1)}, u32[]{:S(2)}, u32[]{:S(2)}) %all-to-all-start) | async-done | bytes 2097184 | tf_op jit(solution)/shard_map/all_to_all | solution.py:55
  119.0 2.5 copy.39
  121.5 2.9 reshape.112
  124.4 2.8 fusion.22
  127.1 49.6 %all-gather.2.cloned.1.call-done = bf16[8192,1024]{1,0:T(8,128)(2,1)} async-done(((bf16[512,1024]{1,0:T(8,128)(2,1)}), bf16[8192,1024]{1,0:T(8,128)(2,1)}) %all-gather.2.cloned.1.call-update) | async-done | bytes 16777232 | tf_op jit(solution)/shard_map/all_gather | solution.py:63
  176.8 15.4 %fusion.8 = (f32[128]{0:T(128)S(1)}, f32[128]{0:T(128)S(1)}, f32[128,8192]{1,0:T(8,128)}) fusion(bf16[128,8192]{1,0:T(8,128)(2,1)} %param.7, f32[128,8192]{1,0:T(8,128)} %bitcast.62, bf16[128,1024]{1,0:T(8,128)(2,1)S(1)} %copy-done, bf16[8192,1024]{1,0:T(8,128)(2,1)} %all-gather.2.cloned.1.call-done, f32[8192]{0:T(1024)S(1)} %copy-done.6), kind=kOutput, calls=%fused_computation.15 | convolution fusion | flops 2154823680 | bytes 27558912 | tf_op jit(solution)/shard_map/dot_general | solution.py:65
  192.2 5.7 %fusion.7 = (bf16[128,8192]{1,0:T(8,128)(2,1)}, bf16[128,8192]{1,0:T(8,128)(2,1)S(1)}) fusion(bf16[128,8192]{1,0:T(8,128)(2,1)} %param.7, f32[128,8192]{1,0:T(8,128)} %get-tuple-element.22, f32[128]{0:T(128)S(1)} %get-tuple-element.16, f32[128]{0:T(128)S(1)} %get-tuple-element.20, f32[128]{0:T(128)S(1)} %get-tuple-element.21, f32[8192]{0:T(1024)S(1)} %copy-done.6), kind=kLoop, calls=%fused_computation.14 | loop fusion | flops 10485760 | bytes 10520064 | tf_op jit(solution)/shard_map/convert_element_type | solution.py:80
  202.3 7.1 %all-to-all-start.3 = ((f32[16,64,128]{2,1,0:T(8,128)}), f32[16,64,128]{2,1,0:T(8,128)S(1)}, u32[]{:S(2)}, u32[]{:S(2)}) async-start(f32[16,64,128]{2,1,0:T(8,128)} %copy.49), calls=%async_computation.3 | async-start | bytes 1048576 | tf_op jit(solution)/shard_map/all_to_all | solution.py:89
  210.0 3.3 copy.55
  213.3 4.4 %copy.45 = f32[16,512,128]{1,2,0:T(8,128)} copy(f32[16,512,128]{1,0,2:T(8,128)S(1)} %bitcast.60) | data formatting | bytes 8388608 | tf_op jit(solution)/shard_map/all_to_all | solution.py:88
  217.7 5.2 %all-to-all-done.3 = f32[16,64,128]{2,1,0:T(8,128)S(1)} async-done(((f32[16,64,128]{2,1,0:T(8,128)}), f32[16,64,128]{2,1,0:T(8,128)S(1)}, u32[]{:S(2)}, u32[]{:S(2)}) %all-to-all-start.3) | async-done | bytes 524320 | tf_op jit(solution)/shard_map/all_to_all | solution.py:89
  222.9 5.3 %all-to-all-start.2 = ((f32[16,512,128]{1,2,0:T(8,128)}), f32[16,512,128]{1,2,0:T(8,128)}, u32[]{:S(2)}, u32[]{:S(2)}) async-start(f32[16,512,128]{1,2,0:T(8,128)} %copy.45), calls=%async_computation.2 | async-start | bytes 8388608 | tf_op jit(solution)/shard_map/all_to_all | solution.py:88
  228.4 8.8 %fusion.15 = bf16[128,1024]{1,0:T(8,128)(2,1)} fusion(f32[128,1024]{1,0:T(8,128)S(1)} %bitcast.64, bf16[128,8192]{1,0:T(8,128)(2,1)S(1)} %get-tuple-element.19, bf16[8192,1024]{1,0:T(8,128)(2,1)} %all-gather.2.cloned.1.call-done), kind=kOutput, calls=%fused_computation.25 | convolution fusion | flops 2147745792 | bytes 19660800 | tf_op jit(solution)/shard_map/dot_general | solution.py:64
  239.6 81.1 %all-to-all-done.2 = f32[16,512,128]{1,2,0:T(8,128)} async-done(((f32[16,512,128]{1,2,0:T(8,128)}), f32[16,512,128]{1,2,0:T(8,128)}, u32[]{:S(2)}, u32[]{:S(2)}) %all-to-all-start.2) | async-done | bytes 4194336 | tf_op jit(solution)/shard_map/all_to_all | solution.py:88
  320.7 6.7 %fusion.11 = f32[512,32,64]{0,1,2:T(8,128)S(1)} fusion(f32[512,32,64]{0,2,1:T(8,128)} %bitcast.13, s32[32]{0:T(128)S(1)} %copy-done.7), kind=kOutput, calls=%fused_computation.18 | convolution fusion | flops 402654208 | bytes 8388736 | tf_op jit(solution)/shard_map/kqr,qa->kar/dot_general | solution.py:94
  327.4 4.4 %copy.47 = f32[512,32,64]{0,2,1:T(8,128)} copy(f32[512,32,64]{0,1,2:T(8,128)S(1)} %fusion.11) | data formatting | bytes 8388608 | tf_op jit(solution)/shard_map/kqr,qa->kar/transpose | solution.py:94
  331.8 5.4 %copy.51 = f32[512,2048]{1,0:T(8,128)} copy(f32[512,2048]{0,1:T(8,128)} %bitcast.61) | data formatting | bytes 8388608
  (44 shorter events, 12.9 us)
Async XLA Ops:
  7.2 33.0 %copy-start = (bf16[128,1024]{1,0:T(8,128)(2,1)S(1)}, bf16[128,1024]{1,0:T(8,128)(2,1)}, u32[]{:S(2)}) copy-start(bf16[128,1024]{1,0:T(8,128)(2,1)} %param.8) | copy-start | bytes 786436
  7.2 169.6 %all-gather.2.cloned.1.call-start = ((), (), s32[]{:S(2)}) async-start(), calls=%async_computation.4 | async-start | bytes 17825792 | tf_op jit(solution)/shard_map/all_gather | solution.py:63
  13.3 20.0 %all-to-all-start.1 = ((bf16[64,16,128]{2,0,1:T(8,128)(2,1)}), bf16[64,16,128]{2,0,1:T(8,128)(2,1)S(1)}, u32[]{:S(2)}, u32[]{:S(2)}) async-start(bf16[64,16,128]{2,0,1:T(8,128)(2,1)} %copy.42), calls=%async_computation.1 | async-start | bytes 524288 | tf_op jit(solution)/shard_map/all_to_all | solution.py:56
  33.3 85.7 %all-to-all-start = ((bf16[512,16,128]{0,2,1:T(8,128)(2,1)}), bf16[512,16,128]{0,2,1:T(8,128)(2,1)S(1)}, u32[]{:S(2)}, u32[]{:S(2)}) async-start(bf16[512,16,128]{0,2,1:T(8,128)(2,1)} %broadcast_select_fusion), calls=%async_computation | async-start | bytes 4194304 | tf_op jit(solution)/shard_map/all_to_all | solution.py:55
  40.2 84.2 %copy-start.4 = (bf16[1024,2,64]{0,2,1:T(8,128)(2,1)}, bf16[1024,2,64]{0,2,1:T(8,128)(2,1)S(1)}, u32[]{:S(2)}) copy-start(bf16[1024,2,64]{0,2,1:T(8,128)(2,1)S(1)} %copy.54) | copy-start | bytes 786436
  124.4 67.9 %copy-start.2 = (bf16[8192,2,64]{0,2,1:T(8,128)(2,1)}, bf16[8192,2,64]{0,2,1:T(8,128)(2,1)S(1)}, u32[]{:S(2)}) copy-start(bf16[8192,2,64]{0,2,1:T(8,128)(2,1)S(1)} %reshape.112) | copy-start | bytes 6291460
  124.4 52.4 %copy-start.6 = (f32[8192]{0:T(1024)S(1)}, f32[8192]{0:T(1024)}, u32[]{:S(2)}) copy-start(f32[8192]{0:T(1024)} %param.9) | copy-start | bytes 98308
  192.2 5.8 %copy-start.3 = (bf16[8192,2,64]{0,2,1:T(8,128)(2,1)S(1)}, bf16[8192,2,64]{0,2,1:T(8,128)(2,1)}, u32[]{:S(2)}) copy-start(bf16[8192,2,64]{0,2,1:T(8,128)(2,1)} %copy-done.2) | copy-start | bytes 6291460
  202.3 20.7 %all-to-all-start.3 = ((f32[16,64,128]{2,1,0:T(8,128)}), f32[16,64,128]{2,1,0:T(8,128)S(1)}, u32[]{:S(2)}, u32[]{:S(2)}) async-start(f32[16,64,128]{2,1,0:T(8,128)} %copy.49), calls=%async_computation.3 | async-start | bytes 1048576 | tf_op jit(solution)/shard_map/all_to_all | solution.py:89
  217.7 10.5 %copy-start.5 = (bf16[1024,2,64]{0,2,1:T(8,128)(2,1)S(1)}, bf16[1024,2,64]{0,2,1:T(8,128)(2,1)}, u32[]{:S(2)}) copy-start(bf16[1024,2,64]{0,2,1:T(8,128)(2,1)} %copy-done.4) | copy-start | bytes 786436
  222.9 97.8 %all-to-all-start.2 = ((f32[16,512,128]{1,2,0:T(8,128)}), f32[16,512,128]{1,2,0:T(8,128)}, u32[]{:S(2)}, u32[]{:S(2)}) async-start(f32[16,512,128]{1,2,0:T(8,128)} %copy.45), calls=%async_computation.2 | async-start | bytes 8388608 | tf_op jit(solution)/shard_map/all_to_all | solution.py:88
  228.4 9.4 %copy-start.7 = (s32[32]{0:T(128)S(1)}, s32[32]{0:T(128)}, u32[]{:S(2)}) copy-start(s32[32]{0:T(128)} %param.13) | copy-start | bytes 388
  331.8 5.4 %copy-start.1 = (bf16[128,1024]{1,0:T(8,128)(2,1)S(1)}, bf16[128,1024]{1,0:T(8,128)(2,1)}, u32[]{:S(2)}) copy-start(bf16[128,1024]{1,0:T(8,128)(2,1)} %param.8) | copy-start | bytes 786436
Sparse Core Ops, SparseCore 0:
  10.2 166.5 all-gather.1
where the time goes:
time: 345 us; the launch traced here: 344 us
  waiting for transfers between devices  221 us (64%)
  matrix products  37.2 us (11%)
  local copies, waits for them, and re-layouts  36.7 us (11%)
  starting transfers between devices  25.2 us (7%)
  between operations  14.3 us (4%)
  other arithmetic  9.86 us (3%)
    all_to_all x1, waiting for transfers between devices, on_device(): lax.all_to_all(term_down, 'fsdp', split_axis=0, concat_axis=1, tiled=True)  81.1 us
    all_to_all x1, waiting for transfers between devices, on_device(): lax.all_to_all(down_table, 'fsdp', split_axis=1, concat_axis=0, tiled=True)  78.6 us
    all_gather x1, waiting for transfers between devices, on_device(): piece = lax.all_gather(value_weight, 'fsdp', axis=0, tiled=True)  49.6 us
    dot_general x1, matrix products, on_device(): lax.dot_general(upstream, piece, (((1,), (1,)), ((), ())), preferred_elem...  15.4 us
    unnamed x19, local copies, waits for them, and re-layouts  11.8 us
    dot_general x1, matrix products, on_device(): value_total = jnp.dot(normed, piece, preferred_element_type=jnp.float32)  8.83 us
    all_to_all x1, starting transfers between devices, on_device(): lax.all_to_all(up_contribution, 'fsdp', split_axis=0, concat_axis=1, tile...  7.07 us
  transfers between devices with their start and end apart: 5, of which 5 were waited for; matrix products, arithmetic and copies ran while one was open for 12% of the time, Pallas kernels for 0%

commit v1 on v0

v1 whole, which is shorter than its diff:
```python
import functools

import jax
import jax.numpy as jnp
import numpy as np
from jax import lax
from jax.experimental import pallas as pl
from jax.experimental.pallas import tpu as pltpu
from jax.sharding import Mesh
from jax.sharding import PartitionSpec as P

RANK = 64
BLK = 64

adapter_scale = 0.5
norm_eps = 1e-05


def over_chips(value, mask):
    chips = lax.axis_size("chip")
    return lax.ppermute(value, "chip", [(i, i ^ mask) for i in range(chips)])


def over_cores(value):
    return lax.ppermute(value, "core", [(0, 1), (1, 0)])


def slot_masks(chips):
    masks = [0]
    step = chips // 2
    while step:
        masks = masks + [m ^ step for m in masks]
        step //= 2
    return masks


def gather_over_chips(mine, chips):
    held, beside = mine, [over_chips(mine, 1)]
    step = chips // 2
    while step > 1:
        arrived = over_chips(held, step)
        beside.append(over_chips(arrived, 1))
        held = jnp.concatenate([held, arrived])
        step //= 2
    return jnp.concatenate([held] + beside)


def sum_over_chips(parts, chips):
    step = 1
    while step < chips:
        half = parts.shape[0] // 2
        arrived = over_chips(parts[half:].astype(jnp.bfloat16), step)
        parts = parts[:half] + arrived.astype(jnp.float32)
        step *= 2
    return parts[0]


def factor_grad_kernel(blocks, scale, tenant_ref, rows_ref, update_ref, out_ref):
    out_ref[...] = jnp.zeros_like(out_ref)
    lane = lax.broadcasted_iota(jnp.int32, (BLK, 2 * RANK), 1)

    def step(b, carry):
        adapter = tenant_ref[b]
        tokens = pl.ds(pl.multiple_of(b * BLK, BLK), BLK)
        update = update_ref[tokens, :]
        update = jnp.where(lane // RANK == adapter % 2, update, jnp.zeros_like(update))
        term = lax.dot_general(
            rows_ref[tokens, :], update, (((0,), (0,)), ((), ())), preferred_element_type=jnp.float32
        )
        columns = pl.ds(pl.multiple_of((adapter // 2) * 2 * RANK, 2 * RANK), 2 * RANK)
        out_ref[:, columns] += scale * term
        return carry

    lax.fori_loop(0, blocks, step, 0)


def factor_grad(rows, update, tenants, width, scale):
    blocks = tenants.shape[0]
    vmem = pl.BlockSpec(memory_space=pltpu.VMEM)
    return pl.pallas_call(
        functools.partial(factor_grad_kernel, blocks, scale),
        out_shape=jax.ShapeDtypeStruct((rows.shape[1], width), jnp.float32),
        in_specs=[pl.BlockSpec(memory_space=pltpu.SMEM), vmem, vmem],
        out_specs=vmem,
        compiler_params=pltpu.CompilerParams(vmem_limit_bytes=40 * 1024 * 1024),
        cost_estimate=pl.CostEstimate(
            flops=2 * rows.size * 2 * RANK,
            bytes_accessed=2 * rows.size + 4 * rows.shape[1] * width,
            transcendentals=0,
        ),
    )(tenants, rows, jnp.concatenate([update, update], axis=1))


def token_grad_kernel(
    slots, width, features, chip_ref, tokens_ref, gain_ref, inverse_ref, back_ref, out_ref, total
):
    inverse = inverse_ref[...]
    total[...] = jnp.zeros_like(total)

    def columns_of(s):
        return pl.ds(pl.multiple_of(chip_ref[s] * width, width), width)

    def add(s, carry):
        columns = columns_of(s)
        gained = gain_ref[:, columns] * back_ref[s].astype(jnp.float32)
        wide = tokens_ref[:, columns].astype(jnp.float32)
        total[...] += jnp.sum(gained * wide, axis=1, keepdims=True)
        return carry

    lax.fori_loop(0, slots, add, 0)
    cubed = inverse * inverse * inverse
    inner = total[...] / features

    def write(s, carry):
        columns = columns_of(s)
        gained = gain_ref[:, columns] * back_ref[s].astype(jnp.float32)
        wide = tokens_ref[:, columns].astype(jnp.float32)
        out_ref[:, columns] = (inverse * gained - wide * cubed * inner).astype(out_ref.dtype)
        return carry

    lax.fori_loop(0, slots, write, 0)


def token_grad(chip_of_slot, tokens, gain, inverse, back):
    slots, rows, width = back.shape
    features = tokens.shape[1]
    vmem = pl.BlockSpec(memory_space=pltpu.VMEM)
    return pl.pallas_call(
        functools.partial(token_grad_kernel, slots, width, features),
        out_shape=jax.ShapeDtypeStruct(tokens.shape, tokens.dtype),
        in_specs=[pl.BlockSpec(memory_space=pltpu.SMEM), vmem, vmem, vmem, vmem],
        out_specs=vmem,
        scratch_shapes=[pltpu.VMEM((rows, 1), jnp.float32)],
        compiler_params=pltpu.CompilerParams(vmem_limit_bytes=32 * 1024 * 1024),
        cost_estimate=pl.CostEstimate(
            flops=10 * tokens.size, bytes_accessed=6 * tokens.size, transcendentals=0
        ),
    )(chip_of_slot, tokens, gain, inverse, back)


def on_device(tokens, upstream, norm_gain, value_weight, down_factor, up_factor, tenant):
    chips = lax.axis_size("chip")
    chip, core = lax.axis_index("chip"), lax.axis_index("core")
    masks = slot_masks(chips)
    chip_of_slot = chip ^ jnp.asarray(masks, jnp.int32)
    slot_of_chip = jnp.asarray(np.argsort(masks), jnp.int32)[chip ^ jnp.arange(chips, dtype=jnp.int32)]

    token_rows, features = tokens.shape
    blocks = token_rows // BLK
    value_width = upstream.shape[1]
    adapters = down_factor.shape[1] // RANK
    width = features // chips
    value_rows = up_factor.shape[0]

    tenants = tenant.reshape(chips, 2, blocks)[chip_of_slot]
    tenants_mine, tenants_other = tenants[:, core].reshape(-1), tenants[:, 1 - core].reshape(-1)

    upstream_all = gather_over_chips(upstream, chips)

    def both_cores(mine):
        other = over_cores(mine)
        pair = jnp.stack([jnp.where(core == 0, mine, other), jnp.where(core == 0, other, mine)])
        return pair.reshape((2 * mine.shape[0],) + mine.shape[1:])

    weight = both_cores(value_weight)
    down = both_cores(down_factor)

    up_table = jnp.take(
        up_factor.reshape(value_rows, adapters, RANK), tenant, axis=1, mode="clip"
    ).reshape(value_rows, -1)
    up_mine = lax.all_to_all(up_table, ("chip", "core"), split_axis=1, concat_axis=0, tiled=True)
    up_blocks = up_mine.reshape(value_width, blocks, RANK)

    wide_tokens = tokens.astype(jnp.float32)
    inverse = lax.rsqrt(jnp.mean(wide_tokens * wide_tokens, axis=1, keepdims=True) + norm_eps)
    normed = (wide_tokens * inverse * norm_gain).astype(jnp.bfloat16)

    def columns_for(mask):
        return lax.dynamic_slice_in_dim(normed, (chip ^ mask) * width, width, 1)

    arrived = [over_chips(columns_for(m), m) if m else columns_for(m) for m in masks]
    normed_all = jnp.concatenate(arrived)

    upstream_blocks = upstream.reshape(blocks, BLK, value_width)
    mixed_output = jnp.einsum("bkv,vbr->bkr", upstream_blocks, up_blocks, preferred_element_type=jnp.float32)
    scaled_mine = (adapter_scale * mixed_output).astype(jnp.bfloat16).reshape(token_rows, RANK)
    scaled_all = lax.all_gather(scaled_mine, ("chip", "core"), axis=0)
    scaled_all = scaled_all.reshape(chips, 2, token_rows, RANK)[chip_of_slot]
    scaled_core = scaled_all[:, core].reshape(-1, RANK)
    scaled_other = scaled_all[:, 1 - core].reshape(-1, RANK)

    down_table = jnp.take(down.reshape(width, adapters, RANK), tenants_mine, axis=1, mode="clip")
    core_blocks = tenants_mine.shape[0]

    back = lax.dot_general(
        upstream_all, weight, (((1,), (1,)), ((), ())), preferred_element_type=jnp.float32
    )
    back = back + jnp.einsum(
        "pvq,opq->pvo",
        scaled_core.reshape(core_blocks, BLK, RANK),
        down_table,
        preferred_element_type=jnp.float32,
    ).reshape(-1, width)
    back = back.astype(jnp.bfloat16).reshape(chips, token_rows, width)
    back_mine = jnp.stack([over_chips(back[s], m) if m else back[s] for s, m in enumerate(masks)])

    values = jnp.dot(normed_all, weight, preferred_element_type=jnp.float32)
    values = sum_over_chips(values.reshape(chips, token_rows, value_width), chips)
    low = jnp.einsum(
        "yci,iya->yca",
        normed_all.reshape(core_blocks, BLK, width),
        down_table,
        preferred_element_type=jnp.float32,
    ).reshape(chips, token_rows, RANK)
    low = lax.psum(low[slot_of_chip], "chip").astype(jnp.bfloat16)
    low_mine = lax.dynamic_index_in_dim(low, chip, 0, keepdims=False).reshape(blocks, BLK, RANK)
    adapter_branch = jnp.einsum(
        "bkr,vbr->bkv", low_mine, up_blocks, preferred_element_type=jnp.float32
    ).reshape(token_rows, value_width)
    adapted_values = (values + adapter_scale * adapter_branch).astype(jnp.bfloat16)

    tenants_both = jnp.concatenate([tenants_mine, tenants_other])

    def my_columns(value, first, count):
        kept = lax.dynamic_slice_in_dim(value, first + core * count, count, 1)
        sent = lax.dynamic_slice_in_dim(value, first + (1 - core) * count, count, 1)
        return jnp.concatenate([kept, over_cores(sent)])

    grad_down = factor_grad(
        my_columns(normed_all, 0, width // 2),
        jnp.concatenate([scaled_core, scaled_other]),
        tenants_both,
        adapters * RANK,
        1.0,
    )
    low_slots = low[chip_of_slot].reshape(-1, RANK)
    grad_up = factor_grad(
        my_columns(upstream_all, chip * 2 * value_rows, value_rows),
        jnp.concatenate([low_slots, over_cores(low_slots)]),
        tenants_both,
        adapters * RANK,
        adapter_scale,
    )

    grad_tokens = token_grad(chip_of_slot, tokens, norm_gain.reshape(1, -1), inverse, back_mine)
    return (adapted_values, grad_tokens, grad_down, grad_up)


def solution(mesh):
    groups, shards = mesh.shape["groups"], mesh.shape["fsdp"]
    chip_mesh = Mesh(mesh.devices.reshape(groups, shards // 2, 2), ("groups", "chip", "core"))
    own = ("chip", "core")
    everywhere = P(("groups",) + own, None)
    in_specs = (everywhere, everywhere, P(), P(own, None), P(own, None), P(own, None), P("groups"))
    out_specs = (everywhere,) * 4
    return jax.shard_map(
        on_device, mesh=chip_mesh, in_specs=in_specs, out_specs=out_specs, check_vma=False
    )
```

time: 345 us -> 288 us (0.83)
  the two profiles are of different devices: /device:TPU:15 before, /device:TPU:0 now
where the time goes in v1:
time: 288 us; the launch traced here: 287 us
  local copies, waits for them, and re-layouts  68.8 us (24%)
  blocking collectives  65.8 us (23%)
  waiting for transfers between devices  55 us (19%)
  starting transfers between devices  45.2 us (16%)
  Pallas kernels  21.9 us (8%)
  other arithmetic  16.7 us (6%)
  matrix products  12.2 us (4%)
    ppermute x22, waiting for transfers between devices, over_chips(): return lax.ppermute(value, 'chip', [(i, i ^ mask) for i in range(chips)])  54.9 us
    psum x1, blocking collectives, on_device(): low = lax.psum(low[slot_of_chip], 'chip').astype(jnp.bfloat16)  41.5 us
    ppermute x22, starting transfers between devices, over_chips(): return lax.ppermute(value, 'chip', [(i, i ^ mask) for i in range(chips)])  41.2 us
    all_gather x1, blocking collectives, on_device(): scaled_all = lax.all_gather(scaled_mine, ('chip', 'core'), axis=0)  24.2 us
    unnamed x48, local copies, waits for them, and re-layouts  18.5 us
    pallas_call x2, Pallas kernels, factor_grad(): pl.pallas_call(functools.partial(factor_grad_kernel, blocks, scale), out_...  17.1 us
    another operation x1, local copies, waits for them, and re-layouts, both_cores(): jnp.stack([jnp.where(core == 0, mine, other), jnp.where(core == 0, other,...  11.2 us
    another operation x1, local copies, waits for them, and re-layouts, on_device(): down.reshape(width, adapters, RANK)  7.77 us
  transfers between devices with their start and end apart: 28, of which 7 were waited for; matrix products, arithmetic and copies ran while one was open for 32% of the time, Pallas kernels for 8%

profile of v1, /device:TPU:0, one launch (start us, length us, event | category | flops | bytes accessed | tf_op | source)
XLA Modules:
  0.0 286.8 jit_solution(4739304833305595708)
XLA Ops:
  0.7 4.1 %collective-permute-start.12 = (bf16[128,1024]{1,0:T(8,128)(2,1)}, bf16[128,1024]{1,0:T(8,128)(2,1)}, u32[]{:S(2)}, u32[]{:S(2)}) collective-permute-start(bf16[128,1024]{1,0:T(8,128)(2,1)} %param.10), channel_id=1, source_target_pairs={{0,8},{2,10},{4,12},{6,14},{8,0},{10,2},{12,4},{14,6},{1,9},{3,11}... | collective-permute-start | bytes 786440 | tf_op jit(solution)/shard_map/ppermute | solution.py:21
  18.9 3.5 %all-to-all-start = ((bf16[64,16,128]{2,0,1:T(8,128)(2,1)}), bf16[64,16,128]{2,0,1:T(8,128)(2,1)S(1)}, u32[]{:S(2)}, u32[]{:S(2)}) async-start(bf16[64,16,128]{2,0,1:T(8,128)(2,1)} %copy.34), calls=%async_computation | async-start | bytes 524288 | tf_op jit(solution)/shard_map/all_to_all | solution.py:171
  29.6 7.9 %collective-permute-done = bf16[128,1024]{1,0:T(8,128)(2,1)} collective-permute-done((bf16[128,1024]{1,0:T(8,128)(2,1)}, bf16[128,1024]{1,0:T(8,128)(2,1)}, u32[]{:S(2)}, u32[]{:S(2)}) %collective-permute-start) | collective-permute-done | bytes 262176 | tf_op jit(solution)/shard_map/ppermute | solution.py:21
  40.0 3.4 %collective-permute-start.5 = (bf16[128,1024]{1,0:T(8,128)(2,1)S(1)}, bf16[128,1024]{1,0:T(8,128)(2,1)S(1)}, u32[]{:S(2)}, u32[]{:S(2)}) collective-permute-start(bf16[128,1024]{1,0:T(8,128)(2,1)S(1)} %copy-done.13), channel_id=1, source_target_pairs={{0,6},{2,4},{4,2},{6,0},{8,14},{10,12},{12,10},{14,8},{1,7},{3,5},... | collective-permute-start | bytes 786440 | tf_op jit(solution)/shard_map/ppermute | solution.py:21
  49.9 14.6 %collective-permute-done.4 = bf16[128,1024]{1,0:T(8,128)(2,1)S(1)} collective-permute-done((bf16[128,1024]{1,0:T(8,128)(2,1)}, bf16[128,1024]{1,0:T(8,128)(2,1)S(1)}, u32[]{:S(2)}, u32[]{:S(2)}) %collective-permute-start.4) | collective-permute-done | bytes 262176 | tf_op jit(solution)/shard_map/ppermute | solution.py:21
  66.7 2.6 constant_dynamic-slice_fusion.4
  73.6 24.2 %all_gather.3 = bf16[16,128,64]{1,2,0:T(8,128)(2,1)} all-gather(bf16[1,128,64]{1,2,0:T(8,128)(2,1)} %all_gather_reshape.3), channel_id=1, replica_groups=mesh['groups'=2,'chip'=8,'core'=2] {'chip','core'}, dimensions={0}, use_global_device_ids=true | all-gather | bytes 278528 | tf_op jit(solution)/shard_map/all_gather | solution.py:187
  125.6 10.0 %shard_map.121 = f32[512,2048]{1,0:T(8,128)} custom-call(s32[32]{0:T(128)S(1)} %pad_add_fusion.tenant_ref, bf16[2048,512]{1,0:T(8,128)(2,1)S(1)} %pad_maximum_fusion.2.rows_ref, bf16[2048,128]{1,0:T(8,128)(2,1)S(1)} %maximum_maximum_fusion.update_ref), custom_call_target="tpu_custom_call" | custom-call | flops 268435456 | bytes 6291456 | tf_op jit(solution)/shard_map/pallas_call | solution.py:80
  135.7 2.5 select_bitcast_fusion.1
  140.6 11.2 %copy.31 = bf16[2,512,2048]{1,0,2:T(2,128)(2,1)} copy(bf16[2,512,2048]{2,1,0:T(8,128)(2,1)} %pad_maximum_fusion) | data formatting | bytes 8388608 | tf_op jit(solution)/shard_map/stack | solution.py:162
  151.8 7.8 %reshape_reshape.3 = bf16[1024,32,64]{0,2,1:T(8,128)(2,1)} reshape(bf16[2,512,2048]{1,0,2:T(2,128)(2,1)} %copy.31) | data formatting | bytes 8388608 | tf_op jit(solution)/shard_map/reshape;reshape | solution.py:192
  159.6 4.2 %gather_fusion.1 = bf16[16,1024,64]{1,2,0:T(8,128)(2,1)} fusion(bf16[1024,32,64]{0,2,1:T(8,128)(2,1)} %reshape_reshape.3, s32[1024]{0:T(1024)S(1)} %pad_clamp_fusion.3), kind=kCustom, calls=%fused_computation.1 | custom fusion | bytes 4194368 | tf_op jit(solution)/shard_map/jit(_take)/gather | solution.py:192
  163.8 3.7 %fusion.4 = f32[16,64,64]{2,1,0:T(8,128)} fusion(bf16[16,64,1024]{2,1,0:T(8,128)(2,1)} %bitcast.83, bf16[16,1024,64]{1,2,0:T(8,128)(2,1)} %gather_fusion.1), kind=kOutput, calls=%fused_computation.18 | convolution fusion | flops 134217728 | bytes 4456448 | tf_op jit(solution)/shard_map/yci,iya->yca/dot_general | solution.py:209
  167.5 2.6 gather_fusion.3
  170.1 41.5 %all-reduce.1 = bf16[8,128,64]{2,1,0:T(8,128)(2,1)S(1)} all-reduce(f32[8,128,64]{2,1,0:T(8,128)} %gather_fusion.3), channel_id=1, replica_groups=mesh['groups'=2,'chip'=8,'core'=2] {'chip'}, use_global_device_ids=true, to_apply=%region_1.2 | all-reduce | flops 65536 | bytes 393216 | tf_op jit(solution)/shard_map/psum | solution.py:215
  219.6 3.3 %collective-permute-start.19 = (bf16[128,1024]{1,0:T(8,128)(2,1)S(1)}, bf16[128,1024]{1,0:T(8,128)(2,1)S(1)}, u32[]{:S(2)}, u32[]{:S(2)}) collective-permute-start(bf16[128,1024]{1,0:T(8,128)(2,1)S(1)} %get-tuple-element.16), channel_id=1, source_target_pairs={{0,12},{2,14},{4,8},{6,10},{8,4},{10,6},{12,0},{14,2},{1,13},{3,15... | collective-permute-start | bytes 786440 | tf_op jit(solution)/shard_map/ppermute | solution.py:21
  226.2 7.1 %shard_map.122 = f32[64,2048]{1,0:T(8,128)} custom-call(s32[32]{0:T(128)S(1)} %pad_add_fusion.tenant_ref, bf16[2048,64]{1,0:T(8,128)(2,1)S(1)} %pad_maximum_fusion.4.rows_ref, bf16[2048,128]{1,0:T(8,128)(2,1)S(1)} %maximum_maximum_fusion.1.update_ref), custom_call_target="tpu_custom_call" | custom-call | flops 33554432 | bytes 786432 | tf_op jit(solution)/shard_map/pallas_call | solution.py:80
  233.3 4.4 %collective-permute-start.22 = (bf16[128,1024]{1,0:T(8,128)(2,1)S(1)}, bf16[128,1024]{1,0:T(8,128)(2,1)S(1)}, u32[]{:S(2)}, u32[]{:S(2)}) collective-permute-start(bf16[128,1024]{1,0:T(8,128)(2,1)S(1)} %get-tuple-element.13), channel_id=1, source_target_pairs={{0,6},{2,4},{4,2},{6,0},{8,14},{10,12},{12,10},{14,8},{1,7},{3,5},... | collective-permute-start | bytes 786440 | tf_op jit(solution)/shard_map/ppermute | solution.py:21
  238.9 3.2 %collective-permute-start.23 = (bf16[128,1024]{1,0:T(8,128)(2,1)S(1)}, bf16[128,1024]{1,0:T(8,128)(2,1)S(1)}, u32[]{:S(2)}, u32[]{:S(2)}) collective-permute-start(bf16[128,1024]{1,0:T(8,128)(2,1)S(1)} %get-tuple-element.12), channel_id=1, source_target_pairs={{0,14},{2,12},{4,10},{6,8},{8,6},{10,4},{12,2},{14,0},{1,15},{3,13... | collective-permute-start | bytes 786440 | tf_op jit(solution)/shard_map/ppermute | solution.py:21
  242.1 7.3 %collective-permute-start.9 = (bf16[2,128,1024]{2,1,0:T(8,128)(2,1)S(1)}, bf16[2,128,1024]{2,1,0:T(8,128)(2,1)S(1)}, u32[]{:S(2)}, u32[]{:S(2)}) collective-permute-start(bf16[2,128,1024]{2,1,0:T(8,128)(2,1)S(1)} %slice.118), channel_id=1, source_target_pairs={{0,4},{2,6},{4,0},{6,2},{8,12},{10,14},{12,8},{14,10},{1,5},{3,7},... | collective-permute-start | bytes 1572872 | tf_op jit(solution)/shard_map/ppermute | solution.py:21
  249.4 12.7 %collective-permute-done.21 = bf16[128,1024]{1,0:T(8,128)(2,1)S(1)} collective-permute-done((bf16[128,1024]{1,0:T(8,128)(2,1)S(1)}, bf16[128,1024]{1,0:T(8,128)(2,1)S(1)}, u32[]{:S(2)}, u32[]{:S(2)}) %collective-permute-start.21) | collective-permute-done | bytes 262176 | tf_op jit(solution)/shard_map/ppermute | solution.py:21
  262.2 9.1 %collective-permute-done.9 = bf16[2,128,1024]{2,1,0:T(8,128)(2,1)S(1)} collective-permute-done((bf16[2,128,1024]{2,1,0:T(8,128)(2,1)S(1)}, bf16[2,128,1024]{2,1,0:T(8,128)(2,1)S(1)}, u32[]{:S(2)}, u32[]{:S(2)}) %collective-permute-start.9) | collective-permute-done | bytes 524320 | tf_op jit(solution)/shard_map/ppermute | solution.py:21
  272.0 4.7 %shard_map.120 = bf16[128,8192]{1,0:T(8,128)(2,1)} custom-call(s32[8]{0:T(128)S(1)} %get-tuple-element.33.chip_ref, bf16[128,8192]{1,0:T(8,128)(2,1)S(1)} %copy-done, f32[1,8192]{1,0:T(1,128)S(1)} %bitcast.82, f32[128,1]{1,0:T(8,128)S(1)} %copy.38.inverse_ref, bf16[8,128,1024]{2,1,0:T(8,128)(2,1)S(1)} %bitcast_dynamic-update-slice_fusion.back_ref), custom_call_target="tpu_custom_call" | custom-call | flops 10485760 | bytes 6291456 | tf_op jit(solution)/shard_map/pallas_call | solution.py:128
  276.8 9.2 %collective-permute-done.10 = bf16[1,128,1024]{2,1,0:T(8,128)(2,1)S(1)} collective-permute-done((bf16[1,128,1024]{2,1,0:T(8,128)(2,1)S(1)}, bf16[1,128,1024]{2,1,0:T(8,128)(2,1)S(1)}, u32[]{:S(2)}, u32[]{:S(2)}) %collective-permute-start.10) | collective-permute-done | bytes 262176 | tf_op jit(solution)/shard_map/ppermute | solution.py:21
  (153 shorter events, 80.6 us)
Async XLA Ops:
  0.7 23.6 %collective-permute-start.12 = (bf16[128,1024]{1,0:T(8,128)(2,1)}, bf16[128,1024]{1,0:T(8,128)(2,1)}, u32[]{:S(2)}, u32[]{:S(2)}) collective-permute-start(bf16[128,1024]{1,0:T(8,128)(2,1)} %param.10), channel_id=1, source_target_pairs={{0,8},{2,10},{4,12},{6,14},{8,0},{10,2},{12,4},{14,6},{1,9},{3,11}... | collective-permute-start | bytes 786440 | tf_op jit(solution)/shard_map/ppermute | solution.py:21
  4.8 104.3 %collective-permute-start.14 = (bf16[128,1024]{1,0:T(8,128)(2,1)}, bf16[128,1024]{1,0:T(8,128)(2,1)}, u32[]{:S(2)}, u32[]{:S(2)}) collective-permute-start(bf16[128,1024]{1,0:T(8,128)(2,1)} %param.10), channel_id=1, source_target_pairs={{0,2},{2,0},{4,6},{6,4},{8,10},{10,8},{12,14},{14,12},{1,3},{3,1},... | collective-permute-start | bytes 786440 | tf_op jit(solution)/shard_map/ppermute | solution.py:21
  10.4 27.2 %collective-permute-start = (bf16[128,1024]{1,0:T(8,128)(2,1)}, bf16[128,1024]{1,0:T(8,128)(2,1)}, u32[]{:S(2)}, u32[]{:S(2)}) collective-permute-start(bf16[128,1024]{1,0:T(8,128)(2,1)} %get-tuple-element.27), channel_id=1, source_target_pairs={{0,8},{2,10},{4,12},{6,14},{8,0},{10,2},{12,4},{14,6},{1,9},{3,11}... | collective-permute-start | bytes 786440 | tf_op jit(solution)/shard_map/ppermute | solution.py:21
  10.7 29.3 %collective-permute-start.1 = (bf16[128,1024]{1,0:T(8,128)(2,1)}, bf16[128,1024]{1,0:T(8,128)(2,1)}, u32[]{:S(2)}, u32[]{:S(2)}) collective-permute-start(bf16[128,1024]{1,0:T(8,128)(2,1)} %get-tuple-element.26), channel_id=1, source_target_pairs={{0,4},{2,6},{4,0},{6,2},{8,12},{10,14},{12,8},{14,10},{1,5},{3,7},... | collective-permute-start | bytes 786440 | tf_op jit(solution)/shard_map/ppermute | solution.py:21
  12.3 32.8 %collective-permute-start.2 = (bf16[128,1024]{1,0:T(8,128)(2,1)}, bf16[128,1024]{1,0:T(8,128)(2,1)}, u32[]{:S(2)}, u32[]{:S(2)}) collective-permute-start(bf16[128,1024]{1,0:T(8,128)(2,1)} %get-tuple-element.25), channel_id=1, source_target_pairs={{0,12},{2,14},{4,8},{6,10},{8,4},{10,6},{12,0},{14,2},{1,13},{3,15... | collective-permute-start | bytes 786440 | tf_op jit(solution)/shard_map/ppermute | solution.py:21
  18.9 50.4 %all-to-all-start = ((bf16[64,16,128]{2,0,1:T(8,128)(2,1)}), bf16[64,16,128]{2,0,1:T(8,128)(2,1)S(1)}, u32[]{:S(2)}, u32[]{:S(2)}) async-start(bf16[64,16,128]{2,0,1:T(8,128)(2,1)} %copy.34), calls=%async_computation | async-start | bytes 524288 | tf_op jit(solution)/shard_map/all_to_all | solution.py:171
  24.3 24.9 %collective-permute-start.3 = (bf16[128,1024]{1,0:T(8,128)(2,1)}, bf16[128,1024]{1,0:T(8,128)(2,1)S(1)}, u32[]{:S(2)}, u32[]{:S(2)}) collective-permute-start(bf16[128,1024]{1,0:T(8,128)(2,1)} %get-tuple-element.24), channel_id=1, source_target_pairs={{0,2},{2,0},{4,6},{6,4},{8,10},{10,8},{12,14},{14,12},{1,3},{3,1},... | collective-permute-start | bytes 786440 | tf_op jit(solution)/shard_map/ppermute | solution.py:21
  37.6 26.9 %collective-permute-start.4 = (bf16[128,1024]{1,0:T(8,128)(2,1)}, bf16[128,1024]{1,0:T(8,128)(2,1)S(1)}, u32[]{:S(2)}, u32[]{:S(2)}) collective-permute-start(bf16[128,1024]{1,0:T(8,128)(2,1)} %get-tuple-element.23), channel_id=1, source_target_pairs={{0,10},{2,8},{4,14},{6,12},{8,2},{10,0},{12,6},{14,4},{1,11},{3,9}... | collective-permute-start | bytes 786440 | tf_op jit(solution)/shard_map/ppermute | solution.py:21
  40.0 25.2 %collective-permute-start.5 = (bf16[128,1024]{1,0:T(8,128)(2,1)S(1)}, bf16[128,1024]{1,0:T(8,128)(2,1)S(1)}, u32[]{:S(2)}, u32[]{:S(2)}) collective-permute-start(bf16[128,1024]{1,0:T(8,128)(2,1)S(1)} %copy-done.13), channel_id=1, source_target_pairs={{0,6},{2,4},{4,2},{6,0},{8,14},{10,12},{12,10},{14,8},{1,7},{3,5},... | collective-permute-start | bytes 786440 | tf_op jit(solution)/shard_map/ppermute | solution.py:21
  45.1 20.8 %collective-permute-start.6 = (bf16[128,1024]{1,0:T(8,128)(2,1)S(1)}, bf16[128,1024]{1,0:T(8,128)(2,1)S(1)}, u32[]{:S(2)}, u32[]{:S(2)}) collective-permute-start(bf16[128,1024]{1,0:T(8,128)(2,1)S(1)} %copy-done.12), channel_id=1, source_target_pairs={{0,14},{2,12},{4,10},{6,8},{8,6},{10,4},{12,2},{14,0},{1,15},{3,13... | collective-permute-start | bytes 786440 | tf_op jit(solution)/shard_map/ppermute | solution.py:21
  49.1 86.6 %collective-permute-start.11 = (bf16[512,2048]{1,0:T(8,128)(2,1)}, bf16[512,2048]{1,0:T(8,128)(2,1)}, u32[]{:S(2)}, u32[]{:S(2)}) collective-permute-start(bf16[512,2048]{1,0:T(8,128)(2,1)} %param.13), channel_id=1, source_target_pairs={{0,1},{1,0},{2,3},{3,2},{4,5},{5,4},{6,7},{7,6},{8,9},{9,8},{10,11... | collective-permute-start | bytes 6291464 | tf_op jit(solution)/shard_map/ppermute | solution.py:25
  64.5 47.9 %collective-permute-start.7 = (bf16[512,1024]{1,0:T(8,128)(2,1)}, bf16[512,1024]{1,0:T(8,128)(2,1)}, u32[]{:S(2)}, u32[]{:S(2)}) collective-permute-start(bf16[512,1024]{1,0:T(8,128)(2,1)} %param.12), channel_id=1, source_target_pairs={{0,1},{1,0},{2,3},{3,2},{4,5},{5,4},{6,7},{7,6},{8,9},{9,8},{10,11... | collective-permute-start | bytes 3145736 | tf_op jit(solution)/shard_map/ppermute | solution.py:25
  65.2 41.5 %collective-permute-start.13 = (bf16[256,1024]{1,0:T(8,128)(2,1)}, bf16[256,1024]{1,0:T(8,128)(2,1)}, u32[]{:S(2)}, u32[]{:S(2)}) collective-permute-start(bf16[256,1024]{1,0:T(8,128)(2,1)} %pad_maximum_fusion.3), channel_id=1, source_target_pairs={{0,4},{2,6},{4,0},{6,2},{8,12},{10,14},{12,8},{14,10},{1,5},{3,7},... | collective-permute-start | bytes 1572872 | tf_op jit(solution)/shard_map/ppermute | solution.py:21
  65.9 44.8 %collective-permute-start.15 = (bf16[128,1024]{1,0:T(8,128)(2,1)}, bf16[128,1024]{1,0:T(8,128)(2,1)}, u32[]{:S(2)}, u32[]{:S(2)}) collective-permute-start(bf16[128,1024]{1,0:T(8,128)(2,1)} %collective-permute-done.12), channel_id=1, source_target_pairs={{0,2},{2,0},{4,6},{6,4},{8,10},{10,8},{12,14},{14,12},{1,3},{3,1},... | collective-permute-start | bytes 786440 | tf_op jit(solution)/shard_map/ppermute | solution.py:21
  106.7 18.7 %collective-permute-start.24 = (bf16[1024,512]{1,0:T(8,128)(2,1)}, bf16[1024,512]{1,0:T(8,128)(2,1)S(1)}, u32[]{:S(2)}, u32[]{:S(2)}) collective-permute-start(bf16[1024,512]{1,0:T(8,128)(2,1)} %get-tuple-element.11), channel_id=1, source_target_pairs={{0,1},{1,0},{2,3},{3,2},{4,5},{5,4},{6,7},{7,6},{8,9},{9,8},{10,11... | collective-permute-start | bytes 3145736 | tf_op jit(solution)/shard_map/ppermute | solution.py:25
  121.0 102.0 %collective-permute-start.8 = (bf16[4,128,1024]{2,1,0:T(8,128)(2,1)}, bf16[4,128,1024]{2,1,0:T(8,128)(2,1)}, u32[]{:S(2)}, u32[]{:S(2)}) collective-permute-start(bf16[4,128,1024]{2,1,0:T(8,128)(2,1)} %bitcast.4), channel_id=1, source_target_pairs={{0,2},{2,0},{4,6},{6,4},{8,10},{10,8},{12,14},{14,12},{1,3},{3,1},... | collective-permute-start | bytes 3145736 | tf_op jit(solution)/shard_map/ppermute | solution.py:21
  218.4 14.9 %collective-permute-start.17 = (bf16[128,1024]{1,0:T(8,128)(2,1)S(1)}, bf16[128,1024]{1,0:T(8,128)(2,1)S(1)}, u32[]{:S(2)}, u32[]{:S(2)}) collective-permute-start(bf16[128,1024]{1,0:T(8,128)(2,1)S(1)} %get-tuple-element.18), channel_id=1, source_target_pairs={{0,8},{2,10},{4,12},{6,14},{8,0},{10,2},{12,4},{14,6},{1,9},{3,11}... | collective-permute-start | bytes 786440 | tf_op jit(solution)/shard_map/ppermute | solution.py:21
  218.5 20.4 %collective-permute-start.18 = (bf16[128,1024]{1,0:T(8,128)(2,1)S(1)}, bf16[128,1024]{1,0:T(8,128)(2,1)S(1)}, u32[]{:S(2)}, u32[]{:S(2)}) collective-permute-start(bf16[128,1024]{1,0:T(8,128)(2,1)S(1)} %get-tuple-element.17), channel_id=1, source_target_pairs={{0,4},{2,6},{4,0},{6,2},{8,12},{10,14},{12,8},{14,10},{1,5},{3,7},... | collective-permute-start | bytes 786440 | tf_op jit(solution)/shard_map/ppermute | solution.py:21
  219.6 22.5 %collective-permute-start.19 = (bf16[128,1024]{1,0:T(8,128)(2,1)S(1)}, bf16[128,1024]{1,0:T(8,128)(2,1)S(1)}, u32[]{:S(2)}, u32[]{:S(2)}) collective-permute-start(bf16[128,1024]{1,0:T(8,128)(2,1)S(1)} %get-tuple-element.16), channel_id=1, source_target_pairs={{0,12},{2,14},{4,8},{6,10},{8,4},{10,6},{12,0},{14,2},{1,13},{3,15... | collective-permute-start | bytes 786440 | tf_op jit(solution)/shard_map/ppermute | solution.py:21
  223.1 26.3 %collective-permute-start.20 = (bf16[128,1024]{1,0:T(8,128)(2,1)S(1)}, bf16[128,1024]{1,0:T(8,128)(2,1)S(1)}, u32[]{:S(2)}, u32[]{:S(2)}) collective-permute-start(bf16[128,1024]{1,0:T(8,128)(2,1)S(1)} %get-tuple-element.15), channel_id=1, source_target_pairs={{0,2},{2,0},{4,6},{6,4},{8,10},{10,8},{12,14},{14,12},{1,3},{3,1},... | collective-permute-start | bytes 786440 | tf_op jit(solution)/shard_map/ppermute | solution.py:21
  225.4 36.7 %collective-permute-start.21 = (bf16[128,1024]{1,0:T(8,128)(2,1)S(1)}, bf16[128,1024]{1,0:T(8,128)(2,1)S(1)}, u32[]{:S(2)}, u32[]{:S(2)}) collective-permute-start(bf16[128,1024]{1,0:T(8,128)(2,1)S(1)} %get-tuple-element.14), channel_id=1, source_target_pairs={{0,10},{2,8},{4,14},{6,12},{8,2},{10,0},{12,6},{14,4},{1,11},{3,9}... | collective-permute-start | bytes 786440 | tf_op jit(solution)/shard_map/ppermute | solution.py:21
  233.3 38.7 %collective-permute-start.22 = (bf16[128,1024]{1,0:T(8,128)(2,1)S(1)}, bf16[128,1024]{1,0:T(8,128)(2,1)S(1)}, u32[]{:S(2)}, u32[]{:S(2)}) collective-permute-start(bf16[128,1024]{1,0:T(8,128)(2,1)S(1)} %get-tuple-element.13), channel_id=1, source_target_pairs={{0,6},{2,4},{4,2},{6,0},{8,14},{10,12},{12,10},{14,8},{1,7},{3,5},... | collective-permute-start | bytes 786440 | tf_op jit(solution)/shard_map/ppermute | solution.py:21
  238.9 33.2 %collective-permute-start.23 = (bf16[128,1024]{1,0:T(8,128)(2,1)S(1)}, bf16[128,1024]{1,0:T(8,128)(2,1)S(1)}, u32[]{:S(2)}, u32[]{:S(2)}) collective-permute-start(bf16[128,1024]{1,0:T(8,128)(2,1)S(1)} %get-tuple-element.12), channel_id=1, source_target_pairs={{0,14},{2,12},{4,10},{6,8},{8,6},{10,4},{12,2},{14,0},{1,15},{3,13... | collective-permute-start | bytes 786440 | tf_op jit(solution)/shard_map/ppermute | solution.py:21
  242.1 29.2 %collective-permute-start.9 = (bf16[2,128,1024]{2,1,0:T(8,128)(2,1)S(1)}, bf16[2,128,1024]{2,1,0:T(8,128)(2,1)S(1)}, u32[]{:S(2)}, u32[]{:S(2)}) collective-permute-start(bf16[2,128,1024]{2,1,0:T(8,128)(2,1)S(1)} %slice.118), channel_id=1, source_target_pairs={{0,4},{2,6},{4,0},{6,2},{8,12},{10,14},{12,8},{14,10},{1,5},{3,7},... | collective-permute-start | bytes 1572872 | tf_op jit(solution)/shard_map/ppermute | solution.py:21
  (20 other events, 208.7 us)

commit v2 on v1

v2 whole, which is shorter than its diff:
```python
import functools

import jax
import jax.numpy as jnp
from jax import lax
from jax.experimental import pallas as pl
from jax.experimental.pallas import tpu as pltpu
from jax.sharding import Mesh
from jax.sharding import PartitionSpec as P

RANK = 64
BLK = 64

adapter_scale = 0.5
norm_eps = 1e-05


def over_chips(value, mask):
    chips = lax.axis_size("chip")
    return lax.ppermute(value, "chip", [(i, i ^ mask) for i in range(chips)])


def over_cores(value):
    return lax.ppermute(value, "core", [(0, 1), (1, 0)])


def near_masks(chips):
    masks, step = [0], chips // 4
    while step:
        masks = masks + [m ^ step for m in masks]
        step //= 2
    return masks


def slot_masks(chips):
    near = near_masks(chips)
    return near + [m ^ (chips // 2) for m in near]


def gather_over_chips(mine, chips):
    held, masks = mine, [0]
    pieces = [(mine, [0]), (over_chips(mine, 1), [1])]
    step = chips // 2
    while step > 1:
        arrived, arrived_masks = over_chips(held, step), [m ^ step for m in masks]
        pieces.append((arrived, arrived_masks))
        pieces.append((over_chips(arrived, 1), [m ^ 1 for m in arrived_masks]))
        held, masks = jnp.concatenate([held, arrived]), masks + arrived_masks
        step //= 2
    return pieces


def gather_small(mine, chips):
    near, step = mine, chips // 4
    far = over_chips(mine, chips // 2)
    held = jnp.stack([near, far])
    while step:
        held = jnp.concatenate([held, over_chips(held, step)], axis=1)
        step //= 2
    return held.reshape((-1,) + mine.shape[1:])


def packed(values, low):
    high = lax.reduce_precision(low, 8, 7)
    return jnp.concatenate([values, high, low - high], axis=-1).astype(jnp.bfloat16)


def unpacked(sent, value_width):
    sent = sent.astype(jnp.float32)
    low = sent[..., value_width : value_width + RANK] + sent[..., value_width + RANK :]
    return sent[..., :value_width], low


def sum_over_chips(sends, values, low, chips):
    value_width = values[0].shape[-1]
    values, low = list(values), list(low)
    for side in (1, 0):
        step, sent = 1, sends[side]
        while True:
            more_values, more_low = unpacked(over_chips(sent, step), value_width)
            values[side] = values[side] + more_values
            low[side] = low[side] + more_low
            half = values[side].shape[0] // 2
            if not half:
                break
            sent = packed(values[side][half:], low[side][half:])
            values[side], low[side] = values[side][:half], low[side][:half]
            step *= 2
    more_values, more_low = unpacked(over_chips(packed(values[1], low[1]), chips // 2), value_width)
    return (values[0] + more_values)[0], (low[0] + more_low)[0]


def adapter_columns(adapter):
    return pl.ds(pl.multiple_of((adapter // 2) * 2 * RANK, 2 * RANK), 2 * RANK)


def back_kernel(masks, pieces, blocks, scalar_ref, tenant_ref, weight_ref, down_ref, scaled_ref, *refs):
    upstream_refs, out_ref = refs[:-1], refs[-1]
    lane = lax.broadcasted_iota(jnp.int32, (BLK, 2 * RANK), 1)
    rows = blocks * BLK
    contract = (((1,), (1,)), ((), ()))
    for upstream_ref, piece_masks in zip(upstream_refs, pieces):
        product = lax.dot_general(
            upstream_ref[...], weight_ref[...], contract, preferred_element_type=jnp.float32
        )
        for at, mask in enumerate(piece_masks):
            slot = masks.index(mask)
            for b in range(blocks):
                adapter = tenant_ref[slot * blocks + b]
                update = scaled_ref[slot * rows + b * BLK : slot * rows + (b + 1) * BLK, :]
                update = jnp.where(lane // RANK == adapter % 2, update, jnp.zeros_like(update))
                term = lax.dot_general(
                    update, down_ref[:, adapter_columns(adapter)], contract, preferred_element_type=jnp.float32
                )
                first = at * rows + b * BLK
                out_ref[scalar_ref[0] ^ mask, b * BLK : (b + 1) * BLK, :] = (
                    product[first : first + BLK] + term
                ).astype(out_ref.dtype)


def back_products(chip, masks, tenants, weight, down, scaled, pieces, token_rows):
    vmem, smem = pl.BlockSpec(memory_space=pltpu.VMEM), pl.BlockSpec(memory_space=pltpu.SMEM)
    width = weight.shape[0]
    slots = len(masks)
    return pl.pallas_call(
        functools.partial(back_kernel, masks, [m for _, m in pieces], token_rows // BLK),
        out_shape=jax.ShapeDtypeStruct((slots, token_rows, width), jnp.bfloat16),
        in_specs=[smem, smem] + [vmem] * (3 + len(pieces)),
        out_specs=vmem,
        compiler_params=pltpu.CompilerParams(vmem_limit_bytes=48 * 1024 * 1024),
        cost_estimate=pl.CostEstimate(
            flops=2 * slots * token_rows * width * weight.shape[1],
            bytes_accessed=2 * (weight.size + down.size + 2 * slots * token_rows * width),
            transcendentals=0,
        ),
    )(chip.reshape(1), tenants, weight, down, scaled, *[rows for rows, _ in pieces])


def value_kernel(slots, blocks, core_ref, tenant_ref, weight_ref, down_ref, *refs):
    normed_refs = refs[:slots]
    sides = (refs[slots : slots + 3], refs[slots + 3 : slots + 6])
    mine_ref, other_ref = refs[slots + 6 :]
    rows, width = normed_refs[0].shape
    half, kept = width // 2, slots // 4
    value_width = weight_ref.shape[1]
    for slot in range(slots):
        normed = normed_refs[slot][...]
        sent_ref, values_ref, low_ref = sides[slot // (slots // 2)]
        at = slot % (slots // 2)
        values = jnp.dot(normed, weight_ref[...], preferred_element_type=jnp.float32)
        low = []
        for b in range(blocks):
            adapter = tenant_ref[slot * blocks + b]
            both = jnp.dot(
                normed[b * BLK : (b + 1) * BLK],
                down_ref[:, adapter_columns(adapter)],
                preferred_element_type=jnp.float32,
            )
            low.append(jnp.where(adapter % 2 == 0, both[:, :RANK], both[:, RANK:]))
        low = jnp.concatenate(low, axis=0)
        if at < kept:
            values_ref[at] = values
            low_ref[at] = low
        else:
            high = low.astype(jnp.bfloat16)
            rest = (low - high.astype(jnp.float32)).astype(jnp.bfloat16)
            sent_ref[at - kept, :, :value_width] = values.astype(jnp.bfloat16)
            sent_ref[at - kept, :, value_width:] = jnp.concatenate([high, rest], axis=1)
        first, second = normed[:, :half], normed[:, half:]
        mine_ref[slot * rows : (slot + 1) * rows, :] = jnp.where(core_ref[0] == 0, first, second)
        other_ref[slot * rows : (slot + 1) * rows, :] = jnp.where(core_ref[0] == 0, second, first)


def value_products(core, tenants, weight, down, normed):
    vmem, smem = pl.BlockSpec(memory_space=pltpu.VMEM), pl.BlockSpec(memory_space=pltpu.SMEM)
    slots = len(normed)
    rows, width = normed[0].shape
    value_width = weight.shape[1]
    side = [
        jax.ShapeDtypeStruct((slots // 4, rows, value_width + 2 * RANK), jnp.bfloat16),
        jax.ShapeDtypeStruct((slots // 4, rows, value_width), jnp.float32),
        jax.ShapeDtypeStruct((slots // 4, rows, RANK), jnp.float32),
    ]
    half = jax.ShapeDtypeStruct((slots * rows, width // 2), jnp.bfloat16)
    return pl.pallas_call(
        functools.partial(value_kernel, slots, rows // BLK),
        out_shape=side + side + [half, half],
        in_specs=[smem, smem] + [vmem] * (2 + slots),
        out_specs=[vmem] * 8,
        compiler_params=pltpu.CompilerParams(vmem_limit_bytes=56 * 1024 * 1024),
        cost_estimate=pl.CostEstimate(
            flops=2 * slots * rows * width * value_width,
            bytes_accessed=2 * (weight.size + down.size + 5 * slots * rows * width),
            transcendentals=0,
        ),
    )(core.reshape(1), tenants, weight, down, *normed)


def factor_grad_kernel(blocks, scale, tenant_ref, *refs):
    out_ref = refs[-1]
    out_ref[...] = jnp.zeros_like(out_ref)
    lane = lax.broadcasted_iota(jnp.int32, (BLK, 2 * RANK), 1)

    for which in range(2):
        rows_ref, update_ref = refs[2 * which], refs[2 * which + 1]

        def step(b, carry, rows_ref=rows_ref, update_ref=update_ref, which=which):
            adapter = tenant_ref[which * blocks + b]
            tokens = pl.ds(pl.multiple_of(b * BLK, BLK), BLK)
            update = update_ref[tokens, :]
            update = jnp.where(lane // RANK == adapter % 2, update, jnp.zeros_like(update))
            term = lax.dot_general(
                rows_ref[tokens, :], update, (((0,), (0,)), ((), ())), preferred_element_type=jnp.float32
            )
            out_ref[:, adapter_columns(adapter)] += scale * term
            return carry

        lax.fori_loop(0, blocks, step, 0)


def factor_grad(rows, update, other_rows, other_update, tenants, width, scale):
    vmem = pl.BlockSpec(memory_space=pltpu.VMEM)
    return pl.pallas_call(
        functools.partial(factor_grad_kernel, tenants.shape[0] // 2, scale),
        out_shape=jax.ShapeDtypeStruct((rows.shape[1], width), jnp.float32),
        in_specs=[pl.BlockSpec(memory_space=pltpu.SMEM)] + [vmem] * 4,
        out_specs=vmem,
        compiler_params=pltpu.CompilerParams(vmem_limit_bytes=40 * 1024 * 1024),
        cost_estimate=pl.CostEstimate(
            flops=4 * rows.size * 2 * RANK,
            bytes_accessed=4 * rows.size + 4 * rows.shape[1] * width,
            transcendentals=0,
        ),
    )(tenants, rows, update, other_rows, other_update)


def token_grad_kernel(slots, width, features, tokens_ref, gain_ref, inverse_ref, back_ref, out_ref):
    inverse = inverse_ref[...]
    total = jnp.zeros_like(inverse)
    for s in range(slots):
        columns = slice(s * width, (s + 1) * width)
        gained = gain_ref[:, columns] * back_ref[s].astype(jnp.float32)
        wide = tokens_ref[:, columns].astype(jnp.float32)
        total += jnp.sum(gained * wide, axis=1, keepdims=True)
    cubed = inverse * inverse * inverse
    inner = total / features
    for s in range(slots):
        columns = slice(s * width, (s + 1) * width)
        gained = gain_ref[:, columns] * back_ref[s].astype(jnp.float32)
        wide = tokens_ref[:, columns].astype(jnp.float32)
        out_ref[:, columns] = (inverse * gained - wide * cubed * inner).astype(out_ref.dtype)


def token_grad(tokens, gain, inverse, back):
    slots, rows, width = back.shape
    vmem = pl.BlockSpec(memory_space=pltpu.VMEM)
    return pl.pallas_call(
        functools.partial(token_grad_kernel, slots, width, tokens.shape[1]),
        out_shape=jax.ShapeDtypeStruct(tokens.shape, tokens.dtype),
        in_specs=[vmem] * 4,
        out_specs=vmem,
        compiler_params=pltpu.CompilerParams(vmem_limit_bytes=32 * 1024 * 1024),
        cost_estimate=pl.CostEstimate(
            flops=10 * tokens.size, bytes_accessed=6 * tokens.size, transcendentals=0
        ),
    )(tokens, gain, inverse, back)


def on_device(tokens, upstream, norm_gain, value_weight, down_factor, up_factor, tenant):
    chips = lax.axis_size("chip")
    chip, core = lax.axis_index("chip"), lax.axis_index("core")
    masks = slot_masks(chips)
    chip_of_slot = chip ^ jnp.asarray(masks, jnp.int32)

    token_rows, features = tokens.shape
    blocks = token_rows // BLK
    value_width = upstream.shape[1]
    adapters = down_factor.shape[1] // RANK
    width = features // chips
    value_rows = up_factor.shape[0]

    tenants = tenant.reshape(chips, 2, blocks)[chip_of_slot]
    tenants_mine, tenants_other = tenants[:, core].reshape(-1), tenants[:, 1 - core].reshape(-1)
    tenants_both = jnp.concatenate([tenants_mine, tenants_other])

    upstream_pieces = gather_over_chips(upstream, chips)

    def both_cores(mine):
        other = over_cores(mine)
        pair = jnp.stack([jnp.where(core == 0, mine, other), jnp.where(core == 0, other, mine)])
        return pair.reshape((2 * mine.shape[0],) + mine.shape[1:])

    weight = both_cores(value_weight)
    down = both_cores(down_factor)

    up_table = jnp.take(
        up_factor.reshape(value_rows, adapters, RANK), tenant, axis=1, mode="clip"
    ).reshape(value_rows, -1)
    up_mine = lax.all_to_all(up_table, ("chip", "core"), split_axis=1, concat_axis=0, tiled=True)
    up_blocks = up_mine.reshape(value_width, blocks, RANK)

    wide_tokens = tokens.astype(jnp.float32)
    inverse = lax.rsqrt(jnp.mean(wide_tokens * wide_tokens, axis=1, keepdims=True) + norm_eps)
    normed = (wide_tokens * inverse * norm_gain).astype(jnp.bfloat16)

    def columns_for(mask):
        return lax.dynamic_slice_in_dim(normed, (chip ^ mask) * width, width, 1)

    arrived = {m: over_chips(columns_for(m), m) if m else columns_for(m) for m in reversed(masks)}
    arrived = [arrived[m] for m in masks]

    upstream_blocks = upstream.reshape(blocks, BLK, value_width)
    mixed_output = jnp.einsum("bkv,vbr->bkr", upstream_blocks, up_blocks, preferred_element_type=jnp.float32)
    scaled_mine = (adapter_scale * mixed_output).astype(jnp.bfloat16).reshape(token_rows, RANK)
    scaled = gather_small(jnp.concatenate([scaled_mine, scaled_mine], axis=1), chips)
    scaled_other = over_cores(scaled)

    back = back_products(chip, masks, tenants_mine, weight, down, scaled, upstream_pieces, token_rows)
    back_mine = lax.all_to_all(back, "chip", split_axis=0, concat_axis=0, tiled=True)
    arrived, back = lax.optimization_barrier((arrived, back))

    products = value_products(core, tenants_mine, weight, down, arrived)
    (near_sent, near_values, near_low, far_sent, far_values, far_low, normed_mine, normed_sent) = products
    values, low = sum_over_chips(
        (near_sent, far_sent), (near_values, far_values), (near_low, far_low), chips
    )
    low_mine = low.astype(jnp.bfloat16)
    adapter_branch = jnp.einsum(
        "bkr,vbr->bkv", low_mine.reshape(blocks, BLK, RANK), up_blocks, preferred_element_type=jnp.float32
    ).reshape(token_rows, value_width)
    adapted_values = (values + adapter_scale * adapter_branch).astype(jnp.bfloat16)

    grad_down = factor_grad(
        normed_mine, scaled, over_cores(normed_sent), scaled_other, tenants_both, adapters * RANK, 1.0
    )
    by_mask = {}
    for rows, piece_masks in upstream_pieces:
        for at, mask in enumerate(piece_masks):
            by_mask[mask] = rows[at * token_rows : (at + 1) * token_rows]

    def upstream_columns(whose):
        first = chip * 2 * value_rows + whose * value_rows
        return jnp.concatenate([lax.dynamic_slice_in_dim(by_mask[m], first, value_rows, 1) for m in masks])

    low_core = gather_small(jnp.concatenate([low_mine, low_mine], axis=1), chips)
    grad_up = factor_grad(
        upstream_columns(core),
        low_core,
        over_cores(upstream_columns(1 - core)),
        over_cores(low_core),
        tenants_both,
        adapters * RANK,
        adapter_scale,
    )

    grad_tokens = token_grad(tokens, norm_gain.reshape(1, -1), inverse, back_mine)
    return (adapted_values, grad_tokens, grad_down, grad_up)


def solution(mesh):
    groups, shards = mesh.shape["groups"], mesh.shape["fsdp"]
    chip_mesh = Mesh(mesh.devices.reshape(groups, shards // 2, 2), ("groups", "chip", "core"))
    own = ("chip", "core")
    everywhere = P(("groups",) + own, None)
    in_specs = (everywhere, everywhere, P(), P(own, None), P(own, None), P(own, None), P("groups"))
    out_specs = (everywhere,) * 4
    return jax.shard_map(
        on_device, mesh=chip_mesh, in_specs=in_specs, out_specs=out_specs, check_vma=False
    )
```

time: 288 us -> 225 us (0.78)
  blocking collectives: 65.8 us -> 0 us
  local copies, waits for them, and re-layouts: 68.8 us -> 27.8 us
  waiting for transfers between devices: 55 us -> 92.1 us
  Pallas kernels: 21.9 us -> 40.5 us
  matrix products: 12.2 us -> 0.42 us
  starting transfers between devices: 45.2 us -> 38.8 us
  other arithmetic: 16.7 us -> 22.5 us
    psum x1 -> x0, blocking collectives: 41.5 us -> none  [on_device(): low = lax.psum(low[slot_of_chip], 'chip').astype(jnp.bfloat16)]
    ppermute x22 -> x23, waiting for transfers between devices: 54.9 us -> 84.4 us  [over_chips(): return lax.ppermute(value, 'chip', [(i, i ^ mask) for i in range(chips)])]
    all_gather x1 -> x0, blocking collectives: 24.2 us -> none  [on_device(): scaled_all = lax.all_gather(scaled_mine, ('chip', 'core'), axis=0)]
    another operation x4 -> x1, local copies, waits for them, and re-layouts: 19.7 us -> 0.08 us  [on_device(): tenants[:, core].reshape(-1)]
    pallas_call x3 -> x5, Pallas kernels: 21.9 us -> 40.5 us  [the longest x2 17.9 us: factor_grad(): pl.pallas_call(functools.partial(factor_grad_kernel, tenants.shape[0] //...]
    ppermute x22 -> x23, starting transfers between devices: 41.2 us -> 29.2 us  [over_chips(): return lax.ppermute(value, 'chip', [(i, i ^ mask) for i in range(chips)])]
    gather x5 -> x0, local copies, waits for them, and re-layouts: 11 us -> none  [the longest x1 4.24 us: on_device(): jnp.take(down.reshape(width, adapters, RANK), tenants_mine, axis=1, mode=...]
    dot_general x5 -> x1, matrix products: 11.1 us -> 0.21 us  [on_device(): jnp.einsum('bkr,vbr->bkv', low_mine.reshape(blocks, BLK, RANK), up_blocks...]
  transfers between devices with their start and end apart: 28 -> 31, of which waited for: 7 -> 13; matrix products, arithmetic and copies ran while one was open for 32% -> 21% of each run, Pallas kernels for 8% -> 16%
where the time goes in v2:
time: 225 us; the launch traced here: 223 us
  waiting for transfers between devices  92.1 us (41%)
  Pallas kernels  40.5 us (18%)
  starting transfers between devices  38.8 us (17%)
  local copies, waits for them, and re-layouts  27.8 us (12%)
  other arithmetic  22.5 us (10%)
    ppermute x23, waiting for transfers between devices, over_chips(): return lax.ppermute(value, 'chip', [(i, i ^ mask) for i in range(chips)])  84.4 us
    ppermute x23, starting transfers between devices, over_chips(): return lax.ppermute(value, 'chip', [(i, i ^ mask) for i in range(chips)])  29.2 us
    pallas_call x2, Pallas kernels, factor_grad(): pl.pallas_call(functools.partial(factor_grad_kernel, tenants.shape[0] //...  17.9 us
    unnamed x72, local copies, waits for them, and re-layouts  11.8 us
    pallas_call x1, Pallas kernels, value_products(): pl.pallas_call(functools.partial(value_kernel, slots, rows // BLK), out_s...  9.4 us
    pallas_call x1, Pallas kernels, back_products(): pl.pallas_call(functools.partial(back_kernel, masks, [m for _, m in piece...  8.32 us
    another operation x4, other arithmetic, both_cores(): jnp.stack([jnp.where(core == 0, mine, other), jnp.where(core == 0, other,...  7.69 us
    all_to_all x1, waiting for transfers between devices, on_device(): lax.all_to_all(up_table, ('chip', 'core'), split_axis=1, concat_axis=0, t...  7.01 us
  transfers between devices with their start and end apart: 31, of which 13 were waited for; matrix products, arithmetic and copies ran while one was open for 21% of the time, Pallas kernels for 16%

profile of v2, /device:TPU:0, one launch (start us, length us, event | category | flops | bytes accessed | tf_op | source)
XLA Modules:
  0.0 223.4 jit_solution(7919679560887824958)
XLA Ops:
  0.6 4.1 %collective-permute-start.13 = (bf16[128,1024]{1,0:T(8,128)(2,1)}, bf16[128,1024]{1,0:T(8,128)(2,1)S(1)}, u32[]{:S(2)}, u32[]{:S(2)}) collective-permute-start(bf16[128,1024]{1,0:T(8,128)(2,1)} %refs_0_.1), channel_id=1, source_target_pairs={{0,8},{2,10},{4,12},{6,14},{8,0},{10,2},{12,4},{14,6},{1,9},{3,11}... | collective-permute-start | bytes 786440 | tf_op jit(solution)/shard_map/ppermute | solution.py:20
  11.5 3.5 %all-to-all-start = ((bf16[64,16,128]{2,0,1:T(8,128)(2,1)}), bf16[64,16,128]{2,0,1:T(8,128)(2,1)S(1)}, u32[]{:S(2)}, u32[]{:S(2)}) async-start(bf16[64,16,128]{2,0,1:T(8,128)(2,1)} %copy.26), calls=%async_computation | async-start | bytes 524288 | tf_op jit(solution)/shard_map/all_to_all | solution.py:299
  18.0 7.0 %all-to-all-done = bf16[64,16,128]{2,0,1:T(8,128)(2,1)S(1)} async-done(((bf16[64,16,128]{2,0,1:T(8,128)(2,1)}), bf16[64,16,128]{2,0,1:T(8,128)(2,1)S(1)}, u32[]{:S(2)}, u32[]{:S(2)}) %all-to-all-start) | async-done | bytes 262176 | tf_op jit(solution)/shard_map/all_to_all | solution.py:299
  27.4 2.8 %constant_dynamic-slice_fusion.1 = (bf16[128,1024]{1,0:T(8,128)(2,1)}, bf16[128,1024]{1,0:T(8,128)(2,1)}, bf16[128,1024]{1,0:T(8,128)(2,1)}, bf16[128,1024]{1,0:...) fusion(bf16[128,8192]{1,0:T(8,128)(2,1)} %fusion.2, ...), kind=kLoop, calls=%fused_computation.75 | loop fusion | bytes 4194336 | tf_op jit(solution)/shard_map/dynamic_slice | solution.py:307
  32.9 2.5 %collective-permute-done.10 = bf16[2,128,128]{1,2,0:T(8,128)(2,1)S(1)} collective-permute-done((bf16[2,128,128]{1,2,0:T(8,128)(2,1)S(1)}, bf16[2,128,128]{1,2,0:T(8,128)(2,1)S(1)}, u32[]{:S(2)}, u32[]{:S(2)}) %collective-permute-start.10) | collective-permute-done | bytes 65568 | tf_op jit(solution)/shard_map/ppermute | solution.py:20
  35.8 2.6 %collective-permute-start.8 = (bf16[128,1024]{1,0:T(8,128)(2,1)}, bf16[128,1024]{1,0:T(8,128)(2,1)}, u32[]{:S(2)}, u32[]{:S(2)}) collective-permute-start(bf16[128,1024]{1,0:T(8,128)(2,1)} %get-tuple-element.40), channel_id=1, source_target_pairs={{0,14},{2,12},{4,10},{6,8},{8,6},{10,4},{12,2},{14,0},{1,15},{3,13... | collective-permute-start | bytes 786440 | tf_op jit(solution)/shard_map/ppermute | solution.py:20
  39.2 5.2 %collective-permute-done.11 = bf16[2,256,128]{1,2,0:T(8,128)(2,1)} collective-permute-done((bf16[2,256,128]{1,2,0:T(8,128)(2,1)S(1)}, bf16[2,256,128]{1,2,0:T(8,128)(2,1)}, u32[]{:S(2)}, u32[]{:S(2)}) %collective-permute-start.11) | collective-permute-done | bytes 131104 | tf_op jit(solution)/shard_map/ppermute | solution.py:20
  50.5 11.2 %collective-permute-done.15.refs_4_ = bf16[256,1024]{1,0:T(8,128)(2,1)S(1)} collective-permute-done((bf16[256,1024]{1,0:T(8,128)(2,1)}, bf16[256,1024]{1,0:T(8,128)(2,1)S(1)}, u32[]{:S(2)}, u32[]{:S(2)}) %collective-permute-start.15) | collective-permute-done | bytes 524320 | tf_op jit(solution)/shard_map/ppermute | solution.py:20
  68.1 2.4 %collective-permute-start.4 = (bf16[128,1024]{1,0:T(8,128)(2,1)S(1)}, bf16[128,1024]{1,0:T(8,128)(2,1)S(1)}, u32[]{:S(2)}, u32[]{:S(2)}) collective-permute-start(bf16[128,1024]{1,0:T(8,128)(2,1)S(1)} %copy-done.19), channel_id=1, source_target_pairs={{0,6},{2,4},{4,2},{6,0},{8,14},{10,12},{12,10},{14,8},{1,7},{3,5},... | collective-permute-start | bytes 786440 | tf_op jit(solution)/shard_map/ppermute | solution.py:20
  72.4 13.8 %collective-permute-done.16.refs_5_ = bf16[256,1024]{1,0:T(8,128)(2,1)S(1)} collective-permute-done((bf16[256,1024]{1,0:T(8,128)(2,1)S(1)}, bf16[256,1024]{1,0:T(8,128)(2,1)S(1)}, u32[]{:S(2)}, u32[]{:S(2)}) %collective-permute-start.16) | collective-permute-done | bytes 524320 | tf_op jit(solution)/shard_map/ppermute | solution.py:20
  86.3 2.4 %pad_maximum_fusion = bf16[2,512,2048]{2,1,0:T(8,128)(2,1)} fusion(bf16[1,512,2048]{2,1,0:T(8,128)(2,1)S(1)} %get-tuple-element.39, bf16[1,512,2048]{2,1,0:T(8,128)(2,1)S(1)} %get-tuple-element.38), kind=kLoop, calls=%fused_computation.7 | loop fusion | flops 2097152 | bytes 8388608 | tf_op jit(solution)/shard_map/stack | solution.py:290
  88.7 8.3 %shard_map.111 = bf16[8,128,1024]{2,1,0:T(8,128)(2,1)S(1)} custom-call(s32[1]{0:T(128)} %bitcast.7.scalar_ref, s32[16]{0:T(128)S(1)} %reshape_squeeze.6.tenant_ref, bf16[1024,1024]{1,0:T(8,128)(2,1)} %bitcast.52, bf16[1024,2048]{1,0:T(8,128)(2,1)} %bitcast.50, bf16[1024,128]{1,0:T(8,128)(2,1)S(1)} %bitcast.44, bf16[128,1024]{1,0:T(8,128)(2,1)S(1)} %copy-done.2, ...), custom_call_target="tpu_custom_call" | custom-call | flops 2147483648 | bytes 10485760 | tf_op jit(solution)/shard_map/pallas_call | solution.py:125
  99.4 9.4 %shard_map.112 = (bf16[2,128,1152]{2,1,0:T(8,128)(2,1)}, f32[2,128,1024]{2,1,0:T(8,128)}, f32[2,128,64]{2,1,0:T(8,128)}, bf16[2,128,1152]{2,1,0:T(8,128)(2,1)}, ...) custom-call(s32[1]{0:T(128)} %bitcast.core_ref, ...), custom_call_target="tpu_custom_call" | custom-call | flops 2147483648 | bytes 16777216 | tf_op jit(solution)/shard_map/pallas_call | solution.py:185
  114.2 5.3 %all-to-all-start.1 = ((bf16[8,128,1024]{2,1,0:T(8,128)(2,1)}), bf16[8,128,1024]{2,1,0:T(8,128)(2,1)}, u32[]{:S(2)}, u32[]{:S(2)}) async-start(bf16[8,128,1024]{2,1,0:T(8,128)(2,1)} %copy-done.1), calls=%async_computation.1 | async-start | bytes 4194304 | tf_op jit(solution)/shard_map/all_to_all | solution.py:319
  121.5 13.6 %collective-permute-done.19 = bf16[2,128,1152]{2,1,0:T(8,128)(2,1)} collective-permute-done((bf16[2,128,1152]{2,1,0:T(8,128)(2,1)}, bf16[2,128,1152]{2,1,0:T(8,128)(2,1)}, u32[]{:S(2)}, u32[]{:S(2)}) %collective-permute-start.19) | collective-permute-done | bytes 589856 | tf_op jit(solution)/shard_map/ppermute | solution.py:20
  138.3 2.4 %collective-permute-start.20 = (bf16[1,128,1152]{2,1,0:T(8,128)(2,1)}, bf16[1,128,1152]{2,1,0:T(8,128)(2,1)}, u32[]{:S(2)}, u32[]{:S(2)}) collective-permute-start(bf16[1,128,1152]{2,1,0:T(8,128)(2,1)} %concatenate.73), channel_id=1, source_target_pairs={{0,4},{2,6},{4,0},{6,2},{8,12},{10,14},{12,8},{14,10},{1,5},{3,7},... | collective-permute-start | bytes 884744 | tf_op jit(solution)/shard_map/ppermute | solution.py:20
  140.7 19.2 %collective-permute-done.17 = bf16[2,128,1152]{2,1,0:T(8,128)(2,1)} collective-permute-done((bf16[2,128,1152]{2,1,0:T(8,128)(2,1)}, bf16[2,128,1152]{2,1,0:T(8,128)(2,1)}, u32[]{:S(2)}, u32[]{:S(2)}) %collective-permute-start.17) | collective-permute-done | bytes 589856 | tf_op jit(solution)/shard_map/ppermute | solution.py:20
  169.9 3.1 %collective-permute-start.21 = (bf16[1,128,1152]{2,1,0:T(8,128)(2,1)}, bf16[1,128,1152]{2,1,0:T(8,128)(2,1)S(1)}, u32[]{:S(2)}, u32[]{:S(2)}) collective-permute-start(bf16[1,128,1152]{2,1,0:T(8,128)(2,1)} %concatenate.74), channel_id=1, source_target_pairs={{0,8},{2,10},{4,12},{6,14},{8,0},{10,2},{12,4},{14,6},{1,9},{3,11}... | collective-permute-start | bytes 884744 | tf_op jit(solution)/shard_map/ppermute | solution.py:20
  177.9 8.2 %collective-permute-done.21 = bf16[1,128,1152]{2,1,0:T(8,128)(2,1)S(1)} collective-permute-done((bf16[1,128,1152]{2,1,0:T(8,128)(2,1)}, bf16[1,128,1152]{2,1,0:T(8,128)(2,1)S(1)}, u32[]{:S(2)}, u32[]{:S(2)}) %collective-permute-start.21) | collective-permute-done | bytes 294944 | tf_op jit(solution)/shard_map/ppermute | solution.py:20
  187.4 3.8 %collective-permute-done.24 = bf16[128,128]{1,0:T(8,128)(2,1)S(1)} collective-permute-done((bf16[128,128]{1,0:T(8,128)(2,1)S(1)}, bf16[128,128]{1,0:T(8,128)(2,1)S(1)}, u32[]{:S(2)}, u32[]{:S(2)}) %collective-permute-start.24) | collective-permute-done | bytes 32800 | tf_op jit(solution)/shard_map/ppermute | solution.py:20
  192.5 10.8 %shard_map.114 = f32[512,2048]{1,0:T(8,128)} custom-call(s32[32]{0:T(128)S(1)} %pad_add_fusion.tenant_ref, bf16[1024,512]{1,0:T(8,128)(2,1)S(1)} %copy-done.3, bf16[1024,128]{1,0:T(8,128)(2,1)S(1)} %bitcast.46, bf16[1024,512]{1,0:T(8,128)(2,1)} %collective-permute-done.22.refs_2_, bf16[1024,128]{1,0:T(8,128)(2,1)} %collective-permute-done.23.refs_3_), custom_call_target="tpu_custom_call" | custom-call | flops 268435456 | bytes 6291456 | tf_op jit(solution)/shard_map/pallas_call | solution.py:223
  205.9 3.9 %collective-permute-done.26 = bf16[2,256,128]{2,1,0:T(8,128)(2,1)S(1)} collective-permute-done((bf16[2,256,128]{2,1,0:T(8,128)(2,1)S(1)}, bf16[2,256,128]{2,1,0:T(8,128)(2,1)S(1)}, u32[]{:S(2)}, u32[]{:S(2)}) %collective-permute-start.26) | collective-permute-done | bytes 131104 | tf_op jit(solution)/shard_map/ppermute | solution.py:20
  211.4 7.1 %shard_map.115 = f32[64,2048]{1,0:T(8,128)} custom-call(s32[32]{0:T(128)S(1)} %pad_add_fusion.tenant_ref, bf16[1024,64]{1,0:T(8,128)(2,1)S(1)} %get-tuple-element.57.refs_0_, bf16[1024,128]{1,0:T(8,128)(2,1)S(1)} %bitcast.48, bf16[1024,64]{1,0:T(8,128)(2,1)S(1)} %collective-permute-done.27.refs_2_, bf16[1024,128]{1,0:T(8,128)(2,1)S(1)} %collective-permute-done.28.refs_3_), custom_call_target="tpu_custom_call" | custom-call | flops 33554432 | bytes 786432 | tf_op jit(solution)/shard_map/pallas_call | solution.py:223
  218.5 4.9 %shard_map.113 = bf16[128,8192]{1,0:T(8,128)(2,1)} custom-call(bf16[128,8192]{1,0:T(8,128)(2,1)S(1)} %copy-done, f32[1,8192]{1,0:T(1,128)S(1)} %bitcast.49, f32[128,1]{1,0:T(8,128)S(1)} %copy.30.inverse_ref, bf16[8,128,1024]{2,1,0:T(8,128)(2,1)} %all-to-all-done.1.back_ref), custom_call_target="tpu_custom_call" | custom-call | flops 10485760 | bytes 6291456 | tf_op jit(solution)/shard_map/pallas_call | solution.py:257
  (177 shorter events, 64.3 us)
Async XLA Ops:
  0.6 35.1 %collective-permute-start.13 = (bf16[128,1024]{1,0:T(8,128)(2,1)}, bf16[128,1024]{1,0:T(8,128)(2,1)S(1)}, u32[]{:S(2)}, u32[]{:S(2)}) collective-permute-start(bf16[128,1024]{1,0:T(8,128)(2,1)} %refs_0_.1), channel_id=1, source_target_pairs={{0,8},{2,10},{4,12},{6,14},{8,0},{10,2},{12,4},{14,6},{1,9},{3,11}... | collective-permute-start | bytes 786440 | tf_op jit(solution)/shard_map/ppermute | solution.py:20
  4.7 61.2 %collective-permute-start.12 = (bf16[128,1024]{1,0:T(8,128)(2,1)}, bf16[128,1024]{1,0:T(8,128)(2,1)}, u32[]{:S(2)}, u32[]{:S(2)}) collective-permute-start(bf16[128,1024]{1,0:T(8,128)(2,1)} %refs_0_.1), channel_id=1, source_target_pairs={{0,2},{2,0},{4,6},{6,4},{8,10},{10,8},{12,14},{14,12},{1,3},{3,1},... | collective-permute-start | bytes 786440 | tf_op jit(solution)/shard_map/ppermute | solution.py:20
  11.5 13.5 %all-to-all-start = ((bf16[64,16,128]{2,0,1:T(8,128)(2,1)}), bf16[64,16,128]{2,0,1:T(8,128)(2,1)S(1)}, u32[]{:S(2)}, u32[]{:S(2)}) async-start(bf16[64,16,128]{2,0,1:T(8,128)(2,1)} %copy.26), calls=%async_computation | async-start | bytes 524288 | tf_op jit(solution)/shard_map/all_to_all | solution.py:299
  15.0 32.2 %collective-permute-start = (bf16[512,1024]{1,0:T(8,128)(2,1)}, bf16[512,1024]{1,0:T(8,128)(2,1)}, u32[]{:S(2)}, u32[]{:S(2)}) collective-permute-start(bf16[512,1024]{1,0:T(8,128)(2,1)} %param.11), channel_id=1, source_target_pairs={{0,1},{1,0},{2,3},{3,2},{4,5},{5,4},{6,7},{7,6},{8,9},{9,8},{10,11... | collective-permute-start | bytes 3145736 | tf_op jit(solution)/shard_map/ppermute | solution.py:24
  15.3 47.1 %collective-permute-start.1 = (bf16[512,2048]{1,0:T(8,128)(2,1)}, bf16[512,2048]{1,0:T(8,128)(2,1)}, u32[]{:S(2)}, u32[]{:S(2)}) collective-permute-start(bf16[512,2048]{1,0:T(8,128)(2,1)} %param.12), channel_id=1, source_target_pairs={{0,1},{1,0},{2,3},{3,2},{4,5},{5,4},{6,7},{7,6},{8,9},{9,8},{10,11... | collective-permute-start | bytes 6291464 | tf_op jit(solution)/shard_map/ppermute | solution.py:24
  35.8 32.3 %collective-permute-start.8 = (bf16[128,1024]{1,0:T(8,128)(2,1)}, bf16[128,1024]{1,0:T(8,128)(2,1)}, u32[]{:S(2)}, u32[]{:S(2)}) collective-permute-start(bf16[128,1024]{1,0:T(8,128)(2,1)} %get-tuple-element.40), channel_id=1, source_target_pairs={{0,14},{2,12},{4,10},{6,8},{8,6},{10,4},{12,2},{14,0},{1,15},{3,13... | collective-permute-start | bytes 786440 | tf_op jit(solution)/shard_map/ppermute | solution.py:20
  44.4 17.3 %collective-permute-start.15 = (bf16[256,1024]{1,0:T(8,128)(2,1)}, bf16[256,1024]{1,0:T(8,128)(2,1)S(1)}, u32[]{:S(2)}, u32[]{:S(2)}) collective-permute-start(bf16[256,1024]{1,0:T(8,128)(2,1)} %pad_maximum_fusion.2), channel_id=1, source_target_pairs={{0,4},{2,6},{4,0},{6,2},{8,12},{10,14},{12,8},{14,10},{1,5},{3,7},... | collective-permute-start | bytes 1572872 | tf_op jit(solution)/shard_map/ppermute | solution.py:20
  47.2 20.9 %collective-permute-start.7 = (bf16[128,1024]{1,0:T(8,128)(2,1)}, bf16[128,1024]{1,0:T(8,128)(2,1)S(1)}, u32[]{:S(2)}, u32[]{:S(2)}) collective-permute-start(bf16[128,1024]{1,0:T(8,128)(2,1)} %get-tuple-element.41), channel_id=1, source_target_pairs={{0,10},{2,8},{4,14},{6,12},{8,2},{10,0},{12,6},{14,4},{1,11},{3,9}... | collective-permute-start | bytes 786440 | tf_op jit(solution)/shard_map/ppermute | solution.py:20
  62.4 23.8 %collective-permute-start.16 = (bf16[256,1024]{1,0:T(8,128)(2,1)S(1)}, bf16[256,1024]{1,0:T(8,128)(2,1)S(1)}, u32[]{:S(2)}, u32[]{:S(2)}) collective-permute-start(bf16[256,1024]{1,0:T(8,128)(2,1)S(1)} %collective-permute-done.15.refs_4_), channel_id=1, source_target_pairs={{0,2},{2,0},{4,6},{6,4},{8,10},{10,8},{12,14},{14,12},{1,3},{3,1},... | collective-permute-start | bytes 1572872 | tf_op jit(solution)/shard_map/ppermute | solution.py:20
  65.9 32.4 %collective-permute-start.6 = (bf16[128,1024]{1,0:T(8,128)(2,1)S(1)}, bf16[128,1024]{1,0:T(8,128)(2,1)S(1)}, u32[]{:S(2)}, u32[]{:S(2)}) collective-permute-start(bf16[128,1024]{1,0:T(8,128)(2,1)S(1)} %copy-done.21), channel_id=1, source_target_pairs={{0,12},{2,14},{4,8},{6,10},{8,4},{10,6},{12,0},{14,2},{1,13},{3,15... | collective-permute-start | bytes 786440 | tf_op jit(solution)/shard_map/ppermute | solution.py:20
  68.1 30.3 %collective-permute-start.5 = (bf16[128,1024]{1,0:T(8,128)(2,1)S(1)}, bf16[128,1024]{1,0:T(8,128)(2,1)S(1)}, u32[]{:S(2)}, u32[]{:S(2)}) collective-permute-start(bf16[128,1024]{1,0:T(8,128)(2,1)S(1)} %copy-done.20), channel_id=1, source_target_pairs={{0,8},{2,10},{4,12},{6,14},{8,0},{10,2},{12,4},{14,6},{1,9},{3,11}... | collective-permute-start | bytes 786440 | tf_op jit(solution)/shard_map/ppermute | solution.py:20
  68.1 30.2 %collective-permute-start.4 = (bf16[128,1024]{1,0:T(8,128)(2,1)S(1)}, bf16[128,1024]{1,0:T(8,128)(2,1)S(1)}, u32[]{:S(2)}, u32[]{:S(2)}) collective-permute-start(bf16[128,1024]{1,0:T(8,128)(2,1)S(1)} %copy-done.19), channel_id=1, source_target_pairs={{0,6},{2,4},{4,2},{6,0},{8,14},{10,12},{12,10},{14,8},{1,7},{3,5},... | collective-permute-start | bytes 786440 | tf_op jit(solution)/shard_map/ppermute | solution.py:20
  72.3 26.0 %collective-permute-start.3 = (bf16[128,1024]{1,0:T(8,128)(2,1)S(1)}, bf16[128,1024]{1,0:T(8,128)(2,1)S(1)}, u32[]{:S(2)}, u32[]{:S(2)}) collective-permute-start(bf16[128,1024]{1,0:T(8,128)(2,1)S(1)} %copy-done.18), channel_id=1, source_target_pairs={{0,2},{2,0},{4,6},{6,4},{8,10},{10,8},{12,14},{14,12},{1,3},{3,1},... | collective-permute-start | bytes 786440 | tf_op jit(solution)/shard_map/ppermute | solution.py:20
  86.2 12.2 %collective-permute-start.2 = (bf16[128,1024]{1,0:T(8,128)(2,1)S(1)}, bf16[128,1024]{1,0:T(8,128)(2,1)S(1)}, u32[]{:S(2)}, u32[]{:S(2)}) collective-permute-start(bf16[128,1024]{1,0:T(8,128)(2,1)S(1)} %copy-done.17), channel_id=1, source_target_pairs={{0,4},{2,6},{4,0},{6,2},{8,12},{10,14},{12,8},{14,10},{1,5},{3,7},... | collective-permute-start | bytes 786440 | tf_op jit(solution)/shard_map/ppermute | solution.py:20
  98.3 94.1 %collective-permute-start.23 = (bf16[1024,128]{1,0:T(8,128)(2,1)S(1)}, bf16[1024,128]{1,0:T(8,128)(2,1)}, u32[]{:S(2)}, u32[]{:S(2)}) collective-permute-start(bf16[1024,128]{1,0:T(8,128)(2,1)S(1)} %bitcast.45), channel_id=1, source_target_pairs={{0,1},{1,0},{2,3},{3,2},{4,5},{5,4},{6,7},{7,6},{8,9},{9,8},{10,11... | collective-permute-start | bytes 786440 | tf_op jit(solution)/shard_map/ppermute | solution.py:24
  108.8 26.4 %collective-permute-start.19 = (bf16[2,128,1152]{2,1,0:T(8,128)(2,1)}, bf16[2,128,1152]{2,1,0:T(8,128)(2,1)}, u32[]{:S(2)}, u32[]{:S(2)}) collective-permute-start(bf16[2,128,1152]{2,1,0:T(8,128)(2,1)} %get-tuple-element.32), channel_id=1, source_target_pairs={{0,2},{2,0},{4,6},{6,4},{8,10},{10,8},{12,14},{14,12},{1,3},{3,1},... | collective-permute-start | bytes 1769480 | tf_op jit(solution)/shard_map/ppermute | solution.py:20
  114.2 104.4 %all-to-all-start.1 = ((bf16[8,128,1024]{2,1,0:T(8,128)(2,1)}), bf16[8,128,1024]{2,1,0:T(8,128)(2,1)}, u32[]{:S(2)}, u32[]{:S(2)}) async-start(bf16[8,128,1024]{2,1,0:T(8,128)(2,1)} %copy-done.1), calls=%async_computation.1 | async-start | bytes 4194304 | tf_op jit(solution)/shard_map/all_to_all | solution.py:319
  119.5 40.4 %collective-permute-start.17 = (bf16[2,128,1152]{2,1,0:T(8,128)(2,1)}, bf16[2,128,1152]{2,1,0:T(8,128)(2,1)}, u32[]{:S(2)}, u32[]{:S(2)}) collective-permute-start(bf16[2,128,1152]{2,1,0:T(8,128)(2,1)} %get-tuple-element.29), channel_id=1, source_target_pairs={{0,2},{2,0},{4,6},{6,4},{8,10},{10,8},{12,14},{14,12},{1,3},{3,1},... | collective-permute-start | bytes 1769480 | tf_op jit(solution)/shard_map/ppermute | solution.py:20
  121.5 70.9 %collective-permute-start.22 = (bf16[1024,512]{1,0:T(8,128)(2,1)}, bf16[1024,512]{1,0:T(8,128)(2,1)}, u32[]{:S(2)}, u32[]{:S(2)}) collective-permute-start(bf16[1024,512]{1,0:T(8,128)(2,1)} %get-tuple-element.35), channel_id=1, source_target_pairs={{0,1},{1,0},{2,3},{3,2},{4,5},{5,4},{6,7},{7,6},{8,9},{9,8},{10,11... | collective-permute-start | bytes 3145736 | tf_op jit(solution)/shard_map/ppermute | solution.py:24
  138.3 27.2 %collective-permute-start.20 = (bf16[1,128,1152]{2,1,0:T(8,128)(2,1)}, bf16[1,128,1152]{2,1,0:T(8,128)(2,1)}, u32[]{:S(2)}, u32[]{:S(2)}) collective-permute-start(bf16[1,128,1152]{2,1,0:T(8,128)(2,1)} %concatenate.73), channel_id=1, source_target_pairs={{0,4},{2,6},{4,0},{6,2},{8,12},{10,14},{12,8},{14,10},{1,5},{3,7},... | collective-permute-start | bytes 884744 | tf_op jit(solution)/shard_map/ppermute | solution.py:20
  164.4 12.4 %collective-permute-start.18 = (bf16[1,128,1152]{2,1,0:T(8,128)(2,1)}, bf16[1,128,1152]{2,1,0:T(8,128)(2,1)}, u32[]{:S(2)}, u32[]{:S(2)}) collective-permute-start(bf16[1,128,1152]{2,1,0:T(8,128)(2,1)} %concatenate.72), channel_id=1, source_target_pairs={{0,4},{2,6},{4,0},{6,2},{8,12},{10,14},{12,8},{14,10},{1,5},{3,7},... | collective-permute-start | bytes 884744 | tf_op jit(solution)/shard_map/ppermute | solution.py:20
  169.9 16.2 %collective-permute-start.21 = (bf16[1,128,1152]{2,1,0:T(8,128)(2,1)}, bf16[1,128,1152]{2,1,0:T(8,128)(2,1)S(1)}, u32[]{:S(2)}, u32[]{:S(2)}) collective-permute-start(bf16[1,128,1152]{2,1,0:T(8,128)(2,1)} %concatenate.74), channel_id=1, source_target_pairs={{0,8},{2,10},{4,12},{6,14},{8,0},{10,2},{12,4},{14,6},{1,9},{3,11}... | collective-permute-start | bytes 884744 | tf_op jit(solution)/shard_map/ppermute | solution.py:20
  191.3 12.0 %collective-permute-start.25 = (bf16[2,128,128]{2,1,0:T(8,128)(2,1)S(1)}, bf16[2,128,128]{2,1,0:T(8,128)(2,1)S(1)}, u32[]{:S(2)}, u32[]{:S(2)}) collective-permute-start(bf16[2,128,128]{2,1,0:T(8,128)(2,1)S(1)} %pad_maximum_fusion.8), channel_id=1, source_target_pairs={{0,4},{2,6},{4,0},{6,2},{8,12},{10,14},{12,8},{14,10},{1,5},{3,7},... | collective-permute-start | bytes 196616 | tf_op jit(solution)/shard_map/ppermute | solution.py:20
  192.3 18.4 %collective-permute-start.27 = (bf16[1024,64]{1,0:T(8,128)(2,1)S(1)}, bf16[1024,64]{1,0:T(8,128)(2,1)S(1)}, u32[]{:S(2)}, u32[]{:S(2)}) collective-permute-start(bf16[1024,64]{1,0:T(8,128)(2,1)S(1)} %get-tuple-element.56), channel_id=1, source_target_pairs={{0,1},{1,0},{2,3},{3,2},{4,5},{5,4},{6,7},{7,6},{8,9},{9,8},{10,11... | collective-permute-start | bytes 393224 | tf_op jit(solution)/shard_map/ppermute | solution.py:24
  (39 other events, 440.7 us)

commit v3 on v0

v3 whole, which is shorter than its diff:
```python
import functools

import jax
import jax.numpy as jnp
from jax import lax
from jax.experimental import pallas as pl
from jax.experimental.pallas import tpu as pltpu
from jax.sharding import Mesh
from jax.sharding import PartitionSpec as P

RANK = 64
BLK = 64
PAIR = 2 * RANK

adapter_scale = 0.5
norm_eps = 1e-05

QUICK = pl.CostEstimate(flops=1, bytes_accessed=1, transcendentals=0)
MIB = 1024 * 1024


def over_line(value, mask):
    size = lax.axis_size("line")
    return lax.ppermute(value, "line", [(i, i ^ mask) for i in range(size)])


def over_pair(value):
    return lax.ppermute(value, "pair", [(0, 1), (1, 0)])


def over_cores(value):
    return lax.ppermute(value, "core", [(0, 1), (1, 0)])


def after(value, *others):
    return lax.optimization_barrier((value,) + others)[0]


def swap_rest(mine, for_core, crossed):
    beside = over_cores(jnp.stack([for_core, crossed[1]]))
    return [mine, beside[0], crossed[0], beside[1]]


def order_kernel(place_ref, *refs):
    for r, ref in enumerate(refs[:-1]):
        refs[-1][place_ref[0] ^ r] = ref[...]


def in_order(parts, place):
    shape = jax.ShapeDtypeStruct((4,) + parts[0].shape, parts[0].dtype)
    ordered = call(order_kernel, shape, [place.reshape(1)], parts, 24)
    return ordered.reshape((-1,) + parts[0].shape[1:])


def gather_line(held):
    size = lax.axis_size("line")
    pieces, slots, step = [(held, [0, size // 2])], [0, size // 2], size // 4
    while step:
        arrived = over_line(held, step)
        more = [s ^ step for s in slots]
        pieces.append((arrived, more))
        slots, step = slots + more, step // 2
        held = jnp.concatenate([held, arrived]) if step else held
    return pieces


def in_slots(pieces):
    rows = pieces[0][0].shape[0] // 2
    found = {m: p[i * rows : (i + 1) * rows] for p, ms in pieces for i, m in enumerate(ms)}
    return jnp.concatenate([found[m] for m in range(len(found))])


def two_terms(low):
    high = lax.reduce_precision(low, 8, 7)
    return jnp.concatenate([high, low - high], axis=-1).astype(jnp.bfloat16)


def one_term(sent):
    sent = sent.astype(jnp.float32)
    return sent[..., :RANK] + sent[..., RANK:]


def adapter_columns(adapter):
    return pl.ds(pl.multiple_of((adapter // 2) * PAIR, PAIR), PAIR)


def adapter_half(both, adapter):
    return jnp.where(adapter % 2 == 0, both[:, :RANK], both[:, RANK:])


def on_diagonal(update):
    row = lax.broadcasted_iota(jnp.int32, update.shape, 0) // BLK
    column = lax.broadcasted_iota(jnp.int32, update.shape, 1) // RANK
    return jnp.where(row == column, update, jnp.zeros_like(update))


def call(kernel, out_shape, scalars, arrays, limit):
    vmem, smem = pl.BlockSpec(memory_space=pltpu.VMEM), pl.BlockSpec(memory_space=pltpu.SMEM)
    return pl.pallas_call(
        kernel,
        out_shape=out_shape,
        in_specs=[smem] * len(scalars) + [vmem] * len(arrays),
        out_specs=jax.tree.map(lambda _: vmem, out_shape),
        cost_estimate=QUICK,
        compiler_params=pltpu.CompilerParams(vmem_limit_bytes=60 * MIB),
    )(*scalars, *arrays)


def first_kernel(slots, wanted, line_ref, tenant_ref, tokens_ref, gain_ref, up_ref, table_ref, inverse_ref, *normed_refs):
    columns_kernel(wanted, tenant_ref, up_ref, table_ref)
    features = tokens_ref.shape[1]
    width = features // slots
    total = jnp.zeros(inverse_ref.shape, jnp.float32)
    for s in range(slots):
        wide = tokens_ref[:, s * width : (s + 1) * width].astype(jnp.float32)
        total += jnp.sum(wide * wide, axis=1, keepdims=True)
    inverse = lax.rsqrt(total / features + norm_eps)
    inverse_ref[...] = inverse
    for s in range(slots):
        columns = pl.ds(pl.multiple_of((line_ref[0] ^ s) * width, width), width)
        wide = tokens_ref[:, columns].astype(jnp.float32)
        normed_refs[s][...] = (wide * inverse * gain_ref[:, columns]).astype(jnp.bfloat16)


def norm_and_up(line, tenant, tokens, gain, up_factor, wanted):
    rows, features = tokens.shape
    slots = len(wanted) // 4
    shapes = [
        jax.ShapeDtypeStruct((len(wanted), up_factor.shape[0], len(wanted[0]) * RANK), up_factor.dtype),
        jax.ShapeDtypeStruct((rows, 1), jnp.float32),
    ] + [jax.ShapeDtypeStruct((rows, features // slots), jnp.bfloat16)] * slots
    return call(
        functools.partial(first_kernel, slots, wanted), shapes, [line, tenant], [tokens, gain, up_factor], 40
    )


def columns_kernel(wanted, tenant_ref, factor_ref, *out_refs):
    refs = [r.at[i] for r in out_refs for i in range(r.shape[0])]
    for d, blocks in enumerate(wanted):
        for first in range(0, len(blocks), 2):
            parts = []
            for b in blocks[first : first + 2]:
                adapter = tenant_ref[b]
                parts.append(adapter_half(factor_ref[:, adapter_columns(adapter)], adapter))
            refs[d][:, first * RANK : first * RANK + PAIR] = jnp.concatenate(parts, axis=1)


def columns_of(wanted, tenants, factor, stacks):
    shapes = [
        jax.ShapeDtypeStruct((n, factor.shape[0], len(wanted[0]) * RANK), factor.dtype) for n in stacks
    ]
    return call(functools.partial(columns_kernel, wanted), shapes, [tenants], [factor], 24)


def scaled_kernel(upstream_ref, far_ref, up_ref, out_ref):
    rows = upstream_ref.shape[0]
    for which, ref in enumerate((upstream_ref, far_ref)):
        mixed = jnp.dot(ref[...], up_ref[...], preferred_element_type=jnp.float32)
        for b in range(rows // BLK):
            at = which * rows + b * BLK
            block = mixed[b * BLK : (b + 1) * BLK, at // BLK * RANK : (at // BLK + 1) * RANK]
            scaled = (adapter_scale * block).astype(out_ref.dtype)
            out_ref[at : at + BLK, :] = jnp.concatenate([scaled, scaled], axis=1)


def back_kernel(pieces, rows, weight_ref, down_ref, scaled_ref, *refs):
    upstream_refs, out_refs = refs[: len(pieces)], refs[len(pieces) :]
    contract = (((1,), (1,)), ((), ()))
    for upstream_ref, slots in zip(upstream_refs, pieces):
        product = lax.dot_general(
            upstream_ref[...], weight_ref[...], contract, preferred_element_type=jnp.float32
        )
        for at, slot in enumerate(slots):
            for r in range(0, rows, 2 * BLK):
                first, held = at * rows + r, slot * rows + r
                column = held // BLK * RANK
                term = lax.dot_general(
                    on_diagonal(scaled_ref[held : held + 2 * BLK, :]),
                    down_ref[:, column : column + PAIR],
                    contract,
                    preferred_element_type=jnp.float32,
                )
                out_refs[slot][r : r + 2 * BLK, :] = (product[first : first + 2 * BLK] + term).astype(jnp.bfloat16)


def value_kernel(slots, weight_ref, down_ref, *refs):
    normed_refs, (values_ref, low_ref, sent_ref) = refs[:slots], refs[slots:]
    value_width = weight_ref.shape[1]
    for slot in range(slots):
        normed = normed_refs[slot][...]
        rows = normed.shape[0]
        values = jnp.dot(normed, weight_ref[...], preferred_element_type=jnp.float32)
        low = []
        for b in range(rows // BLK):
            column = (slot * rows // BLK + b) // 2 * PAIR
            both = jnp.dot(
                normed[b * BLK : (b + 1) * BLK],
                down_ref[:, column : column + PAIR],
                preferred_element_type=jnp.float32,
            )
            low.append(both[:, b % 2 * RANK : (b % 2 + 1) * RANK])
        low = jnp.concatenate(low, axis=0)
        if slot % 2:
            high = low.astype(jnp.bfloat16)
            rest = (low - high.astype(jnp.float32)).astype(jnp.bfloat16)
            sent_ref[slot // 2, :, :value_width] = values.astype(jnp.bfloat16)
            sent_ref[slot // 2, :, value_width:] = jnp.concatenate([high, rest], axis=1)
        else:
            values_ref[slot // 2] = values
            low_ref[slot // 2] = low


def value_products(weight, down, normed):
    slots, rows = len(normed), normed[0].shape[0]
    half, value_width = slots // 2, weight.shape[1]
    shapes = [
        jax.ShapeDtypeStruct((half, rows, value_width), jnp.float32),
        jax.ShapeDtypeStruct((half, rows, RANK), jnp.float32),
        jax.ShapeDtypeStruct((half, rows, value_width + PAIR), jnp.bfloat16),
    ]
    return call(functools.partial(value_kernel, slots), shapes, [], [weight, down, *normed], 56)


def sum_over_line(values, low, crossed, waits):
    value_width, far, step = values.shape[-1], lax.axis_size("line") // 2, 2
    values = values + crossed[..., :value_width].astype(jnp.float32)
    low = low + one_term(crossed[..., value_width:])
    while step < far:
        low = low[::2] + one_term(over_line(two_terms(low[1::2]), step))
        values = values[::2] + over_line(values[1::2].astype(jnp.bfloat16), step).astype(jnp.float32)
        step *= 2
    low = low + one_term(over_line(after(two_terms(low), *waits), far))[::-1]
    return values[0] + over_line(values[1].astype(jnp.bfloat16), far).astype(jnp.float32), low


def terms_kernel(slots, scale, place_ref, update_ref, *refs):
    rows_refs, out_ref = refs[:slots], refs[slots]
    rows, width = rows_refs[0].shape
    shard = width // 4
    for slot in range(slots):
        for r in range(0, rows, 2 * BLK):
            first = slot * rows + r
            term = scale * lax.dot_general(
                rows_refs[slot][r : r + 2 * BLK, :],
                on_diagonal(update_ref[first : first + 2 * BLK, :]),
                (((0,), (0,)), ((), ())),
                preferred_element_type=jnp.float32,
            )
            term = term.astype(jnp.bfloat16)
            column = first // BLK * RANK
            for p in range(4):
                out_ref[place_ref[0] ^ p, :, column : column + PAIR] = term[p * shard : (p + 1) * shard]


def factor_terms(place, update, rows, scale):
    slots, (count, width) = len(rows), rows[0].shape
    shape = jax.ShapeDtypeStruct((4, width // 4, slots * count // BLK * RANK), jnp.bfloat16)
    return call(functools.partial(terms_kernel, slots, scale), shape, [place], [update, *rows], 48)


def owner_kernel(blocks, tenant_ref, *refs):
    out_ref = refs[-1]
    out_ref[...] = jnp.zeros_like(out_ref)
    lane = lax.broadcasted_iota(jnp.int32, (out_ref.shape[0], PAIR), 1) // RANK
    for r, terms_ref in enumerate(refs[:-1]):
        for first in range(0, blocks, 2):
            both = terms_ref[:, first * RANK : first * RANK + PAIR].astype(jnp.float32)
            turned = jnp.concatenate([both[:, RANK:], both[:, :RANK]], axis=1)
            for h in range(2):
                adapter = tenant_ref[r * blocks + first + h]
                side = adapter % 2
                term = jnp.where(side == h, both, turned)
                out_ref[:, adapter_columns(adapter)] += jnp.where(lane == side, term, jnp.zeros_like(term))


def owner_sums(tenants, terms, width):
    blocks = tenants.shape[1]
    shape = jax.ShapeDtypeStruct((terms[0].shape[0], width), jnp.float32)
    return call(functools.partial(owner_kernel, blocks), shape, [tenants.reshape(-1)], terms, 40)


def token_grad_kernel(slots, line_ref, tokens_ref, gain_ref, inverse_ref, *refs):
    back_refs, out_ref = refs[:-1], refs[-1]
    width = back_refs[0].shape[1]
    inverse = inverse_ref[...]
    total = jnp.zeros_like(inverse)

    def load(s):
        columns = pl.ds(pl.multiple_of((line_ref[0] ^ s) * width, width), width)
        gained = gain_ref[:, columns] * back_refs[s][...].astype(jnp.float32)
        return columns, gained, tokens_ref[:, columns].astype(jnp.float32)

    for s in range(slots):
        _, gained, wide = load(s)
        total += jnp.sum(gained * wide, axis=1, keepdims=True)
    cubed = inverse * inverse * inverse
    inner = total / tokens_ref.shape[1]
    for s in range(slots):
        columns, gained, wide = load(s)
        out_ref[:, columns] = (inverse * gained - wide * cubed * inner).astype(out_ref.dtype)


def on_device(tokens, upstream, norm_gain, value_weight, down_factor, up_factor, tenant):
    size, far = lax.axis_size("line"), lax.axis_size("line") // 2
    line, pair, core = lax.axis_index("line"), lax.axis_index("pair"), lax.axis_index("core")
    place = 2 * pair + core
    line_, place_ = line.reshape(1), place.reshape(1)
    rows = tokens.shape[0]
    blocks = rows // BLK
    value_width = upstream.shape[1]
    adapter_width = down_factor.shape[1]
    value_rows = up_factor.shape[0]
    gain = norm_gain.reshape(1, -1)

    tenants_of = tenant.reshape(size, 4, blocks)
    tenants = tenants_of[line ^ jnp.arange(size, dtype=jnp.int32)].transpose(1, 0, 2)
    tenants = tenants[place ^ jnp.arange(4, dtype=jnp.int32)].reshape(4, size * blocks)

    upstream_far = over_line(upstream, far)

    wanted = [
        [e * blocks + b for e in (d, d ^ (4 * far)) for b in range(blocks)] for d in range(4 * size)
    ]
    up_sent, inverse, *normed = norm_and_up(line_, tenant, tokens, gain, up_factor, wanted)
    arrived = [normed[0]] + [over_line(after(normed[s], upstream_far), s) for s in range(1, far + 1)]
    up_mine = lax.all_to_all(
        after(up_sent, upstream_far, over_cores(inverse)), ("line", "pair", "core"), split_axis=0, concat_axis=0, tiled=True
    )
    up_mine = up_mine.reshape(value_width, 2 * blocks * RANK)

    across = over_pair(value_weight)
    down_mine, down_core, down_pair = columns_of(
        [[r * size * blocks + b for b in range(size * blocks)] for r in range(4)],
        tenants.reshape(-1),
        after(down_factor, normed[0]),
        [1, 1, 2],
    )
    down_crossed = over_pair(down_pair)

    pieces = gather_line(jnp.concatenate([upstream, upstream_far]))
    scaled = call(
        scaled_kernel,
        jax.ShapeDtypeStruct((2 * rows, PAIR), jnp.bfloat16),
        [],
        [after(upstream, *arrived[1:], across, down_crossed, *[p for p, _ in pieces]), upstream_far, up_mine],
        16,
    )
    scaled = in_slots(gather_line(scaled))
    arrived += [over_line(after(normed[s], scaled), s) for s in range(far + 1, size)]
    across, down_crossed, scaled = lax.optimization_barrier((across, down_crossed, scaled))
    beside = over_cores(jnp.stack([value_weight, across]))
    weight = in_order([value_weight, beside[0], across, beside[1]], place)
    down = in_order(swap_rest(down_mine[0], down_core[0], down_crossed), place)

    back = call(
        functools.partial(back_kernel, [s for _, s in pieces], rows),
        [jax.ShapeDtypeStruct((rows, weight.shape[0]), jnp.bfloat16)] * size,
        [],
        [weight, down, scaled] + [p for p, _ in pieces],
        56,
    )
    half = rows // 2
    first = over_line(back[far][:half], far)

    values, low, sent = value_products(after(weight, back[0]), down, arrived)
    crossed = over_line(after(sent, first), 1)
    back_mine = {s: over_line(after(back[s], crossed), s) for s in range(1, far)}
    back_mine[0] = back[0]
    back_mine[far] = jnp.concatenate([first, over_line(after(back[far][half:], first), far)])
    for s in range(far + 1, size):
        back_mine[s] = over_line(after(back[s], first), s)
    back_mine = [back_mine[s] for s in range(size)]

    terms = factor_terms(place_, after(scaled, first), arrived, 1.0)
    terms = swap_rest(terms[0], terms[1], over_pair(terms[2:]))
    grad_down = owner_sums(tenants, terms, adapter_width)

    values, low = sum_over_line(values, low, crossed, back_mine[far : far + 1])
    low = low.astype(jnp.bfloat16)
    columns = [
        (lax.dynamic_slice_in_dim(p, line * 4 * value_rows, 4 * value_rows, 1), s)
        for p, s in pieces
    ]
    low_held = jnp.concatenate([low, low], axis=-1).reshape(2 * rows, PAIR)
    low_all = in_slots(gather_line(after(low_held, grad_down, *back_mine[far + 1 :])))
    terms = factor_terms(place_, low_all, [in_slots(columns)], adapter_scale)
    terms = swap_rest(terms[0], terms[1], over_pair(terms[2:]))
    grad_up = owner_sums(tenants, terms, adapter_width)

    adapter_branch = jnp.einsum(
        "bkr,vbr->bkv",
        low[0].reshape(blocks, BLK, RANK),
        up_mine[:, : blocks * RANK].reshape(value_width, blocks, RANK),
        preferred_element_type=jnp.float32,
    ).reshape(rows, value_width)
    adapted_values = (values + adapter_scale * adapter_branch).astype(jnp.bfloat16)

    grad_tokens = call(
        functools.partial(token_grad_kernel, size),
        jax.ShapeDtypeStruct(tokens.shape, tokens.dtype),
        [line_],
        [tokens, gain, after(inverse, grad_down, grad_up), *back_mine],
        32,
    )
    return (adapted_values, grad_tokens, grad_down, grad_up)


def solution(mesh):
    groups, shards = mesh.shape["groups"], mesh.shape["fsdp"]
    line_mesh = Mesh(mesh.devices.reshape(groups, shards // 4, 2, 2), ("groups", "line", "pair", "core"))
    own = ("line", "pair", "core")
    everywhere = P(("groups",) + own, None)
    in_specs = (everywhere, everywhere, P(), P(own, None), P(own, None), P(own, None), P("groups"))
    out_specs = (everywhere,) * 4
    return jax.shard_map(
        on_device, mesh=line_mesh, in_specs=in_specs, out_specs=out_specs, check_vma=False
    )
```

time: 345 us -> 202 us (0.59)
  the two profiles are of different devices: /device:TPU:15 before, /device:TPU:0 now
where the time goes in v3:
time: 202 us; the launch traced here: 201 us
  waiting for transfers between devices  80.9 us (40%)
  Pallas kernels  57.1 us (28%)
  starting transfers between devices  31.3 us (15%)
  local copies, waits for them, and re-layouts  25 us (12%)
  other arithmetic  5.14 us (3%)
    ppermute x14, waiting for transfers between devices, over_line(): return lax.ppermute(value, 'line', [(i, i ^ mask) for i in range(size)])  75.9 us
    pallas_call x12, Pallas kernels, call(): pl.pallas_call(kernel, out_shape=out_shape, in_specs=[smem] * len(scalars...  57.1 us
    ppermute x14, starting transfers between devices, over_line(): return lax.ppermute(value, 'line', [(i, i ^ mask) for i in range(size)])  21.5 us
    squeeze x6, local copies, waits for them, and re-layouts, swap_rest(): return [mine, beside[0], crossed[0], beside[1]]  6.39 us
    ppermute x4, starting transfers between devices, over_pair(): return lax.ppermute(value, 'pair', [(0, 1), (1, 0)])  5.11 us
    slice x4, local copies, waits for them, and re-layouts, on_device(): terms = swap_rest(terms[0], terms[1], over_pair(terms[2:]))  4.7 us
    all_to_all x1, starting transfers between devices, on_device(): lax.all_to_all(after(up_sent, upstream_far, over_cores(inverse)), ('line'...  4.09 us
  transfers between devices with their start and end apart: 23, of which 13 were waited for; matrix products, arithmetic and copies ran while one was open for 12% of the time, Pallas kernels for 24%

profile of v3, /device:TPU:0, one launch (start us, length us, event | category | flops | bytes accessed | tf_op | source)
XLA Modules:
  0.0 200.7 jit_solution(5772341520397229166)
XLA Ops:
  0.6 4.1 %collective-permute-start.2 = (bf16[128,1024]{1,0:T(8,128)(2,1)}, bf16[128,1024]{1,0:T(8,128)(2,1)S(1)}, u32[]{:S(2)}, u32[]{:S(2)}) collective-permute-start(bf16[128,1024]{1,0:T(8,128)(2,1)} %upstream_ref), channel_id=1, source_target_pairs={{0,8},{4,12},{8,0},{12,4},{1,9},{5,13},{9,1},{13,5},{2,10},{6,14},... | collective-permute-start | bytes 786440 | tf_op jit(solution)/shard_map/ppermute | solution.py:24
  7.1 6.3 %shard_map.102 = (bf16[16,64,256]{2,1,0:T(8,128)(2,1)}, f32[128,1]{1,0:T(8,128)}, bf16[128,2048]{1,0:T(8,128)(2,1)}, bf16[128,2048]{1,0:T(8,128)(2,1)}, bf16[128...) custom-call(s32[1]{0:T(128)} %bitcast.5.line_ref, s32[32]{0:T(128)} %tenant_ref.1, bf16[128,8192]{1,0:T(8,128)(2,1)} %tokens_ref.3, ...), custom_call_target="tpu_custom_call" | custom-call | flops 1 | bytes 1 | tf_op jit(solution)/shard_map/pallas_call | solution.py:99
  15.5 6.3 %shard_map.103 = (bf16[1,512,512]{2,1,0:T(8,128)(2,1)}, bf16[1,512,512]{2,1,0:T(8,128)(2,1)}, bf16[2,512,512]{2,1,0:T(8,128)(2,1)}) custom-call(s32[32]{0:T(128)} %reshape_reshape.2.tenant_ref, bf16[512,2048]{1,0:T(8,128)(2,1)} %factor_ref), custom_call_target="tpu_custom_call" | custom-call | flops 1 | bytes 1 | tf_op jit(solution)/shard_map/pallas_call | solution.py:99
  22.2 4.1 %all-to-all-start = ((bf16[16,64,256]{2,1,0:T(8,128)(2,1)}), bf16[16,64,256]{2,1,0:T(8,128)(2,1)S(1)}, u32[]{:S(2)}, u32[]{:S(2)}) async-start(bf16[16,64,256]{2,1,0:T(8,128)(2,1)} %get-tuple-element.47), calls=%async_computation | async-start | bytes 1048576 | tf_op jit(solution)/shard_map/all_to_all | solution.py:326
  28.2 2.4 %collective-permute-start.4 = (bf16[128,2048]{1,0:T(8,128)(2,1)}, bf16[128,2048]{1,0:T(8,128)(2,1)S(1)}, u32[]{:S(2)}, u32[]{:S(2)}) collective-permute-start(bf16[128,2048]{1,0:T(8,128)(2,1)} %get-tuple-element.44), channel_id=1, source_target_pairs={{0,8},{4,12},{8,0},{12,4},{1,9},{5,13},{9,1},{13,5},{2,10},{6,14},... | collective-permute-start | bytes 1572872 | tf_op jit(solution)/shard_map/ppermute | solution.py:24
  31.2 27.7 %collective-permute-done.5.refs_1_ = bf16[256,1024]{1,0:T(8,128)(2,1)S(1)} collective-permute-done((bf16[256,1024]{1,0:T(8,128)(2,1)S(1)}, bf16[256,1024]{1,0:T(8,128)(2,1)S(1)}, u32[]{:S(2)}, u32[]{:S(2)}) %collective-permute-start.5) | collective-permute-done | bytes 524320 | tf_op jit(solution)/shard_map/ppermute | solution.py:24
  58.9 5.2 %collective-permute-done.4.refs_2_ = bf16[128,2048]{1,0:T(8,128)(2,1)S(1)} collective-permute-done((bf16[128,2048]{1,0:T(8,128)(2,1)}, bf16[128,2048]{1,0:T(8,128)(2,1)S(1)}, u32[]{:S(2)}, u32[]{:S(2)}) %collective-permute-start.4) | collective-permute-done | bytes 524320 | tf_op jit(solution)/shard_map/ppermute | solution.py:24
  64.1 7.4 %collective-permute-done.3.refs_1_ = bf16[128,2048]{1,0:T(8,128)(2,1)S(1)} collective-permute-done((bf16[128,2048]{1,0:T(8,128)(2,1)}, bf16[128,2048]{1,0:T(8,128)(2,1)S(1)}, u32[]{:S(2)}, u32[]{:S(2)}) %collective-permute-start.3) | collective-permute-done | bytes 524320 | tf_op jit(solution)/shard_map/ppermute | solution.py:24
  73.2 2.2 %shard_map.104 = bf16[256,128]{1,0:T(8,128)(2,1)} custom-call(bf16[128,1024]{1,0:T(8,128)(2,1)} %upstream_ref, bf16[128,1024]{1,0:T(8,128)(2,1)} %copy-done.11, bf16[1024,256]{1,0:T(8,128)(2,1)} %bitcast.63), custom_call_target="tpu_custom_call" | custom-call | flops 1 | bytes 1 | tf_op jit(solution)/shard_map/pallas_call | solution.py:99
  76.7 3.2 %collective-permute-done.6 = bf16[256,128]{1,0:T(8,128)(2,1)S(1)} collective-permute-done((bf16[256,128]{1,0:T(8,128)(2,1)}, bf16[256,128]{1,0:T(8,128)(2,1)S(1)}, u32[]{:S(2)}, u32[]{:S(2)}) %collective-permute-start.6) | collective-permute-done | bytes 65568 | tf_op jit(solution)/shard_map/ppermute | solution.py:24
  84.8 2.4 %collective-permute-start.9 = (bf16[128,2048]{1,0:T(8,128)(2,1)}, bf16[128,2048]{1,0:T(8,128)(2,1)S(1)}, u32[]{:S(2)}, u32[]{:S(2)}) collective-permute-start(bf16[128,2048]{1,0:T(8,128)(2,1)} %get-tuple-element.56), channel_id=1, source_target_pairs={{0,12},{4,8},{8,4},{12,0},{1,13},{5,9},{9,5},{13,1},{2,14},{6,10},... | collective-permute-start | bytes 1572872 | tf_op jit(solution)/shard_map/ppermute | solution.py:24
  88.8 3.0 %shard_map.106 = bf16[4,512,512]{2,1,0:T(8,128)(2,1)} custom-call(s32[1]{0:T(128)} %bitcast.place_ref, bf16[512,512]{1,0:T(8,128)(2,1)} %bitcast.66, bf16[512,512]{1,0:T(8,128)(2,1)} %get-tuple-element.83.refs_1_, bf16[512,512]{1,0:T(8,128)(2,1)} %get-tuple-element.84.refs_2_, bf16[512,512]{1,0:T(8,128)(2,1)} %get-tuple-element.82.refs_3_), custom_call_target="tpu_custom_call" | custom-call | flops 1 | bytes 1 | tf_op jit(solution)/shard_map/pallas_call | solution.py:99
  91.8 3.1 %slice_bitcast_fusion = (bf16[512,1024]{1,0:T(8,128)(2,1)}, bf16[512,1024]{1,0:T(8,128)(2,1)}) fusion(bf16[2,512,1024]{2,1,0:T(8,128)(2,1)} %collective-permute-done.7), kind=kLoop, calls=%fused_computation.4 | loop fusion | bytes 4194304 | tf_op jit(solution)/shard_map/squeeze | solution.py:352
  94.8 4.5 %shard_map.105 = bf16[4,512,1024]{2,1,0:T(8,128)(2,1)} custom-call(s32[1]{0:T(128)} %bitcast.place_ref, bf16[512,1024]{1,0:T(8,128)(2,1)} %refs_0_.1, bf16[512,1024]{1,0:T(8,128)(2,1)} %get-tuple-element.77.refs_1_, bf16[512,1024]{1,0:T(8,128)(2,1)} %copy-done.2, bf16[512,1024]{1,0:T(8,128)(2,1)} %get-tuple-element.76.refs_3_), custom_call_target="tpu_custom_call" | custom-call | flops 1 | bytes 1 | tf_op jit(solution)/shard_map/pallas_call | solution.py:99
  99.3 7.0 %shard_map.107 = (bf16[128,2048]{1,0:T(8,128)(2,1)}, bf16[128,2048]{1,0:T(8,128)(2,1)}, bf16[128,2048]{1,0:T(8,128)(2,1)}, bf16[128,2048]{1,0:T(8,128)(2,1)}) custom-call(bf16[2048,1024]{1,0:T(8,128)(2,1)} %bitcast.57, bf16[2048,512]{1,0:T(8,128)(2,1)} %bitcast.59, bf16[512,128]{1,0:T(8,128)(2,1)} %pad_maximum_fusion.4.scaled_ref.update_ref, ...), custom_call_target="tpu_custom_call" | custom-call | flops 1 | bytes 1 | tf_op jit(solution)/shard_map/pallas_call | solution.py:99
  107.5 2.6 %collective-permute-start.10 = (bf16[64,2048]{1,0:T(8,128)(2,1)S(1)}, bf16[64,2048]{1,0:T(8,128)(2,1)S(1)}, u32[]{:S(2)}, u32[]{:S(2)}) collective-permute-start(bf16[64,2048]{1,0:T(8,128)(2,1)S(1)} %get-tuple-element.91), channel_id=1, source_target_pairs={{0,8},{4,12},{8,0},{12,4},{1,9},{5,13},{9,1},{13,5},{2,10},{6,14},... | collective-permute-start | bytes 786440 | tf_op jit(solution)/shard_map/ppermute | solution.py:24
  113.5 7.4 %shard_map.108 = (f32[2,128,1024]{2,1,0:T(8,128)}, f32[2,128,64]{2,1,0:T(8,128)}, bf16[2,128,1152]{2,1,0:T(8,128)(2,1)}) custom-call(bf16[2048,1024]{1,0:T(8,128)(2,1)} %bitcast.58, bf16[2048,512]{1,0:T(8,128)(2,1)} %bitcast.60, bf16[128,2048]{1,0:T(8,128)(2,1)} %get-tuple-element.38.refs_0_, bf16[128,2048]{1,0:T(8,128)(2,1)} %copy-done.6, ...), custom_call_target="tpu_custom_call" | custom-call | flops 1 | bytes 1 | tf_op jit(solution)/shard_map/pallas_call | solution.py:99
  122.3 3.0 %collective-permute-start.11 = (bf16[2,128,1152]{2,1,0:T(8,128)(2,1)}, bf16[2,128,1152]{2,1,0:T(8,128)(2,1)S(1)}, u32[]{:S(2)}, u32[]{:S(2)}) collective-permute-start(bf16[2,128,1152]{2,1,0:T(8,128)(2,1)} %get-tuple-element.60), channel_id=1, source_target_pairs={{0,4},{4,0},{8,12},{12,8},{1,5},{5,1},{9,13},{13,9},{2,6},{6,2},{1... | collective-permute-start | bytes 1769480 | tf_op jit(solution)/shard_map/ppermute | solution.py:24
  125.4 3.8 %shard_map.109 = bf16[4,512,512]{2,1,0:T(8,128)(2,1)} custom-call(s32[1]{0:T(128)} %bitcast.place_ref, bf16[512,128]{1,0:T(8,128)(2,1)} %pad_maximum_fusion.4.scaled_ref.update_ref, bf16[128,2048]{1,0:T(8,128)(2,1)} %get-tuple-element.38.refs_0_, bf16[128,2048]{1,0:T(8,128)(2,1)} %copy-done.6, bf16[128,2048]{1,0:T(8,128)(2,1)} %copy-done.5, ...), custom_call_target="tpu_custom_call" | custom-call | flops 1 | bytes 1 | tf_op jit(solution)/shard_map/pallas_call | solution.py:99
  129.2 2.2 %fusion.9 = (bf16[1,512,512]{2,1,0:T(8,128)(2,1)S(1)}, bf16[512,512]{1,0:T(8,128)(2,1)}) fusion(bf16[4,512,512]{2,1,0:T(8,128)(2,1)} %shard_map.109), kind=kLoop, calls=%fused_computation.52 | loop fusion | bytes 2097152 | tf_op jit(solution)/shard_map/slice | solution.py:375
  136.4 17.6 %collective-permute-done.11 = bf16[2,128,1152]{2,1,0:T(8,128)(2,1)S(1)} collective-permute-done((bf16[2,128,1152]{2,1,0:T(8,128)(2,1)}, bf16[2,128,1152]{2,1,0:T(8,128)(2,1)S(1)}, u32[]{:S(2)}, u32[]{:S(2)}) %collective-permute-start.11) | collective-permute-done | bytes 589856 | tf_op jit(solution)/shard_map/ppermute | solution.py:24
  162.9 6.5 %shard_map.110 = f32[512,2048]{1,0:T(8,128)} custom-call(s32[32]{0:T(128)} %reshape_reshape.2.tenant_ref, bf16[512,512]{1,0:T(8,128)(2,1)} %get-tuple-element.75.refs_0_, bf16[512,512]{1,0:T(8,128)(2,1)} %get-tuple-element.79.refs_1_, bf16[512,512]{1,0:T(8,128)(2,1)} %get-tuple-element.80.refs_2_, bf16[512,512]{1,0:T(8,128)(2,1)} %get-tuple-element.78.refs_3_), custom_call_target="tpu_custom_call" | custom-call | flops 1 | bytes 1 | tf_op jit(solution)/shard_map/pallas_call | solution.py:99
  169.4 10.8 %collective-permute-done.18 = bf16[256,128]{1,0:T(8,128)(2,1)S(1)} collective-permute-done((bf16[256,128]{1,0:T(8,128)(2,1)S(1)}, bf16[256,128]{1,0:T(8,128)(2,1)S(1)}, u32[]{:S(2)}, u32[]{:S(2)}) %collective-permute-start.18) | collective-permute-done | bytes 65568 | tf_op jit(solution)/shard_map/ppermute | solution.py:24
  194.5 6.1 %shard_map.113 = bf16[128,8192]{1,0:T(8,128)(2,1)} custom-call(s32[1]{0:T(128)} %bitcast.5.line_ref, bf16[128,8192]{1,0:T(8,128)(2,1)} %tokens_ref.3, f32[1,8192]{1,0:T(1,128)} %bitcast.70, f32[128,1]{1,0:T(8,128)} %get-tuple-element.69.inverse_ref, bf16[128,2048]{1,0:T(8,128)(2,1)} %get-tuple-element.53.refs_0_, bf16[128,2048]{1,0:T(8,128)(2,1)} %copy-done.15, ...), custom_call_target="tpu_custom_call" | custom-call | flops 1 | bytes 1 | tf_op jit(solution)/shard_map/pallas_call | solution.py:99
  (126 shorter events, 51.1 us)
Async XLA Ops:
  0.6 21.6 %collective-permute-start.2 = (bf16[128,1024]{1,0:T(8,128)(2,1)}, bf16[128,1024]{1,0:T(8,128)(2,1)S(1)}, u32[]{:S(2)}, u32[]{:S(2)}) collective-permute-start(bf16[128,1024]{1,0:T(8,128)(2,1)} %upstream_ref), channel_id=1, source_target_pairs={{0,8},{4,12},{8,0},{12,4},{1,9},{5,13},{9,1},{13,5},{2,10},{6,14},... | collective-permute-start | bytes 786440 | tf_op jit(solution)/shard_map/ppermute | solution.py:24
  4.7 66.7 %collective-permute-start = (bf16[512,1024]{1,0:T(8,128)(2,1)}, bf16[512,1024]{1,0:T(8,128)(2,1)S(1)}, u32[]{:S(2)}, u32[]{:S(2)}) collective-permute-start(bf16[512,1024]{1,0:T(8,128)(2,1)} %refs_0_.1), channel_id=1, source_target_pairs={{0,2},{2,0},{1,3},{3,1},{4,6},{6,4},{5,7},{7,5},{8,10},{10,8},{9,1... | collective-permute-start | bytes 3145736 | tf_op jit(solution)/shard_map/ppermute | solution.py:28
  21.7 58.8 %copy-start.1 = (bf16[512,1024]{1,0:T(8,128)(2,1)S(1)}, bf16[512,1024]{1,0:T(8,128)(2,1)}, u32[]{:S(2)}) copy-start(bf16[512,1024]{1,0:T(8,128)(2,1)} %refs_0_.1) | copy-start | bytes 3145732
  21.7 50.6 %collective-permute-start.1 = (bf16[2,512,512]{2,1,0:T(8,128)(2,1)}, bf16[2,512,512]{2,1,0:T(8,128)(2,1)}, u32[]{:S(2)}, u32[]{:S(2)}) collective-permute-start(bf16[2,512,512]{2,1,0:T(8,128)(2,1)} %get-tuple-element.40), channel_id=1, source_target_pairs={{0,2},{2,0},{1,3},{3,1},{4,6},{6,4},{5,7},{7,5},{8,10},{10,8},{9,1... | collective-permute-start | bytes 3145736 | tf_op jit(solution)/shard_map/ppermute | solution.py:28
  22.2 50.1 %all-to-all-start = ((bf16[16,64,256]{2,1,0:T(8,128)(2,1)}), bf16[16,64,256]{2,1,0:T(8,128)(2,1)S(1)}, u32[]{:S(2)}, u32[]{:S(2)}) async-start(bf16[16,64,256]{2,1,0:T(8,128)(2,1)} %get-tuple-element.47), calls=%async_computation | async-start | bytes 1048576 | tf_op jit(solution)/shard_map/all_to_all | solution.py:326
  26.4 32.5 %collective-permute-start.5 = (bf16[256,1024]{1,0:T(8,128)(2,1)S(1)}, bf16[256,1024]{1,0:T(8,128)(2,1)S(1)}, u32[]{:S(2)}, u32[]{:S(2)}) collective-permute-start(bf16[256,1024]{1,0:T(8,128)(2,1)S(1)} %constant_dynamic-update-slice_fusion.refs_0_), channel_id=1, source_target_pairs={{0,4},{4,0},{8,12},{12,8},{1,5},{5,1},{9,13},{13,9},{2,6},{6,2},{1... | collective-permute-start | bytes 1572872 | tf_op jit(solution)/shard_map/ppermute | solution.py:24
  28.2 35.8 %collective-permute-start.4 = (bf16[128,2048]{1,0:T(8,128)(2,1)}, bf16[128,2048]{1,0:T(8,128)(2,1)S(1)}, u32[]{:S(2)}, u32[]{:S(2)}) collective-permute-start(bf16[128,2048]{1,0:T(8,128)(2,1)} %get-tuple-element.44), channel_id=1, source_target_pairs={{0,8},{4,12},{8,0},{12,4},{1,9},{5,13},{9,1},{13,5},{2,10},{6,14},... | collective-permute-start | bytes 1572872 | tf_op jit(solution)/shard_map/ppermute | solution.py:24
  30.6 40.8 %collective-permute-start.3 = (bf16[128,2048]{1,0:T(8,128)(2,1)}, bf16[128,2048]{1,0:T(8,128)(2,1)S(1)}, u32[]{:S(2)}, u32[]{:S(2)}) collective-permute-start(bf16[128,2048]{1,0:T(8,128)(2,1)} %get-tuple-element.42), channel_id=1, source_target_pairs={{0,4},{4,0},{8,12},{12,8},{1,5},{5,1},{9,13},{13,9},{2,6},{6,2},{1... | collective-permute-start | bytes 1572872 | tf_op jit(solution)/shard_map/ppermute | solution.py:24
  75.4 4.5 %collective-permute-start.6 = (bf16[256,128]{1,0:T(8,128)(2,1)}, bf16[256,128]{1,0:T(8,128)(2,1)S(1)}, u32[]{:S(2)}, u32[]{:S(2)}) collective-permute-start(bf16[256,128]{1,0:T(8,128)(2,1)} %shard_map.104), channel_id=1, source_target_pairs={{0,4},{4,0},{8,12},{12,8},{1,5},{5,1},{9,13},{13,9},{2,6},{6,2},{1... | collective-permute-start | bytes 196616 | tf_op jit(solution)/shard_map/ppermute | solution.py:24
  82.0 9.7 %collective-permute-start.7 = (bf16[2,512,1024]{2,1,0:T(8,128)(2,1)}, bf16[2,512,1024]{2,1,0:T(8,128)(2,1)}, u32[]{:S(2)}, u32[]{:S(2)}) collective-permute-start(bf16[2,512,1024]{2,1,0:T(8,128)(2,1)} %pad_maximum_fusion), channel_id=1, source_target_pairs={{0,1},{1,0},{2,3},{3,2},{4,5},{5,4},{6,7},{7,6},{8,9},{9,8},{10,11... | collective-permute-start | bytes 6291464 | tf_op jit(solution)/shard_map/ppermute | solution.py:32
  84.3 3.4 %collective-permute-start.8 = (bf16[2,512,512]{2,1,0:T(8,128)(2,1)S(1)}, bf16[2,512,512]{2,1,0:T(8,128)(2,1)S(1)}, u32[]{:S(2)}, u32[]{:S(2)}) collective-permute-start(bf16[2,512,512]{2,1,0:T(8,128)(2,1)S(1)} %pad_maximum_fusion.1), channel_id=1, source_target_pairs={{0,1},{1,0},{2,3},{3,2},{4,5},{5,4},{6,7},{7,6},{8,9},{9,8},{10,11... | collective-permute-start | bytes 3145736 | tf_op jit(solution)/shard_map/ppermute | solution.py:32
  84.8 27.9 %collective-permute-start.9 = (bf16[128,2048]{1,0:T(8,128)(2,1)}, bf16[128,2048]{1,0:T(8,128)(2,1)S(1)}, u32[]{:S(2)}, u32[]{:S(2)}) collective-permute-start(bf16[128,2048]{1,0:T(8,128)(2,1)} %get-tuple-element.56), channel_id=1, source_target_pairs={{0,12},{4,8},{8,4},{12,0},{1,13},{5,9},{9,5},{13,1},{2,14},{6,10},... | collective-permute-start | bytes 1572872 | tf_op jit(solution)/shard_map/ppermute | solution.py:24
  107.5 14.9 %collective-permute-start.10 = (bf16[64,2048]{1,0:T(8,128)(2,1)S(1)}, bf16[64,2048]{1,0:T(8,128)(2,1)S(1)}, u32[]{:S(2)}, u32[]{:S(2)}) collective-permute-start(bf16[64,2048]{1,0:T(8,128)(2,1)S(1)} %get-tuple-element.91), channel_id=1, source_target_pairs={{0,8},{4,12},{8,0},{12,4},{1,9},{5,13},{9,1},{13,5},{2,10},{6,14},... | collective-permute-start | bytes 786440 | tf_op jit(solution)/shard_map/ppermute | solution.py:24
  122.3 14.0 %collective-permute-start.13 = (bf16[64,2048]{1,0:T(8,128)(2,1)S(1)}, bf16[64,2048]{1,0:T(8,128)(2,1)S(1)}, u32[]{:S(2)}, u32[]{:S(2)}) collective-permute-start(bf16[64,2048]{1,0:T(8,128)(2,1)S(1)} %get-tuple-element.62), channel_id=1, source_target_pairs={{0,8},{4,12},{8,0},{12,4},{1,9},{5,13},{9,1},{13,5},{2,10},{6,14},... | collective-permute-start | bytes 786440 | tf_op jit(solution)/shard_map/ppermute | solution.py:24
  122.3 31.6 %collective-permute-start.11 = (bf16[2,128,1152]{2,1,0:T(8,128)(2,1)}, bf16[2,128,1152]{2,1,0:T(8,128)(2,1)S(1)}, u32[]{:S(2)}, u32[]{:S(2)}) collective-permute-start(bf16[2,128,1152]{2,1,0:T(8,128)(2,1)} %get-tuple-element.60), channel_id=1, source_target_pairs={{0,4},{4,0},{8,12},{12,8},{1,5},{5,1},{9,13},{13,9},{2,6},{6,2},{1... | collective-permute-start | bytes 1769480 | tf_op jit(solution)/shard_map/ppermute | solution.py:24
  131.4 37.9 %collective-permute-start.17 = (bf16[128,2048]{1,0:T(8,128)(2,1)}, bf16[128,2048]{1,0:T(8,128)(2,1)S(1)}, u32[]{:S(2)}, u32[]{:S(2)}) collective-permute-start(bf16[128,2048]{1,0:T(8,128)(2,1)} %get-tuple-element.67), channel_id=1, source_target_pairs={{0,12},{4,8},{8,4},{12,0},{1,13},{5,9},{9,5},{13,1},{2,14},{6,10},... | collective-permute-start | bytes 1572872 | tf_op jit(solution)/shard_map/ppermute | solution.py:24
  132.9 24.3 %collective-permute-start.15 = (bf16[2,512,512]{2,1,0:T(8,128)(2,1)S(1)}, bf16[2,512,512]{2,1,0:T(8,128)(2,1)S(1)}, u32[]{:S(2)}, u32[]{:S(2)}) collective-permute-start(bf16[2,512,512]{2,1,0:T(8,128)(2,1)S(1)} %slice.201), channel_id=1, source_target_pairs={{0,2},{2,0},{1,3},{3,1},{4,6},{6,4},{5,7},{7,5},{8,10},{10,8},{9,1... | collective-permute-start | bytes 3145736 | tf_op jit(solution)/shard_map/ppermute | solution.py:28
  154.2 7.3 %collective-permute-start.14 = (bf16[2,128,128]{2,1,0:T(8,128)(2,1)S(1)}, bf16[2,128,128]{2,1,0:T(8,128)(2,1)S(1)}, u32[]{:S(2)}, u32[]{:S(2)}) collective-permute-start(bf16[2,128,128]{2,1,0:T(8,128)(2,1)S(1)} %pad_maximum_fusion.7), channel_id=1, source_target_pairs={{0,8},{4,12},{8,0},{12,4},{1,9},{5,13},{9,1},{13,5},{2,10},{6,14},... | collective-permute-start | bytes 196616 | tf_op jit(solution)/shard_map/ppermute | solution.py:24
  158.1 3.7 %collective-permute-start.16 = (bf16[2,512,512]{2,1,0:T(8,128)(2,1)S(1)}, bf16[2,512,512]{2,1,0:T(8,128)(2,1)S(1)}, u32[]{:S(2)}, u32[]{:S(2)}) collective-permute-start(bf16[2,512,512]{2,1,0:T(8,128)(2,1)S(1)} %pad_maximum_fusion.2), channel_id=1, source_target_pairs={{0,1},{1,0},{2,3},{3,2},{4,5},{5,4},{6,7},{7,6},{8,9},{9,8},{10,11... | collective-permute-start | bytes 3145736 | tf_op jit(solution)/shard_map/ppermute | solution.py:32
  158.4 31.3 %collective-permute-start.12 = (bf16[128,1024]{1,0:T(8,128)(2,1)S(1)}, bf16[128,1024]{1,0:T(8,128)(2,1)S(1)}, u32[]{:S(2)}, u32[]{:S(2)}) collective-permute-start(bf16[128,1024]{1,0:T(8,128)(2,1)S(1)} %fusion.3), channel_id=1, source_target_pairs={{0,8},{4,12},{8,0},{12,4},{1,9},{5,13},{9,1},{13,5},{2,10},{6,14},... | collective-permute-start | bytes 786440 | tf_op jit(solution)/shard_map/ppermute | solution.py:24
  159.1 34.6 %collective-permute-start.21 = (bf16[128,2048]{1,0:T(8,128)(2,1)S(1)}, bf16[128,2048]{1,0:T(8,128)(2,1)S(1)}, u32[]{:S(2)}, u32[]{:S(2)}) collective-permute-start(bf16[128,2048]{1,0:T(8,128)(2,1)S(1)} %copy-done.18), channel_id=1, source_target_pairs={{0,4},{4,0},{8,12},{12,8},{1,5},{5,1},{9,13},{13,9},{2,6},{6,2},{1... | collective-permute-start | bytes 1572872 | tf_op jit(solution)/shard_map/ppermute | solution.py:24
  169.3 10.8 %collective-permute-start.18 = (bf16[256,128]{1,0:T(8,128)(2,1)S(1)}, bf16[256,128]{1,0:T(8,128)(2,1)S(1)}, u32[]{:S(2)}, u32[]{:S(2)}) collective-permute-start(bf16[256,128]{1,0:T(8,128)(2,1)S(1)} %bitcast.67), channel_id=1, source_target_pairs={{0,4},{4,0},{8,12},{12,8},{1,5},{5,1},{9,13},{13,9},{2,6},{6,2},{1... | collective-permute-start | bytes 196616 | tf_op jit(solution)/shard_map/ppermute | solution.py:24
  183.9 5.0 %collective-permute-start.19 = (bf16[2,64,512]{2,1,0:T(8,128)(2,1)S(1)}, bf16[2,64,512]{2,1,0:T(8,128)(2,1)S(1)}, u32[]{:S(2)}, u32[]{:S(2)}) collective-permute-start(bf16[2,64,512]{2,1,0:T(8,128)(2,1)S(1)} %slice.210), channel_id=1, source_target_pairs={{0,2},{2,0},{1,3},{3,1},{4,6},{6,4},{5,7},{7,5},{8,10},{10,8},{9,1... | collective-permute-start | bytes 393224 | tf_op jit(solution)/shard_map/ppermute | solution.py:28
  189.6 1.4 collective-permute-start.20
  (18 other events, 198.3 us)

commit v4 on v3

v4 whole, which is shorter than its diff:
```python
import functools

import jax
import jax.numpy as jnp
from jax import lax
from jax.experimental import pallas as pl
from jax.experimental.pallas import tpu as pltpu
from jax.sharding import Mesh
from jax.sharding import PartitionSpec as P

RANK = 64
BLK = 64
PAIR = 2 * RANK

adapter_scale = 0.5
norm_eps = 1e-05

QUICK = pl.CostEstimate(flops=1, bytes_accessed=1, transcendentals=0)
MIB = 1024 * 1024


def over_line(value, mask):
    size = lax.axis_size("line")
    return lax.ppermute(value, "line", [(i, i ^ mask) for i in range(size)])


def over_pair(value):
    return lax.ppermute(value, "pair", [(0, 1), (1, 0)])


def over_cores(value):
    return lax.ppermute(value, "core", [(0, 1), (1, 0)])


def after(value, *others):
    return lax.optimization_barrier((value,) + others)[0]


def order_kernel(place_ref, mine_ref, beside_ref, across_ref, corner_ref, out_ref):
    for r, ref in enumerate((mine_ref, beside_ref, across_ref, corner_ref)):
        out_ref[place_ref[0] ^ r] = ref[...] if len(ref.shape) == 2 else ref[0]


def in_order(parts, place):
    rows, width = parts[0].shape
    shape = jax.ShapeDtypeStruct((4, rows, width), parts[0].dtype)
    return call(order_kernel, shape, [place.reshape(1)], parts).reshape(4 * rows, width)


def gather_line(held):
    size = lax.axis_size("line")
    pieces, slots, step = [(held, [0, size // 2])], [0, size // 2], size // 4
    while step:
        arrived = over_line(held, step)
        more = [s ^ step for s in slots]
        pieces.append((arrived, more))
        slots, step = slots + more, step // 2
        held = jnp.concatenate([held, arrived]) if step else held
    return pieces


def in_slots(pieces):
    rows = pieces[0][0].shape[0] // 2
    found = {m: p[i * rows : (i + 1) * rows] for p, ms in pieces for i, m in enumerate(ms)}
    return jnp.concatenate([found[m] for m in range(len(found))])


def two_terms(low):
    high = lax.reduce_precision(low, 8, 7)
    return jnp.concatenate([high, low - high], axis=-1).astype(jnp.bfloat16)


def one_term(sent):
    sent = sent.astype(jnp.float32)
    return sent[..., :RANK] + sent[..., RANK:]


def adapter_columns(adapter):
    return pl.ds(pl.multiple_of((adapter // 2) * PAIR, PAIR), PAIR)


def adapter_half(both, adapter):
    return jnp.where(adapter % 2 == 0, both[:, :RANK], both[:, RANK:])


def on_diagonal(update):
    row = lax.broadcasted_iota(jnp.int32, update.shape, 0) // BLK
    column = lax.broadcasted_iota(jnp.int32, update.shape, 1) // RANK
    return jnp.where(row == column, update, jnp.zeros_like(update))


def grouped(refs, counts):
    refs = iter(refs)
    return [[next(refs) for _ in range(n)] for n in counts]


def whole(parts):
    return parts[0][...] if len(parts) == 1 else jnp.concatenate([p[...] for p in parts], axis=0)


def flat(slots):
    return [part for parts in slots for part in parts]


def call(kernel, out_shape, scalars, arrays, limit=60, scratch=()):
    vmem, smem = pl.BlockSpec(memory_space=pltpu.VMEM), pl.BlockSpec(memory_space=pltpu.SMEM)
    return pl.pallas_call(
        kernel,
        out_shape=out_shape,
        in_specs=[smem] * len(scalars) + [vmem] * len(arrays),
        out_specs=jax.tree.map(lambda _: vmem, out_shape),
        scratch_shapes=scratch,
        cost_estimate=QUICK,
        compiler_params=pltpu.CompilerParams(vmem_limit_bytes=limit * MIB),
    )(*scalars, *arrays)


def first_kernel(counts, wanted, line_ref, tenant_ref, tokens_ref, gain_ref, up_ref, table_ref, inverse_ref, *refs):
    slots = len(counts)
    for d, devices_blocks in enumerate(wanted):
        write_columns([tenant_ref[b] for b in devices_blocks], up_ref, table_ref.at[d])
    features = tokens_ref.shape[1]
    width = features // slots
    total = jnp.zeros(inverse_ref.shape, jnp.float32)
    for s in range(slots):
        wide = tokens_ref[:, s * width : (s + 1) * width].astype(jnp.float32)
        total += jnp.sum(wide * wide, axis=1, keepdims=True)
    inverse = lax.rsqrt(total / features + norm_eps)
    inverse_ref[...] = inverse
    for s in range(slots):
        columns = pl.ds(pl.multiple_of((line_ref[0] ^ s) * width, width), width)
        wide = tokens_ref[:, columns].astype(jnp.float32)
        normed = (wide * inverse * gain_ref[:, columns]).astype(jnp.bfloat16)
        for part, ref in enumerate(grouped(refs, counts)[s]):
            ref[...] = normed[part * ref.shape[0] : (part + 1) * ref.shape[0]]


def parted(counts, rows, width):
    return [jax.ShapeDtypeStruct((rows // n, width), jnp.bfloat16) for n in counts for _ in range(n)]


def norm_and_up(line, tenant, tokens, gain, up_factor, counts, wanted):
    rows, features = tokens.shape
    shapes = [
        jax.ShapeDtypeStruct((len(wanted), up_factor.shape[0], len(wanted[0]) * RANK), up_factor.dtype),
        jax.ShapeDtypeStruct((rows, 1), jnp.float32),
    ] + parted(counts, rows, features // len(counts))
    table, inverse, *normed = call(
        functools.partial(first_kernel, counts, wanted), shapes, [line, tenant], [tokens, gain, up_factor]
    )
    return table, inverse, grouped(normed, counts)


def write_columns(adapters, factor_ref, out_ref):
    for first in range(0, len(adapters), 2):
        parts = [adapter_half(factor_ref[:, adapter_columns(a)], a) for a in adapters[first : first + 2]]
        out_ref[:, first * RANK : first * RANK + PAIR] = jnp.concatenate(parts, axis=1)


def class_adapters(place_ref, tenant_ref, size, blocks, r):
    devices = [(place_ref[0] ^ s) * 4 + (place_ref[1] ^ r) for s in range(size)]
    return [tenant_ref[d * blocks + b] for d in devices for b in range(blocks)]


def down_kernel(size, blocks, place_ref, tenant_ref, factor_ref, mine_ref, core_ref, pair_ref):
    for r, ref in enumerate((mine_ref, core_ref, pair_ref.at[0], pair_ref.at[1])):
        write_columns(class_adapters(place_ref, tenant_ref, size, blocks, r), factor_ref, ref)


def down_columns(place, tenant, down_factor, size, blocks):
    shape = (down_factor.shape[0], size * blocks * RANK)
    shapes = [jax.ShapeDtypeStruct(lead + shape, down_factor.dtype) for lead in ((), (), (2,))]
    return call(functools.partial(down_kernel, size, blocks), shapes, [place, tenant], [down_factor])


def scaled_kernel(upstream_ref, far_ref, up_ref, out_ref):
    rows = upstream_ref.shape[0]
    for which, ref in enumerate((upstream_ref, far_ref)):
        mixed = jnp.dot(ref[...], up_ref[...], preferred_element_type=jnp.float32)
        for b in range(rows // BLK):
            at = which * rows + b * BLK
            block = mixed[b * BLK : (b + 1) * BLK, at // BLK * RANK : (at // BLK + 1) * RANK]
            scaled = (adapter_scale * block).astype(out_ref.dtype)
            out_ref[at : at + BLK, :] = jnp.concatenate([scaled, scaled], axis=1)


def back_kernel(pieces, counts, rows, weight_ref, down_ref, scaled_ref, *refs):
    upstream_refs, out_refs = refs[: len(pieces)], grouped(refs[len(pieces) :], counts)
    contract = (((1,), (1,)), ((), ()))
    for upstream_ref, slots in zip(upstream_refs, pieces):
        product = lax.dot_general(
            upstream_ref[...], weight_ref[...], contract, preferred_element_type=jnp.float32
        )
        for at, slot in enumerate(slots):
            for r in range(0, rows, 2 * BLK):
                first, held = at * rows + r, slot * rows + r
                column = held // BLK * RANK
                term = lax.dot_general(
                    on_diagonal(scaled_ref[held : held + 2 * BLK, :]),
                    down_ref[:, column : column + PAIR],
                    contract,
                    preferred_element_type=jnp.float32,
                )
                back = (product[first : first + 2 * BLK] + term).astype(jnp.bfloat16)
                part = rows // counts[slot]
                step = min(part, 2 * BLK)
                for at_row in range(r, r + 2 * BLK, step):
                    inside = at_row % part
                    out_refs[slot][at_row // part][inside : inside + step, :] = back[at_row - r : at_row - r + step]


def value_kernel(counts, weight_ref, down_ref, *refs):
    normed_refs, (values_ref, low_ref, sent_ref) = grouped(refs[:-3], counts), refs[-3:]
    value_width = weight_ref.shape[1]
    for slot, parts in enumerate(normed_refs):
        normed = whole(parts)
        rows = normed.shape[0]
        values = jnp.dot(normed, weight_ref[...], preferred_element_type=jnp.float32)
        low = []
        for b in range(rows // BLK):
            column = (slot * rows // BLK + b) // 2 * PAIR
            both = jnp.dot(
                normed[b * BLK : (b + 1) * BLK],
                down_ref[:, column : column + PAIR],
                preferred_element_type=jnp.float32,
            )
            low.append(both[:, b % 2 * RANK : (b % 2 + 1) * RANK])
        low = jnp.concatenate(low, axis=0)
        if slot % 2:
            high = low.astype(jnp.bfloat16)
            rest = (low - high.astype(jnp.float32)).astype(jnp.bfloat16)
            sent_ref[slot // 2, :, :value_width] = values.astype(jnp.bfloat16)
            sent_ref[slot // 2, :, value_width:] = jnp.concatenate([high, rest], axis=1)
        else:
            values_ref[slot // 2] = values
            low_ref[slot // 2] = low


def value_products(weight, down, normed):
    rows, half, value_width = normed[0][0].shape[0], len(normed) // 2, weight.shape[1]
    shapes = [
        jax.ShapeDtypeStruct((half, rows, value_width), jnp.float32),
        jax.ShapeDtypeStruct((half, rows, RANK), jnp.float32),
        jax.ShapeDtypeStruct((half, rows, value_width + PAIR), jnp.bfloat16),
    ]
    counts = [len(parts) for parts in normed]
    return call(functools.partial(value_kernel, counts), shapes, [], [weight, down, *flat(normed)])


def sum_over_line(values, low, crossed, meanwhile):
    value_width, far, step = values.shape[-1], lax.axis_size("line") // 2, 2
    values = values + crossed[..., :value_width].astype(jnp.float32)
    low = low + one_term(crossed[..., value_width:])
    while step < far:
        low = low[::2] + one_term(over_line(two_terms(low[1::2]), step))
        values = values[::2] + over_line(values[1::2].astype(jnp.bfloat16), step).astype(jnp.float32)
        step *= 2
    return values, low + one_term(after(over_line(two_terms(low), far), meanwhile))[::-1]


def terms_kernel(counts, scale, place_ref, update_ref, *refs):
    rows_refs, (mine_ref, core_ref, pair_ref, scratch) = grouped(refs[:-4], counts), refs[-4:]
    rows, width = rows_refs[0][0].shape
    shard = width // 4
    for slot, parts in enumerate(rows_refs):
        held = whole(parts)
        for r in range(0, rows, 2 * BLK):
            first = slot * rows + r
            term = scale * lax.dot_general(
                held[r : r + 2 * BLK, :],
                on_diagonal(update_ref[first : first + 2 * BLK, :]),
                (((0,), (0,)), ((), ())),
                preferred_element_type=jnp.float32,
            )
            for p in range(4):
                scratch[p] = term[p * shard : (p + 1) * shard]
            columns = slice(first // BLK * RANK, first // BLK * RANK + PAIR)
            for r4, ref in enumerate((mine_ref, core_ref, pair_ref.at[0], pair_ref.at[1])):
                ref[:, columns] = scratch[place_ref[1] ^ r4].astype(jnp.bfloat16)


def factor_terms(place, update, rows, scale):
    count, width = rows[0][0].shape
    shape = (width // 4, len(rows) * count // BLK * RANK)
    counts = [len(parts) for parts in rows]
    return call(
        functools.partial(terms_kernel, counts, scale),
        [jax.ShapeDtypeStruct(lead + shape, jnp.bfloat16) for lead in ((), (), (2,))],
        [place],
        [update, *flat(rows)],
        scratch=[pltpu.VMEM((4, width // 4, PAIR), jnp.float32)],
    )


def owner_kernel(size, blocks, place_ref, tenant_ref, *refs):
    out_ref = refs[-1]
    out_ref[...] = jnp.zeros_like(out_ref)
    lane = lax.broadcasted_iota(jnp.int32, (out_ref.shape[0], PAIR), 1) // RANK
    for r, terms_ref in enumerate(refs[:-1]):
        adapters = class_adapters(place_ref, tenant_ref, size, blocks, r)
        for first in range(0, len(adapters), 2):
            columns = slice(first * RANK, first * RANK + PAIR)
            both = terms_ref[:, columns] if len(terms_ref.shape) == 2 else terms_ref[0, :, columns]
            both = both.astype(jnp.float32)
            turned = jnp.concatenate([both[:, RANK:], both[:, :RANK]], axis=1)
            for h, adapter in enumerate(adapters[first : first + 2]):
                side = adapter % 2
                term = jnp.where(side == h, both, turned)
                out_ref[:, adapter_columns(adapter)] += jnp.where(lane == side, term, jnp.zeros_like(term))


def owner_sums(place, tenant, size, terms, width):
    blocks = terms[0].shape[1] // RANK // size
    shape = jax.ShapeDtypeStruct((terms[0].shape[0], width), jnp.float32)
    return call(functools.partial(owner_kernel, size, blocks), shape, [place, tenant], terms)


def token_grad_kernel(counts, line_ref, tokens_ref, gain_ref, inverse_ref, *refs):
    back_refs, out_ref = grouped(refs[:-1], counts), refs[-1]
    slots, width = len(counts), back_refs[0][0].shape[1]
    inverse = inverse_ref[...]
    total = jnp.zeros_like(inverse)

    def load(s):
        columns = pl.ds(pl.multiple_of((line_ref[0] ^ s) * width, width), width)
        gained = gain_ref[:, columns] * whole(back_refs[s]).astype(jnp.float32)
        return columns, gained, tokens_ref[:, columns].astype(jnp.float32)

    for s in range(slots):
        _, gained, wide = load(s)
        total += jnp.sum(gained * wide, axis=1, keepdims=True)
    cubed = inverse * inverse * inverse
    inner = total / tokens_ref.shape[1]
    for s in range(slots):
        columns, gained, wide = load(s)
        out_ref[:, columns] = (inverse * gained - wide * cubed * inner).astype(out_ref.dtype)


def on_device(tokens, upstream, norm_gain, value_weight, down_factor, up_factor, tenant):
    size, far = lax.axis_size("line"), lax.axis_size("line") // 2
    line, pair, core = lax.axis_index("line"), lax.axis_index("pair"), lax.axis_index("core")
    place = 2 * pair + core
    line_, place_ = line.reshape(1), jnp.stack([line, place])
    rows = tokens.shape[0]
    blocks = rows // BLK
    value_width = upstream.shape[1]
    adapter_width = down_factor.shape[1]
    value_rows = up_factor.shape[0]
    gain = norm_gain.reshape(1, -1)

    upstream_far = over_line(upstream, far)

    wanted = [
        [e * blocks + b for e in (d, d ^ (4 * far)) for b in range(blocks)] for d in range(4 * size)
    ]
    counts = [1] * size
    up_sent, inverse, normed = norm_and_up(line_, tenant, tokens, gain, up_factor, counts, wanted)
    crossed_far = over_line(after(normed[far][0], upstream_far), far)

    up_mine = lax.all_to_all(
        after(up_sent, upstream_far, over_cores(inverse)), ("line", "pair", "core"), split_axis=0, concat_axis=0, tiled=True
    )
    up_mine = up_mine.reshape(value_width, 2 * blocks * RANK)

    pieces = gather_line(jnp.concatenate([upstream, upstream_far]))
    across = over_pair(value_weight)
    down_mine, down_core, down_pair = down_columns(
        place_, tenant, after(down_factor, normed[0][0]), size, blocks
    )
    down_crossed = over_pair(down_pair)

    scaled = call(
        scaled_kernel,
        jax.ShapeDtypeStruct((2 * rows, PAIR), jnp.bfloat16),
        [],
        [after(upstream, crossed_far, across, down_crossed, *[p for p, _ in pieces]), upstream_far, up_mine],
    )
    across, down_crossed, down_core, weight_mine, scaled = lax.optimization_barrier(
        (across, down_crossed, down_core, value_weight, scaled)
    )
    weight = in_order([weight_mine, over_cores(weight_mine), across, over_cores(across)], place)
    down = in_order([down_mine, over_cores(down_core), down_crossed, over_cores(down_crossed[1])], place)
    scaled = in_slots(gather_line(scaled))
    arrived = [normed[0]] + [[over_line(after(normed[s][0], scaled), s)] for s in range(1, size)]
    arrived[far] = [crossed_far]

    counts = [1] * far + [2] + [1] * (far - 1)
    back = call(
        functools.partial(back_kernel, [s for _, s in pieces], counts, rows),
        parted(counts, rows, weight.shape[0]),
        [],
        [weight, down, scaled] + [p for p, _ in pieces],
    )
    back = grouped(back, counts)
    first = over_line(back[far][0], far)

    terms = factor_terms(place_, after(scaled, back[0][0]), arrived, 1.0)
    values, low, sent = value_products(after(weight, terms[0]), down, arrived)
    back_mine = [back[0]] + [[over_line(back[s][0], s)] for s in range(1, far)]
    crossed = over_line(after(sent, first, *flat(back_mine)), 1)
    back_mine += [[first, over_line(after(back[far][1], first), far)]]

    crossed_terms = over_pair(terms[2])
    terms = [terms[0], over_cores(terms[1]), crossed_terms, over_cores(crossed_terms[1])]
    grad_down = owner_sums(place_, tenant, size, terms, adapter_width)

    values, low = sum_over_line(values, low, crossed, grad_down)
    low = low.astype(jnp.bfloat16)
    back_mine += [[over_line(after(back[s][0], crossed), s)] for s in range(far + 1, size)]
    last = over_line(after(values[1].astype(jnp.bfloat16), low), far)
    values = values[0] + last.astype(jnp.float32)
    columns = [
        (lax.dynamic_slice_in_dim(p, line * 4 * value_rows, 4 * value_rows, 1), s)
        for p, s in pieces
    ]
    low_held = jnp.concatenate([low, low], axis=-1).reshape(2 * rows, PAIR)
    low_all = after(in_slots(gather_line(low_held)), *flat(back_mine[far + 1 :]))
    terms = factor_terms(place_, low_all, [[in_slots(columns)]], adapter_scale)
    crossed_terms = over_pair(terms[2])
    grad_tokens = call(
        functools.partial(token_grad_kernel, counts),
        jax.ShapeDtypeStruct(tokens.shape, tokens.dtype),
        [line_],
        [tokens, gain, after(inverse, terms[0]), *flat(back_mine)],
        32,
    )
    crossed_terms = after(crossed_terms, grad_tokens, last)
    terms = [terms[0], over_cores(terms[1]), crossed_terms, over_cores(crossed_terms[1])]
    grad_up = owner_sums(place_, tenant, size, terms, adapter_width)

    adapter_branch = jnp.einsum(
        "bkr,vbr->bkv",
        low[0].reshape(blocks, BLK, RANK),
        up_mine[:, : blocks * RANK].reshape(value_width, blocks, RANK),
        preferred_element_type=jnp.float32,
    ).reshape(rows, value_width)
    adapted_values = (values + adapter_scale * adapter_branch).astype(jnp.bfloat16)

    return (adapted_values, grad_tokens, grad_down, grad_up)


def solution(mesh):
    groups, shards = mesh.shape["groups"], mesh.shape["fsdp"]
    line_mesh = Mesh(mesh.devices.reshape(groups, shards // 4, 2, 2), ("groups", "line", "pair", "core"))
    own = ("line", "pair", "core")
    everywhere = P(("groups",) + own, None)
    in_specs = (everywhere, everywhere, P(), P(own, None), P(own, None), P(own, None), P("groups"))
    out_specs = (everywhere,) * 4
    return jax.shard_map(
        on_device, mesh=line_mesh, in_specs=in_specs, out_specs=out_specs, check_vma=False
    )
```

time: 202 us -> 187 us (0.926)
  local copies, waits for them, and re-layouts: 25 us -> 10.2 us
  waiting for transfers between devices: 80.9 us -> 71.9 us
  other arithmetic: 5.14 us -> 8.88 us
  starting transfers between devices: 31.3 us -> 34.3 us
    squeeze x7 -> x3, local copies, waits for them, and re-layouts: 9.45 us -> 0.07 us  [the longest x2 0.04 us: on_device(): crossed_terms[1]]
    slice x5 -> x0, local copies, waits for them, and re-layouts: 5.82 us -> none  [the longest x4 4.7 us: on_device(): terms = swap_rest(terms[0], terms[1], over_pair(terms[2:]))]
    ppermute x14, waiting for transfers between devices: 75.9 us -> 71.9 us  [over_line(): return lax.ppermute(value, 'line', [(i, i ^ mask) for i in range(size)])]
    ppermute x4, waiting for transfers between devices: 3.98 us -> 0.01 us  [over_pair(): return lax.ppermute(value, 'pair', [(0, 1), (1, 0)])]
    ppermute x14, starting transfers between devices: 21.5 us -> 24.8 us  [over_line(): return lax.ppermute(value, 'line', [(i, i ^ mask) for i in range(size)])]
    unnamed x40 -> x59, local copies, waits for them, and re-layouts: 4 us -> 5.81 us
  transfers between devices with their start and end apart: 23 -> 27, of which waited for: 13 -> 8; matrix products, arithmetic and copies ran while one was open for 12% -> 8% of each run, Pallas kernels for 24% -> 26%
where the time goes in v4:
time: 187 us; the launch traced here: 184 us
  waiting for transfers between devices  71.9 us (38%)
  Pallas kernels  56.5 us (30%)
  starting transfers between devices  34.3 us (18%)
  local copies, waits for them, and re-layouts  10.2 us (5%)
  other arithmetic  8.88 us (5%)
    ppermute x14, waiting for transfers between devices, over_line(): return lax.ppermute(value, 'line', [(i, i ^ mask) for i in range(size)])  71.9 us
    pallas_call x12, Pallas kernels, call(): pl.pallas_call(kernel, out_shape=out_shape, in_specs=[smem] * len(scalars...  56.5 us
    ppermute x14, starting transfers between devices, over_line(): return lax.ppermute(value, 'line', [(i, i ^ mask) for i in range(size)])  24.8 us
    unnamed x59, local copies, waits for them, and re-layouts  5.81 us
    all_to_all x1, starting transfers between devices, on_device(): lax.all_to_all(after(up_sent, upstream_far, over_cores(inverse)), ('line'...  4.09 us
    ppermute x4, starting transfers between devices, over_pair(): return lax.ppermute(value, 'pair', [(0, 1), (1, 0)])  4 us
  transfers between devices with their start and end apart: 27, of which 8 were waited for; matrix products, arithmetic and copies ran while one was open for 8% of the time, Pallas kernels for 26%

profile of v4, /device:TPU:0, one launch (start us, length us, event | category | flops | bytes accessed | tf_op | source)
XLA Modules:
  0.0 184.0 jit_solution(18103502419056421269)
XLA Ops:
  0.6 4.1 %collective-permute-start.2 = (bf16[128,1024]{1,0:T(8,128)(2,1)}, bf16[128,1024]{1,0:T(8,128)(2,1)S(1)}, u32[]{:S(2)}, u32[]{:S(2)}) collective-permute-start(bf16[128,1024]{1,0:T(8,128)(2,1)} %upstream_ref), channel_id=1, source_target_pairs={{0,8},{4,12},{8,0},{12,4},{1,9},{5,13},{9,1},{13,5},{2,10},{6,14},... | collective-permute-start | bytes 786440 | tf_op jit(solution)/shard_map/ppermute | solution.py:24
  6.3 6.3 %shard_map.102 = (bf16[16,64,256]{2,1,0:T(8,128)(2,1)}, f32[128,1]{1,0:T(8,128)}, bf16[128,2048]{1,0:T(8,128)(2,1)}, bf16[128,2048]{1,0:T(8,128)(2,1)}, bf16[128...) custom-call(s32[1]{0:T(128)} %bitcast.1.line_ref, s32[32]{0:T(128)} %tenant_ref.7, bf16[128,8192]{1,0:T(8,128)(2,1)} %tokens_ref.3, ...), custom_call_target="tpu_custom_call" | custom-call | flops 1 | bytes 1 | tf_op jit(solution)/shard_map/pallas_call | solution.py:107
  13.1 6.3 %shard_map.103 = (bf16[512,512]{1,0:T(8,128)(2,1)}, bf16[512,512]{1,0:T(8,128)(2,1)}, bf16[2,512,512]{2,1,0:T(8,128)(2,1)}) custom-call(s32[2]{0:T(128)} %pad_add_fusion.place_ref, s32[32]{0:T(128)} %tenant_ref.7, bf16[512,2048]{1,0:T(8,128)(2,1)} %factor_ref), custom_call_target="tpu_custom_call" | custom-call | flops 1 | bytes 1 | tf_op jit(solution)/shard_map/pallas_call | solution.py:107
  20.0 4.1 %all-to-all-start = ((bf16[16,64,256]{2,1,0:T(8,128)(2,1)}), bf16[16,64,256]{2,1,0:T(8,128)(2,1)S(1)}, u32[]{:S(2)}, u32[]{:S(2)}) async-start(bf16[16,64,256]{2,1,0:T(8,128)(2,1)} %get-tuple-element.56), calls=%async_computation | async-start | bytes 1048576 | tf_op jit(solution)/shard_map/all_to_all | solution.py:360
  25.9 2.4 %collective-permute-start.3 = (bf16[128,2048]{1,0:T(8,128)(2,1)S(1)}, bf16[128,2048]{1,0:T(8,128)(2,1)S(1)}, u32[]{:S(2)}, u32[]{:S(2)}) collective-permute-start(bf16[128,2048]{1,0:T(8,128)(2,1)S(1)} %copy-done.27), channel_id=1, source_target_pairs={{0,8},{4,12},{8,0},{12,4},{1,9},{5,13},{9,1},{13,5},{2,10},{6,14},... | collective-permute-start | bytes 1572872 | tf_op jit(solution)/shard_map/ppermute | solution.py:24
  28.3 27.8 %collective-permute-done.4.refs_1_ = bf16[256,1024]{1,0:T(8,128)(2,1)S(1)} collective-permute-done((bf16[256,1024]{1,0:T(8,128)(2,1)S(1)}, bf16[256,1024]{1,0:T(8,128)(2,1)S(1)}, u32[]{:S(2)}, u32[]{:S(2)}) %collective-permute-start.4) | collective-permute-done | bytes 524320 | tf_op jit(solution)/shard_map/ppermute | solution.py:24
  56.2 5.5 %collective-permute-done.3.refs_2_ = bf16[128,2048]{1,0:T(8,128)(2,1)S(1)} collective-permute-done((bf16[128,2048]{1,0:T(8,128)(2,1)S(1)}, bf16[128,2048]{1,0:T(8,128)(2,1)S(1)}, u32[]{:S(2)}, u32[]{:S(2)}) %collective-permute-start.3) | collective-permute-done | bytes 524320 | tf_op jit(solution)/shard_map/ppermute | solution.py:24
  62.6 2.2 %shard_map.104 = bf16[256,128]{1,0:T(8,128)(2,1)} custom-call(bf16[128,1024]{1,0:T(8,128)(2,1)} %upstream_ref, bf16[128,1024]{1,0:T(8,128)(2,1)} %copy-done.17, bf16[1024,256]{1,0:T(8,128)(2,1)} %bitcast.39), custom_call_target="tpu_custom_call" | custom-call | flops 1 | bytes 1 | tf_op jit(solution)/shard_map/pallas_call | solution.py:107
  66.7 2.6 %collective-permute-done.7 = bf16[256,128]{1,0:T(8,128)(2,1)S(1)} collective-permute-done((bf16[256,128]{1,0:T(8,128)(2,1)}, bf16[256,128]{1,0:T(8,128)(2,1)S(1)}, u32[]{:S(2)}, u32[]{:S(2)}) %collective-permute-start.7) | collective-permute-done | bytes 65568 | tf_op jit(solution)/shard_map/ppermute | solution.py:24
  72.3 3.1 %shard_map.106 = bf16[4,512,512]{2,1,0:T(8,128)(2,1)} custom-call(s32[1]{0:T(128)} %bitcast.place_ref, bf16[512,512]{1,0:T(8,128)(2,1)} %get-tuple-element.60.mine_ref, bf16[512,512]{1,0:T(8,128)(2,1)} %collective-permute-done.8.beside_ref, bf16[2,512,512]{2,1,0:T(8,128)(2,1)} %copy-done.8, bf16[512,512]{1,0:T(8,128)(2,1)} %copy-done.21), custom_call_target="tpu_custom_call" | custom-call | flops 1 | bytes 1 | tf_op jit(solution)/shard_map/pallas_call | solution.py:107
  76.4 4.5 %shard_map.105 = bf16[4,512,1024]{2,1,0:T(8,128)(2,1)} custom-call(s32[1]{0:T(128)} %bitcast.place_ref, bf16[512,1024]{1,0:T(8,128)(2,1)} %mine_ref, bf16[512,1024]{1,0:T(8,128)(2,1)} %copy-done.15, bf16[512,1024]{1,0:T(8,128)(2,1)} %collective-permute-done.across_ref, bf16[512,1024]{1,0:T(8,128)(2,1)} %collective-permute-done.6.corner_ref), custom_call_target="tpu_custom_call" | custom-call | flops 1 | bytes 1 | tf_op jit(solution)/shard_map/pallas_call | solution.py:107
  80.8 6.9 %shard_map.107 = (bf16[128,2048]{1,0:T(8,128)(2,1)}, bf16[128,2048]{1,0:T(8,128)(2,1)}, bf16[64,2048]{1,0:T(8,128)(2,1)}, bf16[64,2048]{1,0:T(8,128)(2,1)}, bf16[128,2048]{1,0:T(8,128)(2,1)}) custom-call(bf16[2048,1024]{1,0:T(8,128)(2,1)} %bitcast.35, bf16[2048,512]{1,0:T(8,128)(2,1)} %bitcast.37, bf16[512,128]{1,0:T(8,128)(2,1)} %pad_maximum_fusion.1.scaled_ref.update_ref, ...), custom_call_target="tpu_custom_call" | custom-call | flops 1 | bytes 1 | tf_op jit(solution)/shard_map/pallas_call | solution.py:107
  87.8 6.5 %collective-permute-done.11.refs_3_ = bf16[128,2048]{1,0:T(8,128)(2,1)S(1)} collective-permute-done((bf16[128,2048]{1,0:T(8,128)(2,1)}, bf16[128,2048]{1,0:T(8,128)(2,1)S(1)}, u32[]{:S(2)}, u32[]{:S(2)}) %collective-permute-start.11) | collective-permute-done | bytes 524320 | tf_op jit(solution)/shard_map/ppermute | solution.py:24
  95.1 4.1 %shard_map.108 = (bf16[512,512]{1,0:T(8,128)(2,1)}, bf16[512,512]{1,0:T(8,128)(2,1)}, bf16[2,512,512]{2,1,0:T(8,128)(2,1)}) custom-call(s32[2]{0:T(128)} %pad_add_fusion.place_ref, bf16[512,128]{1,0:T(8,128)(2,1)} %pad_maximum_fusion.1.scaled_ref.update_ref, bf16[128,2048]{1,0:T(8,128)(2,1)} %get-tuple-element.48.refs_0_, bf16[128,2048]{1,0:T(8,128)(2,1)} %copy-done.11, ...), custom_call_target="tpu_custom_call" | custom-call | flops 1 | bytes 1 | tf_op jit(solution)/shard_map/pallas_call | solution.py:107
  103.6 7.4 %shard_map.109 = (f32[2,128,1024]{2,1,0:T(8,128)}, f32[2,128,64]{2,1,0:T(8,128)}, bf16[2,128,1152]{2,1,0:T(8,128)(2,1)}) custom-call(bf16[2048,1024]{1,0:T(8,128)(2,1)} %bitcast.36, bf16[2048,512]{1,0:T(8,128)(2,1)} %bitcast.38, bf16[128,2048]{1,0:T(8,128)(2,1)} %get-tuple-element.48.refs_0_, bf16[128,2048]{1,0:T(8,128)(2,1)} %copy-done.11, ...), custom_call_target="tpu_custom_call" | custom-call | flops 1 | bytes 1 | tf_op jit(solution)/shard_map/pallas_call | solution.py:107
  111.0 5.1 %collective-permute-done.12.refs_2_ = bf16[64,2048]{1,0:T(8,128)(2,1)S(1)} collective-permute-done((bf16[64,2048]{1,0:T(8,128)(2,1)S(1)}, bf16[64,2048]{1,0:T(8,128)(2,1)S(1)}, u32[]{:S(2)}, u32[]{:S(2)}) %collective-permute-start.12) | collective-permute-done | bytes 262176 | tf_op jit(solution)/shard_map/ppermute | solution.py:24
  116.1 2.2 %collective-permute-done.13.refs_1_ = bf16[128,2048]{1,0:T(8,128)(2,1)S(1)} collective-permute-done((bf16[128,2048]{1,0:T(8,128)(2,1)S(1)}, bf16[128,2048]{1,0:T(8,128)(2,1)S(1)}, u32[]{:S(2)}, u32[]{:S(2)}) %collective-permute-start.13) | collective-permute-done | bytes 524320 | tf_op jit(solution)/shard_map/ppermute | solution.py:24
  125.1 13.4 %collective-permute-done.14 = bf16[2,128,1152]{2,1,0:T(8,128)(2,1)} collective-permute-done((bf16[2,128,1152]{2,1,0:T(8,128)(2,1)}, bf16[2,128,1152]{2,1,0:T(8,128)(2,1)}, u32[]{:S(2)}, u32[]{:S(2)}) %collective-permute-start.14) | collective-permute-done | bytes 589856 | tf_op jit(solution)/shard_map/ppermute | solution.py:24
  142.5 2.4 %collective-permute-start.21 = (bf16[128,2048]{1,0:T(8,128)(2,1)}, bf16[128,2048]{1,0:T(8,128)(2,1)S(1)}, u32[]{:S(2)}, u32[]{:S(2)}) collective-permute-start(bf16[128,2048]{1,0:T(8,128)(2,1)} %get-tuple-element.83), channel_id=1, source_target_pairs={{0,12},{4,8},{8,4},{12,0},{1,13},{5,9},{9,5},{13,1},{2,14},{6,10},... | collective-permute-start | bytes 1572872 | tf_op jit(solution)/shard_map/ppermute | solution.py:24
  145.7 6.4 %shard_map.110 = f32[512,2048]{1,0:T(8,128)} custom-call(s32[2]{0:T(128)} %pad_add_fusion.place_ref, s32[32]{0:T(128)} %tenant_ref.7, bf16[512,512]{1,0:T(8,128)(2,1)} %get-tuple-element.69.refs_0_, bf16[512,512]{1,0:T(8,128)(2,1)} %copy-done.20, bf16[2,512,512]{2,1,0:T(8,128)(2,1)} %copy-done.9, bf16[512,512]{1,0:T(8,128)(2,1)} %collective-permute-done.18.refs_3_), custom_call_target="tpu_custom_call" | custom-call | flops 1 | bytes 1 | tf_op jit(solution)/shard_map/pallas_call | solution.py:107
  155.0 5.4 %collective-permute-start.19 = (bf16[128,1024]{1,0:T(8,128)(2,1)}, bf16[128,1024]{1,0:T(8,128)(2,1)}, u32[]{:S(2)}, u32[]{:S(2)}) collective-permute-start(bf16[128,1024]{1,0:T(8,128)(2,1)} %fusion.3), channel_id=1, source_target_pairs={{0,8},{4,12},{8,0},{12,4},{1,9},{5,13},{9,1},{13,5},{2,10},{6,14},... | collective-permute-start | bytes 786440 | tf_op jit(solution)/shard_map/ppermute | solution.py:24
  165.1 5.0 %shard_map.112 = bf16[128,8192]{1,0:T(8,128)(2,1)} custom-call(s32[1]{0:T(128)} %bitcast.1.line_ref, bf16[128,8192]{1,0:T(8,128)(2,1)S(1)} %copy-done, f32[1,8192]{1,0:T(1,128)S(1)} %bitcast.34, f32[128,1]{1,0:T(8,128)S(1)} %copy-done.3, bf16[128,2048]{1,0:T(8,128)(2,1)S(1)} %copy-done.1, bf16[128,2048]{1,0:T(8,128)(2,1)S(1)} %collective-permute-done.13.refs_1_, ...), custom_call_target="tpu_custom_call" | custom-call | flops 1 | bytes 1 | tf_op jit(solution)/shard_map/pallas_call | solution.py:107
  170.1 8.7 %collective-permute-done.19 = bf16[128,1024]{1,0:T(8,128)(2,1)} collective-permute-done((bf16[128,1024]{1,0:T(8,128)(2,1)}, bf16[128,1024]{1,0:T(8,128)(2,1)}, u32[]{:S(2)}, u32[]{:S(2)}) %collective-permute-start.19) | collective-permute-done | bytes 262176 | tf_op jit(solution)/shard_map/ppermute | solution.py:24
  181.9 2.1 %shard_map.113 = f32[64,2048]{1,0:T(8,128)} custom-call(s32[2]{0:T(128)} %pad_add_fusion.place_ref, s32[32]{0:T(128)} %tenant_ref.7, bf16[64,512]{1,0:T(8,128)(2,1)} %get-tuple-element.85.refs_0_, bf16[64,512]{1,0:T(8,128)(2,1)} %copy-done.24, bf16[2,64,512]{2,1,0:T(8,128)(2,1)} %copy-done.22, bf16[64,512]{1,0:T(8,128)(2,1)} %copy-done.25), custom_call_target="tpu_custom_call" | custom-call | flops 1 | bytes 1 | tf_op jit(solution)/shard_map/pallas_call | solution.py:107
  (130 shorter events, 38.4 us)
Async XLA Ops:
  0.6 19.3 %collective-permute-start.2 = (bf16[128,1024]{1,0:T(8,128)(2,1)}, bf16[128,1024]{1,0:T(8,128)(2,1)S(1)}, u32[]{:S(2)}, u32[]{:S(2)}) collective-permute-start(bf16[128,1024]{1,0:T(8,128)(2,1)} %upstream_ref), channel_id=1, source_target_pairs={{0,8},{4,12},{8,0},{12,4},{1,9},{5,13},{9,1},{13,5},{2,10},{6,14},... | collective-permute-start | bytes 786440 | tf_op jit(solution)/shard_map/ppermute | solution.py:24
  4.7 57.0 %collective-permute-start = (bf16[512,1024]{1,0:T(8,128)(2,1)}, bf16[512,1024]{1,0:T(8,128)(2,1)}, u32[]{:S(2)}, u32[]{:S(2)}) collective-permute-start(bf16[512,1024]{1,0:T(8,128)(2,1)} %mine_ref), channel_id=1, source_target_pairs={{0,2},{2,0},{1,3},{3,1},{4,6},{6,4},{5,7},{7,5},{8,10},{10,8},{9,1... | collective-permute-start | bytes 3145736 | tf_op jit(solution)/shard_map/ppermute | solution.py:28
  19.5 42.2 %collective-permute-start.1 = (bf16[2,512,512]{2,1,0:T(8,128)(2,1)}, bf16[2,512,512]{2,1,0:T(8,128)(2,1)S(1)}, u32[]{:S(2)}, u32[]{:S(2)}) collective-permute-start(bf16[2,512,512]{2,1,0:T(8,128)(2,1)} %get-tuple-element.50), channel_id=1, source_target_pairs={{0,2},{2,0},{1,3},{3,1},{4,6},{6,4},{5,7},{7,5},{8,10},{10,8},{9,1... | collective-permute-start | bytes 3145736 | tf_op jit(solution)/shard_map/ppermute | solution.py:28
  20.0 41.7 %all-to-all-start = ((bf16[16,64,256]{2,1,0:T(8,128)(2,1)}), bf16[16,64,256]{2,1,0:T(8,128)(2,1)S(1)}, u32[]{:S(2)}, u32[]{:S(2)}) async-start(bf16[16,64,256]{2,1,0:T(8,128)(2,1)} %get-tuple-element.56), calls=%async_computation | async-start | bytes 1048576 | tf_op jit(solution)/shard_map/all_to_all | solution.py:360
  24.1 32.0 %collective-permute-start.4 = (bf16[256,1024]{1,0:T(8,128)(2,1)S(1)}, bf16[256,1024]{1,0:T(8,128)(2,1)S(1)}, u32[]{:S(2)}, u32[]{:S(2)}) collective-permute-start(bf16[256,1024]{1,0:T(8,128)(2,1)S(1)} %constant_dynamic-update-slice_fusion.refs_0_), channel_id=1, source_target_pairs={{0,4},{4,0},{8,12},{12,8},{1,5},{5,1},{9,13},{13,9},{2,6},{6,2},{1... | collective-permute-start | bytes 1572872 | tf_op jit(solution)/shard_map/ppermute | solution.py:24
  25.9 35.7 %collective-permute-start.3 = (bf16[128,2048]{1,0:T(8,128)(2,1)S(1)}, bf16[128,2048]{1,0:T(8,128)(2,1)S(1)}, u32[]{:S(2)}, u32[]{:S(2)}) collective-permute-start(bf16[128,2048]{1,0:T(8,128)(2,1)S(1)} %copy-done.27), channel_id=1, source_target_pairs={{0,8},{4,12},{8,0},{12,4},{1,9},{5,13},{9,1},{13,5},{2,10},{6,14},... | collective-permute-start | bytes 1572872 | tf_op jit(solution)/shard_map/ppermute | solution.py:24
  64.9 10.5 %collective-permute-start.5 = (bf16[512,1024]{1,0:T(8,128)(2,1)}, bf16[512,1024]{1,0:T(8,128)(2,1)S(1)}, u32[]{:S(2)}, u32[]{:S(2)}) collective-permute-start(bf16[512,1024]{1,0:T(8,128)(2,1)} %mine_ref), channel_id=1, source_target_pairs={{0,1},{1,0},{2,3},{3,2},{4,5},{5,4},{6,7},{7,6},{8,9},{9,8},{10,11... | collective-permute-start | bytes 3145736 | tf_op jit(solution)/shard_map/ppermute | solution.py:32
  65.4 10.0 %collective-permute-start.6 = (bf16[512,1024]{1,0:T(8,128)(2,1)}, bf16[512,1024]{1,0:T(8,128)(2,1)}, u32[]{:S(2)}, u32[]{:S(2)}) collective-permute-start(bf16[512,1024]{1,0:T(8,128)(2,1)} %collective-permute-done.across_ref), channel_id=1, source_target_pairs={{0,1},{1,0},{2,3},{3,2},{4,5},{5,4},{6,7},{7,6},{8,9},{9,8},{10,11... | collective-permute-start | bytes 3145736 | tf_op jit(solution)/shard_map/ppermute | solution.py:32
  66.3 6.0 %collective-permute-start.8 = (bf16[512,512]{1,0:T(8,128)(2,1)}, bf16[512,512]{1,0:T(8,128)(2,1)}, u32[]{:S(2)}, u32[]{:S(2)}) collective-permute-start(bf16[512,512]{1,0:T(8,128)(2,1)} %get-tuple-element.61), channel_id=1, source_target_pairs={{0,1},{1,0},{2,3},{3,2},{4,5},{5,4},{6,7},{7,6},{8,9},{9,8},{10,11... | collective-permute-start | bytes 1572872 | tf_op jit(solution)/shard_map/ppermute | solution.py:32
  69.9 17.9 %collective-permute-start.10 = (bf16[128,2048]{1,0:T(8,128)(2,1)}, bf16[128,2048]{1,0:T(8,128)(2,1)S(1)}, u32[]{:S(2)}, u32[]{:S(2)}) collective-permute-start(bf16[128,2048]{1,0:T(8,128)(2,1)} %get-tuple-element.66), channel_id=1, source_target_pairs={{0,4},{4,0},{8,12},{12,8},{1,5},{5,1},{9,13},{13,9},{2,6},{6,2},{1... | collective-permute-start | bytes 1572872 | tf_op jit(solution)/shard_map/ppermute | solution.py:24
  70.7 23.6 %collective-permute-start.11 = (bf16[128,2048]{1,0:T(8,128)(2,1)}, bf16[128,2048]{1,0:T(8,128)(2,1)S(1)}, u32[]{:S(2)}, u32[]{:S(2)}) collective-permute-start(bf16[128,2048]{1,0:T(8,128)(2,1)} %get-tuple-element.68), channel_id=1, source_target_pairs={{0,12},{4,8},{8,4},{12,0},{1,13},{5,9},{9,5},{13,1},{2,14},{6,10},... | collective-permute-start | bytes 1572872 | tf_op jit(solution)/shard_map/ppermute | solution.py:24
  99.3 25.5 %collective-permute-start.17 = (bf16[2,512,512]{2,1,0:T(8,128)(2,1)}, bf16[2,512,512]{2,1,0:T(8,128)(2,1)S(1)}, u32[]{:S(2)}, u32[]{:S(2)}) collective-permute-start(bf16[2,512,512]{2,1,0:T(8,128)(2,1)} %get-tuple-element.78), channel_id=1, source_target_pairs={{0,2},{2,0},{1,3},{3,1},{4,6},{6,4},{5,7},{7,5},{8,10},{10,8},{9,1... | collective-permute-start | bytes 3145736 | tf_op jit(solution)/shard_map/ppermute | solution.py:28
  100.6 17.7 %collective-permute-start.13 = (bf16[128,2048]{1,0:T(8,128)(2,1)S(1)}, bf16[128,2048]{1,0:T(8,128)(2,1)S(1)}, u32[]{:S(2)}, u32[]{:S(2)}) collective-permute-start(bf16[128,2048]{1,0:T(8,128)(2,1)S(1)} %copy-done.26), channel_id=1, source_target_pairs={{0,4},{4,0},{8,12},{12,8},{1,5},{5,1},{9,13},{13,9},{2,6},{6,2},{1... | collective-permute-start | bytes 1572872 | tf_op jit(solution)/shard_map/ppermute | solution.py:24
  102.6 13.5 %collective-permute-start.12 = (bf16[64,2048]{1,0:T(8,128)(2,1)S(1)}, bf16[64,2048]{1,0:T(8,128)(2,1)S(1)}, u32[]{:S(2)}, u32[]{:S(2)}) collective-permute-start(bf16[64,2048]{1,0:T(8,128)(2,1)S(1)} %copy-done.28), channel_id=1, source_target_pairs={{0,8},{4,12},{8,0},{12,4},{1,9},{5,13},{9,1},{13,5},{2,10},{6,14},... | collective-permute-start | bytes 786440 | tf_op jit(solution)/shard_map/ppermute | solution.py:24
  118.3 20.1 %collective-permute-start.14 = (bf16[2,128,1152]{2,1,0:T(8,128)(2,1)}, bf16[2,128,1152]{2,1,0:T(8,128)(2,1)}, u32[]{:S(2)}, u32[]{:S(2)}) collective-permute-start(bf16[2,128,1152]{2,1,0:T(8,128)(2,1)} %get-tuple-element.75), channel_id=1, source_target_pairs={{0,4},{4,0},{8,12},{12,8},{1,5},{5,1},{9,13},{13,9},{2,6},{6,2},{1... | collective-permute-start | bytes 1769480 | tf_op jit(solution)/shard_map/ppermute | solution.py:24
  123.0 21.9 %collective-permute-start.16 = (bf16[512,512]{1,0:T(8,128)(2,1)}, bf16[512,512]{1,0:T(8,128)(2,1)S(1)}, u32[]{:S(2)}, u32[]{:S(2)}) collective-permute-start(bf16[512,512]{1,0:T(8,128)(2,1)} %get-tuple-element.77), channel_id=1, source_target_pairs={{0,1},{1,0},{2,3},{3,2},{4,5},{5,4},{6,7},{7,6},{8,9},{9,8},{10,11... | collective-permute-start | bytes 1572872 | tf_op jit(solution)/shard_map/ppermute | solution.py:32
  123.0 42.0 %collective-permute-start.22 = (bf16[64,2048]{1,0:T(8,128)(2,1)}, bf16[64,2048]{1,0:T(8,128)(2,1)}, u32[]{:S(2)}, u32[]{:S(2)}) collective-permute-start(bf16[64,2048]{1,0:T(8,128)(2,1)} %get-tuple-element.88), channel_id=1, source_target_pairs={{0,8},{4,12},{8,0},{12,4},{1,9},{5,13},{9,1},{13,5},{2,10},{6,14},... | collective-permute-start | bytes 786440 | tf_op jit(solution)/shard_map/ppermute | solution.py:24
  124.8 20.1 %collective-permute-start.18 = (bf16[512,512]{1,0:T(8,128)(2,1)S(1)}, bf16[512,512]{1,0:T(8,128)(2,1)}, u32[]{:S(2)}, u32[]{:S(2)}) collective-permute-start(bf16[512,512]{1,0:T(8,128)(2,1)S(1)} %slice_bitcast_fusion), channel_id=1, source_target_pairs={{0,1},{1,0},{2,3},{3,2},{4,5},{5,4},{6,7},{7,6},{8,9},{9,8},{10,11... | collective-permute-start | bytes 1572872 | tf_op jit(solution)/shard_map/ppermute | solution.py:32
  139.6 12.5 %collective-permute-start.15 = (bf16[2,128,128]{2,1,0:T(8,128)(2,1)S(1)}, bf16[2,128,128]{2,1,0:T(8,128)(2,1)}, u32[]{:S(2)}, u32[]{:S(2)}) collective-permute-start(bf16[2,128,128]{2,1,0:T(8,128)(2,1)S(1)} %pad_maximum_fusion.3), channel_id=1, source_target_pairs={{0,8},{4,12},{8,0},{12,4},{1,9},{5,13},{9,1},{13,5},{2,10},{6,14},... | collective-permute-start | bytes 196616 | tf_op jit(solution)/shard_map/ppermute | solution.py:24
  142.5 18.6 %collective-permute-start.21 = (bf16[128,2048]{1,0:T(8,128)(2,1)}, bf16[128,2048]{1,0:T(8,128)(2,1)S(1)}, u32[]{:S(2)}, u32[]{:S(2)}) collective-permute-start(bf16[128,2048]{1,0:T(8,128)(2,1)} %get-tuple-element.83), channel_id=1, source_target_pairs={{0,12},{4,8},{8,4},{12,0},{1,13},{5,9},{9,5},{13,1},{2,14},{6,10},... | collective-permute-start | bytes 1572872 | tf_op jit(solution)/shard_map/ppermute | solution.py:24
  154.3 6.1 %collective-permute-start.20 = (bf16[256,128]{1,0:T(8,128)(2,1)S(1)}, bf16[256,128]{1,0:T(8,128)(2,1)S(1)}, u32[]{:S(2)}, u32[]{:S(2)}) collective-permute-start(bf16[256,128]{1,0:T(8,128)(2,1)S(1)} %bitcast.43), channel_id=1, source_target_pairs={{0,4},{4,0},{8,12},{12,8},{1,5},{5,1},{9,13},{13,9},{2,6},{6,2},{1... | collective-permute-start | bytes 196616 | tf_op jit(solution)/shard_map/ppermute | solution.py:24
  155.0 23.9 %collective-permute-start.19 = (bf16[128,1024]{1,0:T(8,128)(2,1)}, bf16[128,1024]{1,0:T(8,128)(2,1)}, u32[]{:S(2)}, u32[]{:S(2)}) collective-permute-start(bf16[128,1024]{1,0:T(8,128)(2,1)} %fusion.3), channel_id=1, source_target_pairs={{0,8},{4,12},{8,0},{12,4},{1,9},{5,13},{9,1},{13,5},{2,10},{6,14},... | collective-permute-start | bytes 786440 | tf_op jit(solution)/shard_map/ppermute | solution.py:24
  163.1 7.0 %collective-permute-start.24 = (bf16[2,64,512]{2,1,0:T(8,128)(2,1)}, bf16[2,64,512]{2,1,0:T(8,128)(2,1)S(1)}, u32[]{:S(2)}, u32[]{:S(2)}) collective-permute-start(bf16[2,64,512]{2,1,0:T(8,128)(2,1)} %get-tuple-element.90), channel_id=1, source_target_pairs={{0,2},{2,0},{1,3},{3,1},{4,6},{6,4},{5,7},{7,5},{8,10},{10,8},{9,1... | collective-permute-start | bytes 393224 | tf_op jit(solution)/shard_map/ppermute | solution.py:28
  165.0 15.7 %collective-permute-start.23 = (bf16[64,512]{1,0:T(8,128)(2,1)}, bf16[64,512]{1,0:T(8,128)(2,1)S(1)}, u32[]{:S(2)}, u32[]{:S(2)}) collective-permute-start(bf16[64,512]{1,0:T(8,128)(2,1)} %get-tuple-element.89), channel_id=1, source_target_pairs={{0,1},{1,0},{2,3},{3,2},{4,5},{5,4},{6,7},{7,6},{8,9},{9,8},{10,11... | collective-permute-start | bytes 196616 | tf_op jit(solution)/shard_map/ppermute | solution.py:32
  (32 other events, 359.5 us)

commit v5 on v4

--- a/solution.py
+++ b/solution.py
@@ -44,7 +44,7 @@
 def in_order(parts, place):
     rows, width = parts[0].shape
     shape = jax.ShapeDtypeStruct((4, rows, width), parts[0].dtype)
-    return call(order_kernel, shape, [place.reshape(1)], parts).reshape(4 * rows, width)
+    return call(order_kernel, shape, [place.reshape(1)], parts, 20).reshape(4 * rows, width)
 
 
 def gather_line(held):
@@ -157,14 +157,14 @@
         out_ref[:, first * RANK : first * RANK + PAIR] = jnp.concatenate(parts, axis=1)
 
 
-def class_adapters(place_ref, tenant_ref, size, blocks, r):
-    devices = [(place_ref[0] ^ s) * 4 + (place_ref[1] ^ r) for s in range(size)]
+def class_adapters(place_ref, tenant_ref, slots, blocks, r):
+    devices = [(place_ref[0] ^ s) * 4 + (place_ref[1] ^ r) for s in slots]
     return [tenant_ref[d * blocks + b] for d in devices for b in range(blocks)]
 
 
 def down_kernel(size, blocks, place_ref, tenant_ref, factor_ref, mine_ref, core_ref, pair_ref):
     for r, ref in enumerate((mine_ref, core_ref, pair_ref.at[0], pair_ref.at[1])):
-        write_columns(class_adapters(place_ref, tenant_ref, size, blocks, r), factor_ref, ref)
+        write_columns(class_adapters(place_ref, tenant_ref, range(size), blocks, r), factor_ref, ref)
 
 
 def down_columns(place, tenant, down_factor, size, blocks):
@@ -244,10 +244,10 @@
         jax.ShapeDtypeStruct((half, rows, value_width + PAIR), jnp.bfloat16),
     ]
     counts = [len(parts) for parts in normed]
-    return call(functools.partial(value_kernel, counts), shapes, [], [weight, down, *flat(normed)])
-
-
-def sum_over_line(values, low, crossed, meanwhile):
+    return call(functools.partial(value_kernel, counts), shapes, [], [weight, down, *flat(normed)], 32)
+
+
+def sum_over_line(values, low, crossed):
     value_width, far, step = values.shape[-1], lax.axis_size("line") // 2, 2
     values = values + crossed[..., :value_width].astype(jnp.float32)
     low = low + one_term(crossed[..., value_width:])
@@ -255,17 +255,17 @@
         low = low[::2] + one_term(over_line(two_terms(low[1::2]), step))
         values = values[::2] + over_line(values[1::2].astype(jnp.bfloat16), step).astype(jnp.float32)
         step *= 2
-    return values, low + one_term(after(over_line(two_terms(low), far), meanwhile))[::-1]
-
-
-def terms_kernel(counts, scale, place_ref, update_ref, *refs):
+    return values, low + one_term(over_line(two_terms(low), far))[::-1]
+
+
+def terms_kernel(counts, slots, scale, place_ref, update_ref, *refs):
     rows_refs, (mine_ref, core_ref, pair_ref, scratch) = grouped(refs[:-4], counts), refs[-4:]
     rows, width = rows_refs[0][0].shape
     shard = width // 4
-    for slot, parts in enumerate(rows_refs):
+    for at, (slot, parts) in enumerate(zip(slots, rows_refs)):
         held = whole(parts)
         for r in range(0, rows, 2 * BLK):
-            first = slot * rows + r
+            first, column = slot * rows + r, (at * rows + r) // BLK * RANK
             term = scale * lax.dot_general(
                 held[r : r + 2 * BLK, :],
                 on_diagonal(update_ref[first : first + 2 * BLK, :]),
@@ -274,30 +274,31 @@
             )
             for p in range(4):
                 scratch[p] = term[p * shard : (p + 1) * shard]
-            columns = slice(first // BLK * RANK, first // BLK * RANK + PAIR)
+            columns = slice(column, column + PAIR)
             for r4, ref in enumerate((mine_ref, core_ref, pair_ref.at[0], pair_ref.at[1])):
                 ref[:, columns] = scratch[place_ref[1] ^ r4].astype(jnp.bfloat16)
 
 
-def factor_terms(place, update, rows, scale):
-    count, width = rows[0][0].shape
+def factor_terms(place, update, rows, slots, scale):
+    count, width = rows[0][0].shape[0], rows[0][0].shape[1]
     shape = (width // 4, len(rows) * count // BLK * RANK)
     counts = [len(parts) for parts in rows]
     return call(
-        functools.partial(terms_kernel, counts, scale),
+        functools.partial(terms_kernel, counts, slots, scale),
         [jax.ShapeDtypeStruct(lead + shape, jnp.bfloat16) for lead in ((), (), (2,))],
         [place],
         [update, *flat(rows)],
+        32,
         scratch=[pltpu.VMEM((4, width // 4, PAIR), jnp.float32)],
     )
 
 
-def owner_kernel(size, blocks, place_ref, tenant_ref, *refs):
+def owner_kernel(groups, blocks, place_ref, tenant_ref, *refs):
     out_ref = refs[-1]
     out_ref[...] = jnp.zeros_like(out_ref)
     lane = lax.broadcasted_iota(jnp.int32, (out_ref.shape[0], PAIR), 1) // RANK
-    for r, terms_ref in enumerate(refs[:-1]):
-        adapters = class_adapters(place_ref, tenant_ref, size, blocks, r)
+    for at, terms_ref in enumerate(refs[:-1]):
+        adapters = class_adapters(place_ref, tenant_ref, groups[at // 4], blocks, at % 4)
         for first in range(0, len(adapters), 2):
             columns = slice(first * RANK, first * RANK + PAIR)
             both = terms_ref[:, columns] if len(terms_ref.shape) == 2 else terms_ref[0, :, columns]
@@ -309,10 +310,14 @@
                 out_ref[:, adapter_columns(adapter)] += jnp.where(lane == side, term, jnp.zeros_like(term))
 
 
-def owner_sums(place, tenant, size, terms, width):
-    blocks = terms[0].shape[1] // RANK // size
+def owner_sums(place, tenant, groups, terms, width):
+    blocks = terms[0].shape[1] // RANK // len(groups[0])
     shape = jax.ShapeDtypeStruct((terms[0].shape[0], width), jnp.float32)
-    return call(functools.partial(owner_kernel, size, blocks), shape, [place, tenant], terms)
+    return call(functools.partial(owner_kernel, groups, blocks), shape, [place, tenant], terms, 24)
+
+
+def four_terms(terms, crossed):
+    return [terms[0], over_cores(terms[1]), crossed, over_cores(crossed[1])]
 
 
 def token_grad_kernel(counts, line_ref, tokens_ref, gain_ref, inverse_ref, *refs):
@@ -384,38 +389,50 @@
     arrived = [normed[0]] + [[over_line(after(normed[s][0], scaled), s)] for s in range(1, size)]
     arrived[far] = [crossed_far]
 
+    columns = [
+        (lax.dynamic_slice_in_dim(p, line * 4 * value_rows, 4 * value_rows, 1), s)
+        for p, s in pieces
+    ]
+    columns = in_slots(columns)
+
+    early_slots, late_slots = [0, far], [s for s in range(1, size) if s != far]
+    early = factor_terms(place_, scaled, [arrived[s] for s in early_slots], early_slots, 1.0)
+    early_crossed = over_pair(early[2])
+
     counts = [1] * far + [2] + [1] * (far - 1)
     back = call(
         functools.partial(back_kernel, [s for _, s in pieces], counts, rows),
         parted(counts, rows, weight.shape[0]),
         [],
-        [weight, down, scaled] + [p for p, _ in pieces],
+        [after(weight, early[0], columns), down, scaled] + [p for p, _ in pieces],
+        32,
     )
     back = grouped(back, counts)
     first = over_line(back[far][0], far)
 
-    terms = factor_terms(place_, after(scaled, back[0][0]), arrived, 1.0)
-    values, low, sent = value_products(after(weight, terms[0]), down, arrived)
+    values, low, sent = value_products(after(weight, back[0][0]), down, arrived)
     back_mine = [back[0]] + [[over_line(back[s][0], s)] for s in range(1, far)]
-    crossed = over_line(after(sent, first, *flat(back_mine)), 1)
+    crossed = over_line(after(sent, first, early_crossed, *flat(back_mine)), 1)
     back_mine += [[first, over_line(after(back[far][1], first), far)]]
-
-    crossed_terms = over_pair(terms[2])
-    terms = [terms[0], over_cores(terms[1]), crossed_terms, over_cores(crossed_terms[1])]
-    grad_down = owner_sums(place_, tenant, size, terms, adapter_width)
-
-    values, low = sum_over_line(values, low, crossed, grad_down)
+    crossed = after(crossed, back_mine[far][1])
+
+    late = factor_terms(place_, after(scaled, first, sent), [arrived[s] for s in late_slots], late_slots, 1.0)
+    late_crossed = over_pair(late[2])
+    early, late, early_crossed, late_crossed, _ = lax.optimization_barrier(
+        (early[:2], late[:2], early_crossed, late_crossed, crossed)
+    )
+    terms = four_terms(early, early_crossed) + four_terms(late, late_crossed)
+    grad_down = owner_sums(place_, tenant, [early_slots, late_slots], terms, adapter_width)
+
+    values, low = sum_over_line(values, low, crossed)
     low = low.astype(jnp.bfloat16)
     back_mine += [[over_line(after(back[s][0], crossed), s)] for s in range(far + 1, size)]
-    last = over_line(after(values[1].astype(jnp.bfloat16), low), far)
+    last = over_line(after(values[1].astype(jnp.bfloat16), *flat(back_mine[far + 1 :])), far)
     values = values[0] + last.astype(jnp.float32)
-    columns = [
-        (lax.dynamic_slice_in_dim(p, line * 4 * value_rows, 4 * value_rows, 1), s)
-        for p, s in pieces
-    ]
     low_held = jnp.concatenate([low, low], axis=-1).reshape(2 * rows, PAIR)
-    low_all = after(in_slots(gather_line(low_held)), *flat(back_mine[far + 1 :]))
-    terms = factor_terms(place_, low_all, [[in_slots(columns)]], adapter_scale)
+    low_pieces = [(after(p, grad_down), s) for p, s in gather_line(low_held)]
+    low_all = after(in_slots(low_pieces), *flat(back_mine[far + 1 :]))
+    terms = factor_terms(place_, low_all, [[columns]], [0], adapter_scale)
     crossed_terms = over_pair(terms[2])
     grad_tokens = call(
         functools.partial(token_grad_kernel, counts),
@@ -425,8 +442,8 @@
         32,
     )
     crossed_terms = after(crossed_terms, grad_tokens, last)
-    terms = [terms[0], over_cores(terms[1]), crossed_terms, over_cores(crossed_terms[1])]
-    grad_up = owner_sums(place_, tenant, size, terms, adapter_width)
+    terms = four_terms(terms, crossed_terms)
+    grad_up = owner_sums(place_, tenant, [list(range(size))], terms, adapter_width)
 
     adapter_branch = jnp.einsum(
         "bkr,vbr->bkv",

time: 187 us -> 177 us (0.947); the launches traced: 184 us -> 177 us
  Pallas kernels: 56.5 us -> 38.9 us
  waiting for transfers between devices: 71.9 us -> 87.6 us
  other arithmetic: 8.88 us -> 3.95 us
    pallas_call x12 -> x13, Pallas kernels: 56.5 us -> 38.9 us  [call(): pl.pallas_call(kernel, out_shape=out_shape, in_specs=[smem] * len(scalars...]
    ppermute x14, waiting for transfers between devices: 71.9 us -> 86 us  [over_line(): return lax.ppermute(value, 'line', [(i, i ^ mask) for i in range(size)])]
    concatenate x3, other arithmetic: 2.03 us -> 0.04 us  [in_slots(): return jnp.concatenate([found[m] for m in range(len(found))])]
    ppermute x4 -> x5, starting transfers between devices: 4 us -> 5.37 us  [over_pair(): return lax.ppermute(value, 'pair', [(0, 1), (1, 0)])]
    unnamed x59 -> x61, local copies, waits for them, and re-layouts: 5.81 us -> 6.29 us
  transfers between devices with their start and end apart: 27 -> 30, of which waited for: 8 -> 11; matrix products, arithmetic and copies ran while one was open for 8% -> 4% of each run, Pallas kernels for 26% -> 20%
where the time goes in v5:
time: 177 us
  waiting for transfers between devices  87.6 us (49%)
  Pallas kernels  38.9 us (22%)
  starting transfers between devices  34.8 us (20%)
  local copies, waits for them, and re-layouts  10 us (6%)
  other arithmetic  3.95 us (2%)
    ppermute x14, waiting for transfers between devices, over_line(): return lax.ppermute(value, 'line', [(i, i ^ mask) for i in range(size)])  86 us
    pallas_call x13, Pallas kernels, call(): pl.pallas_call(kernel, out_shape=out_shape, in_specs=[smem] * len(scalars...  38.9 us
    ppermute x14, starting transfers between devices, over_line(): return lax.ppermute(value, 'line', [(i, i ^ mask) for i in range(size)])  23.1 us
    unnamed x61, local copies, waits for them, and re-layouts  6.29 us
    ppermute x5, starting transfers between devices, over_pair(): return lax.ppermute(value, 'pair', [(0, 1), (1, 0)])  5.37 us
    all_to_all x1, starting transfers between devices, on_device(): lax.all_to_all(after(up_sent, upstream_far, over_cores(inverse)), ('line'...  4.42 us
  transfers between devices with their start and end apart: 30, of which 11 were waited for; matrix products, arithmetic and copies ran while one was open for 4% of the time, Pallas kernels for 20%

profile of v5, /device:TPU:0, one launch (start us, length us, event | category | flops | bytes accessed | tf_op | source)
XLA Modules:
  0.0 176.6 jit_solution(10059339959093697548)
XLA Ops:
  0.6 4.1 %collective-permute-start.2 = (bf16[128,1024]{1,0:T(8,128)(2,1)}, bf16[128,1024]{1,0:T(8,128)(2,1)S(1)}, u32[]{:S(2)}, u32[]{:S(2)}) collective-permute-start(bf16[128,1024]{1,0:T(8,128)(2,1)} %upstream_ref), channel_id=1, source_target_pairs={{0,8},{4,12},{8,0},{12,4},{1,9},{5,13},{9,1},{13,5},{2,10},{6,14},... | collective-permute-start | bytes 786440 | tf_op jit(solution)/shard_map/ppermute | solution.py:24
  6.3 6.2 %shard_map.102 = (bf16[16,64,256]{2,1,0:T(8,128)(2,1)}, f32[128,1]{1,0:T(8,128)}, bf16[128,2048]{1,0:T(8,128)(2,1)}, bf16[128,2048]{1,0:T(8,128)(2,1)}, bf16[128...) custom-call(s32[1]{0:T(128)} %bitcast.1.line_ref, s32[32]{0:T(128)} %tenant_ref.7, bf16[128,8192]{1,0:T(8,128)(2,1)} %tokens_ref.3, ...), custom_call_target="tpu_custom_call" | custom-call | flops 1 | bytes 1 | tf_op jit(solution)/shard_map/pallas_call | solution.py:107
  13.1 6.3 %shard_map.103 = (bf16[512,512]{1,0:T(8,128)(2,1)}, bf16[512,512]{1,0:T(8,128)(2,1)}, bf16[2,512,512]{2,1,0:T(8,128)(2,1)}) custom-call(s32[2]{0:T(128)} %pad_add_fusion.place_ref, s32[32]{0:T(128)} %tenant_ref.7, bf16[512,2048]{1,0:T(8,128)(2,1)} %factor_ref), custom_call_target="tpu_custom_call" | custom-call | flops 1 | bytes 1 | tf_op jit(solution)/shard_map/pallas_call | solution.py:107
  19.9 4.4 %all-to-all-start = ((bf16[16,64,256]{2,1,0:T(8,128)(2,1)}), bf16[16,64,256]{2,1,0:T(8,128)(2,1)}, u32[]{:S(2)}, u32[]{:S(2)}) async-start(bf16[16,64,256]{2,1,0:T(8,128)(2,1)} %get-tuple-element.68), calls=%async_computation | async-start | bytes 1048576 | tf_op jit(solution)/shard_map/all_to_all | solution.py:365
  24.4 2.6 %collective-permute-start.3 = (bf16[128,2048]{1,0:T(8,128)(2,1)}, bf16[128,2048]{1,0:T(8,128)(2,1)S(1)}, u32[]{:S(2)}, u32[]{:S(2)}) collective-permute-start(bf16[128,2048]{1,0:T(8,128)(2,1)} %get-tuple-element.65), channel_id=1, source_target_pairs={{0,8},{4,12},{8,0},{12,4},{1,9},{5,13},{9,1},{13,5},{2,10},{6,14},... | collective-permute-start | bytes 1572872 | tf_op jit(solution)/shard_map/ppermute | solution.py:24
  27.0 1.6 collective-permute-start.4
  28.5 33.2 %collective-permute-done.3.refs_1_.refs_2_ = bf16[128,2048]{1,0:T(8,128)(2,1)S(1)} collective-permute-done((bf16[128,2048]{1,0:T(8,128)(2,1)}, bf16[128,2048]{1,0:T(8,128)(2,1)S(1)}, u32[]{:S(2)}, u32[]{:S(2)}) %collective-permute-start.3) | collective-permute-done | bytes 524320 | tf_op jit(solution)/shard_map/ppermute | solution.py:24
  61.8 2.4 %shard_map.104 = bf16[256,128]{1,0:T(8,128)(2,1)} custom-call(bf16[128,1024]{1,0:T(8,128)(2,1)} %upstream_ref, bf16[128,1024]{1,0:T(8,128)(2,1)} %copy-done.27, bf16[1024,256]{1,0:T(8,128)(2,1)} %bitcast.3.up_ref), custom_call_target="tpu_custom_call" | custom-call | flops 1 | bytes 1 | tf_op jit(solution)/shard_map/pallas_call | solution.py:107
  66.3 3.0 %collective-permute-done.7 = bf16[256,128]{1,0:T(8,128)(2,1)S(1)} collective-permute-done((bf16[256,128]{1,0:T(8,128)(2,1)}, bf16[256,128]{1,0:T(8,128)(2,1)S(1)}, u32[]{:S(2)}, u32[]{:S(2)}) %collective-permute-start.7) | collective-permute-done | bytes 65568 | tf_op jit(solution)/shard_map/ppermute | solution.py:24
  77.8 3.2 %shard_map.108 = (bf16[128,2048]{1,0:T(8,128)(2,1)S(1)}, bf16[128,2048]{1,0:T(8,128)(2,1)S(1)}, bf16[64,2048]{1,0:T(8,128)(2,1)S(1)}, bf16[64,2048]{1,0:T(8,128)(2,1)}, bf16[128,2048]{1,0:T(8,128)(2,1)S(1)}) custom-call(bf16[2048,1024]{1,0:T(8,128)(2,1)S(1)} %bitcast.31, bf16[2048,512]{1,0:T(8,128)(2,1)S(1)} %bitcast.33, ...), custom_call_target="tpu_custom_call" | custom-call | flops 1 | bytes 1 | tf_op jit(solution)/shard_map/pallas_call | solution.py:107
  83.6 1.9 %collective-permute-start.12 = (bf16[64,2048]{1,0:T(8,128)(2,1)S(1)}, bf16[64,2048]{1,0:T(8,128)(2,1)S(1)}, u32[]{:S(2)}, u32[]{:S(2)}) collective-permute-start(bf16[64,2048]{1,0:T(8,128)(2,1)S(1)} %get-tuple-element.85), channel_id=1, source_target_pairs={{0,8},{4,12},{8,0},{12,4},{1,9},{5,13},{9,1},{13,5},{2,10},{6,14},... | collective-permute-start | bytes 786440 | tf_op jit(solution)/shard_map/ppermute | solution.py:24
  85.5 9.5 %collective-permute-done.11.refs_3_.refs_1_ = bf16[128,2048]{1,0:T(8,128)(2,1)S(1)} collective-permute-done((bf16[128,2048]{1,0:T(8,128)(2,1)S(1)}, bf16[128,2048]{1,0:T(8,128)(2,1)S(1)}, u32[]{:S(2)}, u32[]{:S(2)}) %collective-permute-start.11) | collective-permute-done | bytes 524320 | tf_op jit(solution)/shard_map/ppermute | solution.py:24
  95.1 4.0 %shard_map.109 = (f32[2,128,1024]{2,1,0:T(8,128)S(1)}, f32[2,128,64]{2,1,0:T(8,128)S(1)}, bf16[2,128,1152]{2,1,0:T(8,128)(2,1)}) custom-call(bf16[2048,1024]{1,0:T(8,128)(2,1)S(1)} %bitcast.32, bf16[2048,512]{1,0:T(8,128)(2,1)S(1)} %bitcast.34, bf16[128,2048]{1,0:T(8,128)(2,1)S(1)} %copy-done.1, ...), custom_call_target="tpu_custom_call" | custom-call | flops 1 | bytes 1 | tf_op jit(solution)/shard_map/pallas_call | solution.py:107
  99.8 8.8 %collective-permute-done.12.refs_2_ = bf16[64,2048]{1,0:T(8,128)(2,1)S(1)} collective-permute-done((bf16[64,2048]{1,0:T(8,128)(2,1)S(1)}, bf16[64,2048]{1,0:T(8,128)(2,1)S(1)}, u32[]{:S(2)}, u32[]{:S(2)}) %collective-permute-start.12) | collective-permute-done | bytes 262176 | tf_op jit(solution)/shard_map/ppermute | solution.py:24
  112.5 1.7 collective-permute-start.16
  118.3 11.9 %collective-permute-done.16.refs_3_ = bf16[64,2048]{1,0:T(8,128)(2,1)S(1)} collective-permute-done((bf16[64,2048]{1,0:T(8,128)(2,1)}, bf16[64,2048]{1,0:T(8,128)(2,1)S(1)}, u32[]{:S(2)}, u32[]{:S(2)}) %collective-permute-start.16) | collective-permute-done | bytes 262176 | tf_op jit(solution)/shard_map/ppermute | solution.py:24
  130.3 2.2 %collective-permute-done.15 = bf16[2,128,1152]{2,1,0:T(8,128)(2,1)} collective-permute-done((bf16[2,128,1152]{2,1,0:T(8,128)(2,1)}, bf16[2,128,1152]{2,1,0:T(8,128)(2,1)}, u32[]{:S(2)}, u32[]{:S(2)}) %collective-permute-start.15) | collective-permute-done | bytes 589856 | tf_op jit(solution)/shard_map/ppermute | solution.py:24
  134.7 2.4 %collective-permute-start.17 = (bf16[128,2048]{1,0:T(8,128)(2,1)}, bf16[128,2048]{1,0:T(8,128)(2,1)S(1)}, u32[]{:S(2)}, u32[]{:S(2)}) collective-permute-start(bf16[128,2048]{1,0:T(8,128)(2,1)} %copy-done.22), channel_id=1, source_target_pairs={{0,12},{4,8},{8,4},{12,0},{1,13},{5,9},{9,5},{13,1},{2,14},{6,10},... | collective-permute-start | bytes 1572872 | tf_op jit(solution)/shard_map/ppermute | solution.py:24
  140.1 10.9 %collective-permute-done.19 = bf16[2,128,128]{2,1,0:T(8,128)(2,1)S(1)} collective-permute-done((bf16[2,128,128]{2,1,0:T(8,128)(2,1)S(1)}, bf16[2,128,128]{2,1,0:T(8,128)(2,1)S(1)}, u32[]{:S(2)}, u32[]{:S(2)}) %collective-permute-start.19) | collective-permute-done | bytes 65568 | tf_op jit(solution)/shard_map/ppermute | solution.py:24
  152.5 6.2 %shard_map.111 = f32[512,2048]{1,0:T(8,128)} custom-call(s32[2]{0:T(128)S(1)} %copy-done.20, s32[32]{0:T(128)S(1)} %copy-done.21, bf16[512,256]{1,0:T(8,128)(2,1)S(1)} %copy-done.15, bf16[512,256]{1,0:T(8,128)(2,1)S(1)} %collective-permute-done.21.refs_1_, bf16[2,512,256]{2,1,0:T(8,128)(2,1)} %collective-permute-done.13.refs_2_, ...), custom_call_target="tpu_custom_call" | custom-call | flops 1 | bytes 1 | tf_op jit(solution)/shard_map/pallas_call | solution.py:107
  158.7 3.7 %collective-permute-start.18 = (bf16[128,1024]{1,0:T(8,128)(2,1)S(1)}, bf16[128,1024]{1,0:T(8,128)(2,1)S(1)}, u32[]{:S(2)}, u32[]{:S(2)}) collective-permute-start(bf16[128,1024]{1,0:T(8,128)(2,1)S(1)} %fusion.3), channel_id=1, source_target_pairs={{0,8},{4,12},{8,0},{12,4},{1,9},{5,13},{9,1},{13,5},{2,10},{6,14},... | collective-permute-start | bytes 786440 | tf_op jit(solution)/shard_map/ppermute | solution.py:24
  164.4 4.0 %shard_map.113 = bf16[128,8192]{1,0:T(8,128)(2,1)} custom-call(s32[1]{0:T(128)} %bitcast.1.line_ref, bf16[128,8192]{1,0:T(8,128)(2,1)S(1)} %copy-done, f32[1,8192]{1,0:T(1,128)S(1)} %bitcast.36, f32[128,1]{1,0:T(8,128)S(1)} %copy-done.19, bf16[128,2048]{1,0:T(8,128)(2,1)S(1)} %copy-done.8, bf16[128,2048]{1,0:T(8,128)(2,1)S(1)} %copy-done.10, ...), custom_call_target="tpu_custom_call" | custom-call | flops 1 | bytes 1 | tf_op jit(solution)/shard_map/pallas_call | solution.py:107
  168.4 5.2 %collective-permute-done.18 = bf16[128,1024]{1,0:T(8,128)(2,1)S(1)} collective-permute-done((bf16[128,1024]{1,0:T(8,128)(2,1)S(1)}, bf16[128,1024]{1,0:T(8,128)(2,1)S(1)}, u32[]{:S(2)}, u32[]{:S(2)}) %collective-permute-start.18) | collective-permute-done | bytes 262176 | tf_op jit(solution)/shard_map/ppermute | solution.py:24
  174.9 1.7 shard_map.114
  (139 shorter events, 34.3 us)
Async XLA Ops:
  0.6 19.2 %collective-permute-start.2 = (bf16[128,1024]{1,0:T(8,128)(2,1)}, bf16[128,1024]{1,0:T(8,128)(2,1)S(1)}, u32[]{:S(2)}, u32[]{:S(2)}) collective-permute-start(bf16[128,1024]{1,0:T(8,128)(2,1)} %upstream_ref), channel_id=1, source_target_pairs={{0,8},{4,12},{8,0},{12,4},{1,9},{5,13},{9,1},{13,5},{2,10},{6,14},... | collective-permute-start | bytes 786440 | tf_op jit(solution)/shard_map/ppermute | solution.py:24
  4.7 57.0 %collective-permute-start = (bf16[512,1024]{1,0:T(8,128)(2,1)}, bf16[512,1024]{1,0:T(8,128)(2,1)}, u32[]{:S(2)}, u32[]{:S(2)}) collective-permute-start(bf16[512,1024]{1,0:T(8,128)(2,1)} %mine_ref), channel_id=1, source_target_pairs={{0,2},{2,0},{1,3},{3,1},{4,6},{6,4},{5,7},{7,5},{8,10},{10,8},{9,1... | collective-permute-start | bytes 3145736 | tf_op jit(solution)/shard_map/ppermute | solution.py:28
  19.4 42.4 %collective-permute-start.1 = (bf16[2,512,512]{2,1,0:T(8,128)(2,1)}, bf16[2,512,512]{2,1,0:T(8,128)(2,1)S(1)}, u32[]{:S(2)}, u32[]{:S(2)}) collective-permute-start(bf16[2,512,512]{2,1,0:T(8,128)(2,1)} %get-tuple-element.62), channel_id=1, source_target_pairs={{0,2},{2,0},{1,3},{3,1},{4,6},{6,4},{5,7},{7,5},{8,10},{10,8},{9,1... | collective-permute-start | bytes 3145736 | tf_op jit(solution)/shard_map/ppermute | solution.py:28
  19.9 41.9 %all-to-all-start = ((bf16[16,64,256]{2,1,0:T(8,128)(2,1)}), bf16[16,64,256]{2,1,0:T(8,128)(2,1)}, u32[]{:S(2)}, u32[]{:S(2)}) async-start(bf16[16,64,256]{2,1,0:T(8,128)(2,1)} %get-tuple-element.68), calls=%async_computation | async-start | bytes 1048576 | tf_op jit(solution)/shard_map/all_to_all | solution.py:365
  24.4 37.4 %collective-permute-start.3 = (bf16[128,2048]{1,0:T(8,128)(2,1)}, bf16[128,2048]{1,0:T(8,128)(2,1)S(1)}, u32[]{:S(2)}, u32[]{:S(2)}) collective-permute-start(bf16[128,2048]{1,0:T(8,128)(2,1)} %get-tuple-element.65), channel_id=1, source_target_pairs={{0,8},{4,12},{8,0},{12,4},{1,9},{5,13},{9,1},{13,5},{2,10},{6,14},... | collective-permute-start | bytes 1572872 | tf_op jit(solution)/shard_map/ppermute | solution.py:24
  27.0 34.8 %collective-permute-start.4 = (bf16[256,1024]{1,0:T(8,128)(2,1)S(1)}, bf16[256,1024]{1,0:T(8,128)(2,1)S(1)}, u32[]{:S(2)}, u32[]{:S(2)}) collective-permute-start(bf16[256,1024]{1,0:T(8,128)(2,1)S(1)} %constant_dynamic-update-slice_fusion.refs_0_), channel_id=1, source_target_pairs={{0,4},{4,0},{8,12},{12,8},{1,5},{5,1},{9,13},{13,9},{2,6},{6,2},{1... | collective-permute-start | bytes 1572872 | tf_op jit(solution)/shard_map/ppermute | solution.py:24
  64.2 11.0 %collective-permute-start.5 = (bf16[512,1024]{1,0:T(8,128)(2,1)}, bf16[512,1024]{1,0:T(8,128)(2,1)S(1)}, u32[]{:S(2)}, u32[]{:S(2)}) collective-permute-start(bf16[512,1024]{1,0:T(8,128)(2,1)} %mine_ref), channel_id=1, source_target_pairs={{0,1},{1,0},{2,3},{3,2},{4,5},{5,4},{6,7},{7,6},{8,9},{9,8},{10,11... | collective-permute-start | bytes 3145736 | tf_op jit(solution)/shard_map/ppermute | solution.py:32
  64.2 11.0 %collective-permute-start.6 = (bf16[512,1024]{1,0:T(8,128)(2,1)}, bf16[512,1024]{1,0:T(8,128)(2,1)S(1)}, u32[]{:S(2)}, u32[]{:S(2)}) collective-permute-start(bf16[512,1024]{1,0:T(8,128)(2,1)} %collective-permute-done.across_ref), channel_id=1, source_target_pairs={{0,1},{1,0},{2,3},{3,2},{4,5},{5,4},{6,7},{7,6},{8,9},{9,8},{10,11... | collective-permute-start | bytes 3145736 | tf_op jit(solution)/shard_map/ppermute | solution.py:32
  65.0 8.6 %collective-permute-start.9 = (bf16[512,512]{1,0:T(8,128)(2,1)S(1)}, bf16[512,512]{1,0:T(8,128)(2,1)S(1)}, u32[]{:S(2)}, u32[]{:S(2)}) collective-permute-start(bf16[512,512]{1,0:T(8,128)(2,1)S(1)} %slice_bitcast_fusion.1), channel_id=1, source_target_pairs={{0,1},{1,0},{2,3},{3,2},{4,5},{5,4},{6,7},{7,6},{8,9},{9,8},{10,11... | collective-permute-start | bytes 1572872 | tf_op jit(solution)/shard_map/ppermute | solution.py:32
  69.4 16.2 %collective-permute-start.10 = (bf16[128,2048]{1,0:T(8,128)(2,1)S(1)}, bf16[128,2048]{1,0:T(8,128)(2,1)S(1)}, u32[]{:S(2)}, u32[]{:S(2)}) collective-permute-start(bf16[128,2048]{1,0:T(8,128)(2,1)S(1)} %copy-done.29), channel_id=1, source_target_pairs={{0,4},{4,0},{8,12},{12,8},{1,5},{5,1},{9,13},{13,9},{2,6},{6,2},{1... | collective-permute-start | bytes 1572872 | tf_op jit(solution)/shard_map/ppermute | solution.py:24
  72.2 22.9 %collective-permute-start.11 = (bf16[128,2048]{1,0:T(8,128)(2,1)S(1)}, bf16[128,2048]{1,0:T(8,128)(2,1)S(1)}, u32[]{:S(2)}, u32[]{:S(2)}) collective-permute-start(bf16[128,2048]{1,0:T(8,128)(2,1)S(1)} %copy-done.28), channel_id=1, source_target_pairs={{0,12},{4,8},{8,4},{12,0},{1,13},{5,9},{9,5},{13,1},{2,14},{6,10},... | collective-permute-start | bytes 1572872 | tf_op jit(solution)/shard_map/ppermute | solution.py:24
  73.6 26.2 %collective-permute-start.13 = (bf16[2,512,256]{2,1,0:T(8,128)(2,1)S(1)}, bf16[2,512,256]{2,1,0:T(8,128)(2,1)}, u32[]{:S(2)}, u32[]{:S(2)}) collective-permute-start(bf16[2,512,256]{2,1,0:T(8,128)(2,1)S(1)} %get-tuple-element.86), channel_id=1, source_target_pairs={{0,2},{2,0},{1,3},{3,1},{4,6},{6,4},{5,7},{7,5},{8,10},{10,8},{9,1... | collective-permute-start | bytes 1572872 | tf_op jit(solution)/shard_map/ppermute | solution.py:28
  82.6 27.9 %collective-permute-start.14 = (bf16[128,2048]{1,0:T(8,128)(2,1)S(1)}, bf16[128,2048]{1,0:T(8,128)(2,1)S(1)}, u32[]{:S(2)}, u32[]{:S(2)}) collective-permute-start(bf16[128,2048]{1,0:T(8,128)(2,1)S(1)} %get-tuple-element.87), channel_id=1, source_target_pairs={{0,4},{4,0},{8,12},{12,8},{1,5},{5,1},{9,13},{13,9},{2,6},{6,2},{1... | collective-permute-start | bytes 1572872 | tf_op jit(solution)/shard_map/ppermute | solution.py:24
  83.6 25.0 %collective-permute-start.12 = (bf16[64,2048]{1,0:T(8,128)(2,1)S(1)}, bf16[64,2048]{1,0:T(8,128)(2,1)S(1)}, u32[]{:S(2)}, u32[]{:S(2)}) collective-permute-start(bf16[64,2048]{1,0:T(8,128)(2,1)S(1)} %get-tuple-element.85), channel_id=1, source_target_pairs={{0,8},{4,12},{8,0},{12,4},{1,9},{5,13},{9,1},{13,5},{2,10},{6,14},... | collective-permute-start | bytes 786440 | tf_op jit(solution)/shard_map/ppermute | solution.py:24
  111.3 21.2 %collective-permute-start.15 = (bf16[2,128,1152]{2,1,0:T(8,128)(2,1)}, bf16[2,128,1152]{2,1,0:T(8,128)(2,1)}, u32[]{:S(2)}, u32[]{:S(2)}) collective-permute-start(bf16[2,128,1152]{2,1,0:T(8,128)(2,1)} %get-tuple-element.88), channel_id=1, source_target_pairs={{0,4},{4,0},{8,12},{12,8},{1,5},{5,1},{9,13},{13,9},{2,6},{6,2},{1... | collective-permute-start | bytes 1769480 | tf_op jit(solution)/shard_map/ppermute | solution.py:24
  112.5 17.7 %collective-permute-start.16 = (bf16[64,2048]{1,0:T(8,128)(2,1)}, bf16[64,2048]{1,0:T(8,128)(2,1)S(1)}, u32[]{:S(2)}, u32[]{:S(2)}) collective-permute-start(bf16[64,2048]{1,0:T(8,128)(2,1)} %get-tuple-element.90), channel_id=1, source_target_pairs={{0,8},{4,12},{8,0},{12,4},{1,9},{5,13},{9,1},{13,5},{2,10},{6,14},... | collective-permute-start | bytes 786440 | tf_op jit(solution)/shard_map/ppermute | solution.py:24
  117.3 21.1 %collective-permute-start.20 = (bf16[2,512,256]{2,1,0:T(8,128)(2,1)S(1)}, bf16[2,512,256]{2,1,0:T(8,128)(2,1)S(1)}, u32[]{:S(2)}, u32[]{:S(2)}) collective-permute-start(bf16[2,512,256]{2,1,0:T(8,128)(2,1)S(1)} %get-tuple-element.101), channel_id=1, source_target_pairs={{0,2},{2,0},{1,3},{3,1},{4,6},{6,4},{5,7},{7,5},{8,10},{10,8},{9,1... | collective-permute-start | bytes 1572872 | tf_op jit(solution)/shard_map/ppermute | solution.py:28
  133.6 17.4 %collective-permute-start.19 = (bf16[2,128,128]{2,1,0:T(8,128)(2,1)S(1)}, bf16[2,128,128]{2,1,0:T(8,128)(2,1)S(1)}, u32[]{:S(2)}, u32[]{:S(2)}) collective-permute-start(bf16[2,128,128]{2,1,0:T(8,128)(2,1)S(1)} %pad_maximum_fusion.3), channel_id=1, source_target_pairs={{0,8},{4,12},{8,0},{12,4},{1,9},{5,13},{9,1},{13,5},{2,10},{6,14},... | collective-permute-start | bytes 196616 | tf_op jit(solution)/shard_map/ppermute | solution.py:24
  134.7 24.0 %collective-permute-start.17 = (bf16[128,2048]{1,0:T(8,128)(2,1)}, bf16[128,2048]{1,0:T(8,128)(2,1)S(1)}, u32[]{:S(2)}, u32[]{:S(2)}) collective-permute-start(bf16[128,2048]{1,0:T(8,128)(2,1)} %copy-done.22), channel_id=1, source_target_pairs={{0,12},{4,8},{8,4},{12,0},{1,13},{5,9},{9,5},{13,1},{2,14},{6,10},... | collective-permute-start | bytes 1572872 | tf_op jit(solution)/shard_map/ppermute | solution.py:24
  138.4 12.9 %collective-permute-start.21 = (bf16[512,256]{1,0:T(8,128)(2,1)S(1)}, bf16[512,256]{1,0:T(8,128)(2,1)S(1)}, u32[]{:S(2)}, u32[]{:S(2)}) collective-permute-start(bf16[512,256]{1,0:T(8,128)(2,1)S(1)} %copy-done.24), channel_id=1, source_target_pairs={{0,1},{1,0},{2,3},{3,2},{4,5},{5,4},{6,7},{7,6},{8,9},{9,8},{10,11... | collective-permute-start | bytes 786440 | tf_op jit(solution)/shard_map/ppermute | solution.py:32
  139.4 12.0 %collective-permute-start.22 = (bf16[512,256]{1,0:T(8,128)(2,1)S(1)}, bf16[512,256]{1,0:T(8,128)(2,1)S(1)}, u32[]{:S(2)}, u32[]{:S(2)}) collective-permute-start(bf16[512,256]{1,0:T(8,128)(2,1)S(1)} %slice_bitcast_fusion.3), channel_id=1, source_target_pairs={{0,1},{1,0},{2,3},{3,2},{4,5},{5,4},{6,7},{7,6},{8,9},{9,8},{10,11... | collective-permute-start | bytes 786440 | tf_op jit(solution)/shard_map/ppermute | solution.py:32
  140.0 11.4 %collective-permute-start.23 = (bf16[512,256]{1,0:T(8,128)(2,1)S(1)}, bf16[512,256]{1,0:T(8,128)(2,1)S(1)}, u32[]{:S(2)}, u32[]{:S(2)}) collective-permute-start(bf16[512,256]{1,0:T(8,128)(2,1)S(1)} %get-tuple-element.106), channel_id=1, source_target_pairs={{0,1},{1,0},{2,3},{3,2},{4,5},{5,4},{6,7},{7,6},{8,9},{9,8},{10,11... | collective-permute-start | bytes 786440 | tf_op jit(solution)/shard_map/ppermute | solution.py:32
  158.7 14.9 %collective-permute-start.18 = (bf16[128,1024]{1,0:T(8,128)(2,1)S(1)}, bf16[128,1024]{1,0:T(8,128)(2,1)S(1)}, u32[]{:S(2)}, u32[]{:S(2)}) collective-permute-start(bf16[128,1024]{1,0:T(8,128)(2,1)S(1)} %fusion.3), channel_id=1, source_target_pairs={{0,8},{4,12},{8,0},{12,4},{1,9},{5,13},{9,1},{13,5},{2,10},{6,14},... | collective-permute-start | bytes 786440 | tf_op jit(solution)/shard_map/ppermute | solution.py:24
  164.3 10.2 %collective-permute-start.26 = (bf16[64,512]{1,0:T(8,128)(2,1)S(1)}, bf16[64,512]{1,0:T(8,128)(2,1)S(1)}, u32[]{:S(2)}, u32[]{:S(2)}) collective-permute-start(bf16[64,512]{1,0:T(8,128)(2,1)S(1)} %get-tuple-element.113), channel_id=1, source_target_pairs={{0,1},{1,0},{2,3},{3,2},{4,5},{5,4},{6,7},{7,6},{8,9},{9,8},{10,11... | collective-permute-start | bytes 196616 | tf_op jit(solution)/shard_map/ppermute | solution.py:32
  (36 other events, 384.9 us)
